TPU v7x, 32 devices: a whole 2x2x4 slice. The times are simulated.
32 devices in a mesh: tile: 4 (over x, core), dev: 8 (over z, y).
Axes of the slice: x: 2, y: 2, z: 4, core: 2. Of those that a mesh axis runs over, the one named last changes fastest.
Arguments:
- features: bfloat16 [256, 64, 128], P(('tile', 'dev')), may hold values from -6 to 6
- morton_pos: int32 [256], P(('tile', 'dev')), may hold values from 0 to 63, as said below
- neighbours: int32 [256, 27], P(('tile', 'dev')), may hold values from 0 to 24, as said below
- rim: int32 [128], P(('tile', 'dev')), may hold values from 0 to 7, as said below
- cotangent: bfloat16 [256, 64, 128], P(('tile', 'dev')), may hold values from -6 to 6
- weight_one: bfloat16 [3456, 128], replicated, may hold values from -0.109375 to 0.109375
- weight_two: bfloat16 [3456, 128], replicated, may hold values from -0.109375 to 0.109375
Outputs:
- output: bfloat16 [256, 64, 128], P(('tile', 'dev'))
- input_grad: bfloat16 [256, 64, 128], P(('tile', 'dev'))
- grad_one: float32 [3456, 128], replicated
- grad_two: float32 [3456, 128], replicated
Inputs may be any that keep to these rules, and one draw needn't show every extreme that they name: `morton_pos`: within each super-tile the positions form a permutation of its 64 Morton rows; the 8 scan rows of one device go to at most 2 rows of any one device (position // 8), a bound reached in every draw. `neighbours`: lists come from block coordinates of a sparse map, each device owning a box of 6 x 6 x 2 block cells, tile stepping along x and dev along y: block a's neighbour at offset o is b exactly when b's neighbour at offset 26 - o is a; every block that a neighbouring device reads is in that device's rim list; the four corner columns of every box are empty, so no block reads a device diagonal to its own. `rim`: 4 different blocks of the device.
All inputs are finite; a program needn't handle non-finite values.
Results may differ from a plain program's by a relative error of at most 0.0033.
Values may be sent and summed in bfloat16 or wider, within the bound.
No kernel may reach another device: no remote copies, remote signals or barrier semaphores. Data moves between devices by JAX's collectives and lax.ppermute only.
A program may use at most 128 MiB of HBM per device.

v0:
```python
import functools
import math

import jax
import jax.numpy as jnp
from jax import lax
from jax.experimental import pallas as pl
from jax.experimental.pallas import tpu as pltpu
from jax.sharding import PartitionSpec as P

EDGE = 4
OFFSETS = 27
LABEL_ROWS = 16
BF16 = jnp.bfloat16
F32 = jnp.float32


def cube_plan():
    cell = {}
    for i in range(EDGE):
        for j in range(EDGE):
            for k in range(EDGE):
                cell[(i + 1, j + 1, k + 1)] = (i * EDGE + j) * EDGE + k
    copies = []
    free = EDGE**3
    for offset in range(OFFSETS):
        steps = (offset // 9 - 1, offset // 3 % 3 - 1, offset % 3 - 1)
        if steps == (0, 0, 0):
            continue
        ranges = [
            {-1: [(0, EDGE - 1)], 0: [(u + 1, u) for u in range(EDGE)], 1: [(EDGE + 1, 0)]}[step]
            for step in steps
        ]
        sources = []
        for x, i in ranges[0]:
            for y, j in ranges[1]:
                for z, k in ranges[2]:
                    cell[(x, y, z)] = free + len(sources)
                    sources.append((i * EDGE + j) * EDGE + k)
        at = 0
        while at < len(sources):
            count, stride = 1, 1
            if at + 1 < len(sources):
                stride = sources[at + 1] - sources[at]
                while (
                    at + count < len(sources)
                    and sources[at + count] - sources[at + count - 1] == stride
                ):
                    count += 1
            if count == 1:
                stride = 1
            copies.append((offset, sources[at], count, stride, free + at))
            at += count
        free += len(sources)
    return cell, copies, free


CELL, COPIES, CELLS = cube_plan()


def cell_runs(offset, flip):
    steps = (offset // 9, offset // 3 % 3, offset % 3)
    if flip:
        steps = tuple(2 - step for step in steps)
    runs = []
    for i in range(EDGE):
        for j in range(EDGE):
            for k in range(EDGE):
                at = CELL[(i + steps[0], j + steps[1], k + steps[2])]
                if runs and runs[-1][0] + runs[-1][1] == at:
                    runs[-1][1] += 1
                else:
                    runs.append([at, 1])
    return runs


def fill_table(table, own, sides, meta, at=0):
    blocks = own.shape[0]
    rims = sides[0].shape[0] if at is None else sides[0].shape[1]
    tile_odd = meta[0]
    dev_odd = meta[1]
    firsts = (
        blocks + rims * (1 - tile_odd),
        blocks + rims * tile_odd,
        blocks + rims * (3 - dev_odd),
        blocks + rims * (2 + dev_odd),
    )
    table[0:blocks] = own[...].astype(F32)
    for first, side in zip(firsts, sides):
        table[pl.ds(first, rims)] = (side[...] if at is None else side[at]).astype(F32)
    table[blocks + 4 * rims] = jnp.zeros(table.shape[1:], F32)


def fill_cells(cells, table, near, blocks):
    voxels = table.shape[1]
    for a in range(blocks):
        cells[pl.ds(a, voxels, stride=blocks), :] = table[a]
        for offset, first, count, stride, at in COPIES:
            e = near[a, offset]
            source = pl.ds(first, count) if stride == 1 else pl.ds(first, count, stride=stride)
            if count == 1:
                cells[pl.ds(at * blocks + a, 1), :] = table[e, source, :]
            else:
                cells[pl.ds(at * blocks + a, count, stride=blocks), :] = table[e, source, :]


def fill_columns(columns, cells, blocks, flip):
    channels = cells.shape[1]
    for offset in range(OFFSETS):
        parts = [
            cells[pl.ds(at * blocks, count * blocks), :] for at, count in cell_runs(offset, flip)
        ]
        columns[:, offset * channels : (offset + 1) * channels] = jnp.concatenate(
            parts, axis=0
        ).astype(BF16)


def transpose_blocks(target, source):
    channels = source.shape[1]
    for offset in range(OFFSETS):
        rows = slice(offset * channels, (offset + 1) * channels)
        target[rows, :] = source[rows, :].T


def pack_kernel(morton_pos, rim, features, cotangent, outgoing, rim_rows, flat_index):
    blocks, voxels, channels = features.shape
    peers, rows, _ = outgoing.shape
    capacity = (rows - LABEL_ROWS) // voxels
    outgoing[...] = jnp.zeros(outgoing.shape, BF16)
    for p in range(peers):
        outgoing[p, capacity * voxels :, :] = jnp.full((LABEL_ROWS, channels), blocks, BF16)
    lane = lax.broadcasted_iota(jnp.int32, (LABEL_ROWS, channels), 1)
    devs = [lax.div(morton_pos[r], blocks) for r in range(blocks)]
    for r in range(blocks):
        slot = morton_pos[r] - devs[r] * blocks
        place = jnp.int32(0)
        for earlier in range(r):
            place = place + (devs[earlier] == devs[r]).astype(jnp.int32)
        flat_index[r] = devs[r] * capacity + place
        outgoing[devs[r], pl.ds(pl.multiple_of(place * voxels, voxels), voxels), :] = features[r]
        held = outgoing[devs[r], capacity * voxels :, :].astype(F32)
        outgoing[devs[r], capacity * voxels :, :] = jnp.where(
            lane == place, slot.astype(F32), held
        ).astype(BF16)
    for h in range(rim_rows.shape[0]):
        rim_rows[h] = cotangent[rim[h]]


def unpack_kernel(slots, rim, arrived, morton, rim_rows):
    blocks, voxels, channels = morton.shape
    peers, rows, _ = arrived.shape
    capacity = (rows - LABEL_ROWS) // voxels
    for p in range(peers):
        for c in range(capacity):
            slot = slots[p * capacity + c]

            @pl.when(slot < blocks)
            def _():
                morton[slot] = arrived[p, c * voxels : (c + 1) * voxels, :]

    for h in range(rim_rows.shape[0]):
        rim_rows[h] = morton[rim[h]]


def first_kernel(
    near, meta, cotangent, side_a, side_b, side_c, side_d, weight_one, weight_two,
    columns, hidden_grad, flipped_one, table, cells, flipped_two,
):
    blocks = cotangent.shape[0]
    fill_table(table, cotangent, (side_a, side_b, side_c, side_d), meta, None)
    fill_cells(cells, table, near, blocks)
    fill_columns(columns, cells, blocks, True)
    transpose_blocks(flipped_two, weight_two)
    hidden_grad[...] = jnp.dot(columns[...], flipped_two[...], preferred_element_type=F32)
    transpose_blocks(flipped_one, weight_one)


def middle_kernel(
    near, meta, rim, morton, side_a, side_b, side_c, side_d, weight_one, grad_columns, hidden_grad,
    hidden, pre_grad, rim_rows, keep_two, send_two, keep_one, send_one,
    table, cells, columns, hidden_va, pre_grad_va, halves,
):
    blocks, voxels, channels = morton.shape
    half = channels // 2
    core = meta[0]
    fill_table(table, morton, (side_a, side_b, side_c, side_d), meta, None)
    fill_cells(cells, table, near, blocks)
    fill_columns(columns, cells, blocks, False)
    pre_one = jnp.dot(columns[...], weight_one[...], preferred_element_type=F32)
    gate = jax.nn.sigmoid(pre_one)
    hidden_flat = (pre_one * gate).astype(BF16)
    pre_grad_flat = (hidden_grad[...] * gate * (1.0 + pre_one * (1.0 - gate))).astype(BF16)
    hidden_va[...] = hidden_flat.astype(F32)
    pre_grad_va[...] = pre_grad_flat.astype(F32)
    for a in range(blocks):
        hidden[a] = hidden_va[pl.ds(a, voxels, stride=blocks), :].astype(BF16)
        pre_grad[a] = pre_grad_va[pl.ds(a, voxels, stride=blocks), :].astype(BF16)
    for h in range(rim_rows.shape[1]):
        rim_rows[0, h] = hidden[rim[h]]
        rim_rows[1, h] = pre_grad[rim[h]]
    turned = hidden_flat.T
    for offset in range(OFFSETS):
        part = jnp.dot(
            turned,
            grad_columns[:, offset * channels : (offset + 1) * channels],
            preferred_element_type=F32,
        )
        halves[core, offset] = part[:half]
        halves[1 - core, offset] = part[half:]
    keep_two[0:OFFSETS] = halves[0]
    send_two[0:OFFSETS] = halves[1]
    turned = pre_grad_flat.T
    for offset in range(OFFSETS):
        part = jnp.dot(
            turned,
            columns[:, offset * channels : (offset + 1) * channels],
            preferred_element_type=F32,
        ).T
        halves[core, offset] = part[:half]
        halves[1 - core, offset] = part[half:]
    keep_one[0:OFFSETS] = halves[0]
    send_one[0:OFFSETS] = halves[1]
    for ref in (keep_two, send_two, keep_one, send_one):
        ref[OFFSETS] = jnp.zeros(ref.shape[1:], F32)


def last_kernel(
    near, meta, slots, hidden, pre_grad, morton, cotangent, side_a, side_b, side_c, side_d,
    weight_two, flipped_one, output, returning, table, cells, columns, result, natural,
):
    blocks, voxels, channels = morton.shape
    peers, rows, _ = returning.shape
    capacity = rows // voxels
    sides = (side_a, side_b, side_c, side_d)
    fill_table(table, hidden, sides, meta, 0)
    fill_cells(cells, table, near, blocks)
    fill_columns(columns, cells, blocks, False)
    result[...] = jnp.dot(columns[...], weight_two[...], preferred_element_type=F32)
    for a in range(blocks):
        output[a] = (
            morton[a].astype(F32) + result[pl.ds(a, voxels, stride=blocks), :]
        ).astype(BF16)
    fill_table(table, pre_grad, sides, meta, 1)
    fill_cells(cells, table, near, blocks)
    fill_columns(columns, cells, blocks, True)
    result[...] = jnp.dot(columns[...], flipped_one[...], preferred_element_type=F32)
    for a in range(blocks):
        natural[a] = (
            result[pl.ds(a, voxels, stride=blocks), :] + cotangent[a].astype(F32)
        ).astype(BF16)
    natural[blocks] = jnp.zeros((voxels, channels), BF16)
    for p in range(peers):
        for c in range(capacity):
            returning[p, c * voxels : (c + 1) * voxels, :] = natural[slots[p * capacity + c]]


def restore_kernel(flat_index, coming_back, input_grad):
    blocks, voxels, channels = input_grad.shape
    for r in range(blocks):
        input_grad[r] = coming_back[flat_index[r]]


def core_sum_kernel(meta, keep, received, total, out_a, out_b, out_c, held):
    held[...] = keep[...] + received[...]
    rows = total.shape[1]
    mine = meta[2] + 2 * meta[3]

    def part(index):
        return held[:, pl.ds(pl.multiple_of(index * rows, rows), rows), :]

    total[...] = part(mine)
    out_a[...] = part(mine ^ 1).astype(BF16)
    out_b[...] = part(mine ^ 2).astype(BF16)
    out_c[...] = part(mine ^ 3).astype(BF16)


def quad_sum_kernel(meta, total, in_a, in_b, in_c, keep, send, held):
    held[...] = (
        total[...] + in_a[...].astype(F32) + in_b[...].astype(F32) + in_c[...].astype(F32)
    )
    count = keep.shape[0]
    keep[...] = held[pl.ds(meta[4] * count, count)]
    send[...] = held[pl.ds((1 - meta[4]) * count, count)].astype(send.dtype)


def add_kernel(left, right, total):
    total[...] = (left[...].astype(F32) + right[...].astype(F32)).astype(total.dtype)


def join_kernel(meta, mine, other, joined):
    count = mine.shape[0]
    joined[pl.ds(meta[4] * count, count)] = mine[...]
    joined[pl.ds((1 - meta[4]) * count, count)] = other[...]


def quad_join_kernel(meta, mine, in_a, in_b, in_c, joined):
    rows = mine.shape[1]
    index = meta[2] + 2 * meta[3]
    for m, ref in enumerate((mine, in_a, in_b, in_c)):
        joined[:, pl.ds(pl.multiple_of((index ^ m) * rows, rows), rows), :] = ref[...]


def finish_kernel(scale, meta, mine, other, grad):
    rows = mine.shape[1]
    channels = mine.shape[2]
    first = pl.multiple_of(meta[0] * rows, rows)
    second = pl.multiple_of((1 - meta[0]) * rows, rows)
    for offset in range(OFFSETS):
        grad[pl.ds(offset * channels + first, rows), :] = mine[offset].astype(F32) * scale
        grad[pl.ds(offset * channels + second, rows), :] = other[offset].astype(F32) * scale


SMEM = pl.BlockSpec(memory_space=pltpu.SMEM)
VMEM = pl.BlockSpec(memory_space=pltpu.VMEM)


def call(kernel, scalars, arrays, outs, scratch=(), smem_outs=(), flops=0, name=None):
    shapes = [jax.ShapeDtypeStruct(shape, dtype) for shape, dtype in outs]
    shapes += [jax.ShapeDtypeStruct(shape, jnp.int32) for shape in smem_outs]
    moved = sum(x.size * x.dtype.itemsize for x in arrays)
    moved += sum(math.prod(s.shape) * s.dtype.itemsize for s in shapes)
    return pl.pallas_call(
        kernel,
        out_shape=shapes,
        in_specs=[SMEM] * len(scalars) + [VMEM] * len(arrays),
        out_specs=[VMEM] * len(outs) + [SMEM] * len(smem_outs),
        scratch_shapes=[pltpu.VMEM(shape, dtype) for shape, dtype in scratch],
        compiler_params=pltpu.CompilerParams(vmem_limit_bytes=48 * 2**20),
        cost_estimate=pl.CostEstimate(flops=flops, bytes_accessed=moved, transcendentals=0),
        name=name,
    )(*scalars, *arrays)


def halo(rows):
    sides = []
    for axis in ("tile", "dev"):
        count = lax.axis_size(axis)
        even = [(i, i ^ 1) for i in range(count)]
        odd = []
        for i in range(1, count - 1, 2):
            odd += [(i, i + 1), (i + 1, i)]
        sides += [lax.ppermute(rows, axis, even), lax.ppermute(rows, axis, odd)]
    return sides


def swap(rows, tile_bit, dev_bit):
    tiles, devs = lax.axis_size("tile"), lax.axis_size("dev")
    pairs = [
        (t * devs + d, (t ^ tile_bit) * devs + (d ^ dev_bit))
        for t in range(tiles)
        for d in range(devs)
    ]
    return lax.ppermute(rows, ("tile", "dev"), pairs)


def reduce_all(meta, keep, send, scale):
    tiles, devs = lax.axis_size("tile"), lax.axis_size("dev")
    count, rows, channels = keep.shape
    quarter = rows // 4
    small = (count, quarter, channels)
    received = swap(send, 1, 0)
    total, out_a, out_b, out_c = call(
        core_sum_kernel, [meta], [keep, received],
        [(small, F32), (small, BF16), (small, BF16), (small, BF16)],
        [(keep.shape, F32)], name="core_sum",
    )
    in_a, in_b, in_c = swap(out_a, 2, 0), swap(out_b, 0, 1), swap(out_c, 2, 1)
    part = (count // 2, quarter, channels)
    keep, send = call(
        quad_sum_kernel, [meta], [total, in_a, in_b, in_c], [(part, F32), (part, F32)],
        [(small, F32)], name="quad_sum",
    )
    received = swap(send, 0, 2)
    rest = [(0, 1 << bit) for bit in range(2, devs.bit_length() - 1)]
    rest += [(1 << bit, 0) for bit in range(2, tiles.bit_length() - 1)]
    wire = BF16 if len(rest) == 1 else F32
    (mine,) = call(add_kernel, [], [keep, received], [(part, wire)], name="pair_sum")
    for step, (tile_bit, dev_bit) in enumerate(rest):
        other = swap(mine, tile_bit, dev_bit)
        kind = BF16 if step == len(rest) - 1 else wire
        (mine,) = call(add_kernel, [], [mine, other], [(part, kind)], name="far_sum")
    other = swap(mine, 0, 2)
    (mine,) = call(join_kernel, [meta], [mine, other], [(small, BF16)], name="pair_join")
    others = [swap(mine, 2, 0), swap(mine, 0, 1), swap(mine, 2, 1)]
    (mine,) = call(
        quad_join_kernel, [meta], [mine, *others], [((count, rows, channels), BF16)],
        name="quad_join",
    )
    other = swap(mine, 1, 0)
    (grad,) = call(
        functools.partial(finish_kernel, scale), [meta], [mine, other],
        [((OFFSETS * channels, channels), F32)], name="finish",
    )
    return grad


def per_device(features, morton_pos, neighbours, rim, cotangent, weight_one, weight_two):
    blocks, voxels, channels = features.shape
    rims = rim.shape[0]
    peers = lax.axis_size("dev")
    tiles = lax.axis_size("tile")
    capacity = 2 * ((blocks + peers - 1) // peers)
    t, d = lax.axis_index("tile"), lax.axis_index("dev")
    meta = jnp.stack([t & 1, d & 1, (t >> 1) & 1, d & 1, (d >> 1) & 1]).astype(jnp.int32)
    block = (blocks, voxels, channels)
    rows = blocks * voxels
    depth = OFFSETS * channels
    table = ((blocks + 4 * rims + 1, voxels, channels), F32)
    cells = ((CELLS * blocks, channels), F32)
    columns = ((rows, depth), BF16)
    flat = ((rows, channels), F32)
    rim_shape = (rims, voxels, channels)
    macs = rows * depth * channels

    outgoing, cot_rim, flat_index = call(
        pack_kernel, [morton_pos, rim], [features, cotangent],
        [((peers, capacity * voxels + LABEL_ROWS, channels), BF16), (rim_shape, BF16)],
        smem_outs=[(blocks,)], name="pack",
    )
    arrived = lax.all_to_all(outgoing, "dev", split_axis=0, concat_axis=0, tiled=True)
    cot_sides = halo(cot_rim)
    grad_columns, hidden_grad, flipped_one = call(
        first_kernel, [neighbours, meta], [cotangent, *cot_sides, weight_one, weight_two],
        [columns, flat, ((depth, channels), BF16)],
        [table, cells, ((depth, channels), BF16)], flops=2 * macs, name="hidden_grad",
    )
    slots = arrived[:, capacity * voxels, :capacity].astype(jnp.int32).reshape(-1)
    morton, morton_rim = call(
        unpack_kernel, [slots, rim], [arrived], [(block, BF16), (rim_shape, BF16)], name="unpack"
    )
    sides = halo(morton_rim)
    padded = (OFFSETS + 1, channels // 2, channels)
    hidden, pre_grad, rim_rows, keep_two, send_two, keep_one, send_one = call(
        middle_kernel, [neighbours, meta, rim],
        [morton, *sides, weight_one, grad_columns, hidden_grad],
        [(block, BF16), (block, BF16), ((2,) + rim_shape, BF16)] + [(padded, F32)] * 4,
        [table, cells, columns, flat, flat, ((2, OFFSETS, channels // 2, channels), F32)],
        flops=6 * macs, name="middle",
    )
    scale = 1.0 / math.sqrt(blocks * voxels * tiles * peers)
    grad_two = reduce_all(meta, keep_two, send_two, scale)
    grad_one = reduce_all(meta, keep_one, send_one, scale)
    sides = halo(rim_rows)
    output, returning = call(
        last_kernel, [neighbours, meta, slots],
        [hidden, pre_grad, morton, cotangent, *sides, weight_two, flipped_one],
        [(block, BF16), ((peers, capacity * voxels, channels), BF16)],
        [table, cells, columns, flat, ((blocks + 1, voxels, channels), BF16)],
        flops=4 * macs, name="last",
    )
    coming_back = lax.all_to_all(returning, "dev", split_axis=0, concat_axis=0, tiled=True)
    (input_grad,) = call(
        restore_kernel, [flat_index], [coming_back.reshape(peers * capacity, voxels, channels)],
        [(block, BF16)], name="restore",
    )
    return (output, input_grad, grad_one, grad_two)


def solution(mesh):
    placed = (
        P(("tile", "dev"), None, None),
        P(("tile", "dev")),
        P(("tile", "dev"), None),
        P(("tile", "dev")),
        P(("tile", "dev"), None, None),
        P(),
        P(),
    )
    return jax.shard_map(
        per_device,
        mesh=mesh,
        in_specs=placed,
        out_specs=(P(("tile", "dev"), None, None), P(("tile", "dev"), None, None), P(), P()),
        check_vma=False,
    )
```

profile of v0, /device:TPU:0, one launch (start us, length us, event | category | flops | bytes accessed | tf_op | source)
XLA Modules:
  0.0 112.8 jit_solution(1081074225799090918)
XLA Ops:
  5.1 7.3 %all-to-all-start = ((bf16[8,144,128]{2,1,0:T(8,128)(2,1)}), bf16[8,144,128]{2,1,0:T(8,128)(2,1)S(1)}, u32[]{:S(2)}, u32[]{:S(2)}) async-start(bf16[8,144,128]{2,1,0:T(8,128)(2,1)} %get-tuple-element.33), calls=%async_computation | async-start | bytes 589824 | tf_op jit(solution)/shard_map/all_to_all | solution.py:420
  13.1 4.8 %collective-permute-start.6 = (bf16[4,64,128]{2,1,0:T(8,128)(2,1)S(1)}, bf16[4,64,128]{2,1,0:T(8,128)(2,1)S(1)}, u32[]{:S(2)}, u32[]{:S(2)}) collective-permute-start(bf16[4,64,128]{2,1,0:T(8,128)(2,1)S(1)} %get-tuple-element.36), channel_id=1, source_target_pairs={{0,1},{1,0},{2,3},{3,2},{4,5},{5,4},{6,7},{7,6},{8,9},{9,8},{10,11... | collective-permute-start | bytes 196616 | tf_op jit(solution)/shard_map/ppermute | solution.py:342
  18.5 2.9 %collective-permute-start.4 = (bf16[4,64,128]{2,1,0:T(8,128)(2,1)S(1)}, bf16[4,64,128]{2,1,0:T(8,128)(2,1)S(1)}, u32[]{:S(2)}, u32[]{:S(2)}) collective-permute-start(bf16[4,64,128]{2,1,0:T(8,128)(2,1)S(1)} %get-tuple-element.36), channel_id=1, source_target_pairs={{0,8},{8,0},{16,24},{24,16},{1,9},{9,1},{17,25},{25,17},{2,10},{10... | collective-permute-start | bytes 196616 | tf_op jit(solution)/shard_map/ppermute | solution.py:342
  24.9 3.1 %collective-permute-start.2 = (bf16[4,64,128]{2,1,0:T(8,128)(2,1)S(1)}, bf16[4,64,128]{2,1,0:T(8,128)(2,1)S(1)}, u32[]{:S(2)}, u32[]{:S(2)}) collective-permute-start(bf16[4,64,128]{2,1,0:T(8,128)(2,1)S(1)} %get-tuple-element.35), channel_id=1, source_target_pairs={{0,1},{1,0},{2,3},{3,2},{4,5},{5,4},{6,7},{7,6},{8,9},{9,8},{10,11... | collective-permute-start | bytes 196616 | tf_op jit(solution)/shard_map/ppermute | solution.py:342
  28.7 2.9 %collective-permute-start = (bf16[4,64,128]{2,1,0:T(8,128)(2,1)S(1)}, bf16[4,64,128]{2,1,0:T(8,128)(2,1)S(1)}, u32[]{:S(2)}, u32[]{:S(2)}) collective-permute-start(bf16[4,64,128]{2,1,0:T(8,128)(2,1)S(1)} %get-tuple-element.35), channel_id=1, source_target_pairs={{0,8},{8,0},{16,24},{24,16},{1,9},{9,1},{17,25},{25,17},{2,10},{10... | collective-permute-start | bytes 196616 | tf_op jit(solution)/shard_map/ppermute | solution.py:342
  35.6 3.7 %hidden_grad.1 = (bf16[512,3456]{1,0:T(8,128)(2,1)}, f32[512,128]{1,0:T(8,128)S(1)}, bf16[3456,128]{1,0:T(8,128)(2,1)S(1)}) custom-call(s32[8,27]{1,0:T(8,128)S(1)} %copy-done.8, s32[5]{0:T(128)S(1)} %stack.20.meta, bf16[8,64,128]{2,1,0:T(8,128)(2,1)S(1)} %copy-done.5, bf16[4,64,128]{2,1,0:T(8,128)(2,1)S(1)} %collective-permute-done.4.side_a, ...), custom_call_target="tpu_custom_call" | custom-call | flops 452984832 | bytes 6848512 | tf_op jit(solution)/shard_map/hidden_grad/pallas_call | solution.py:322
  39.3 7.3 %middle.1 = (bf16[8,64,128]{2,1,0:T(8,128)(2,1)S(1)}, bf16[8,64,128]{2,1,0:T(8,128)(2,1)S(1)}, bf16[2,4,64,128]{3,2,1,0:T(8,128)(2,1)S(1)}, f32[28,64,128]{2,1,0...) custom-call(s32[8,27]{1,0:T(8,128)S(1)} %copy-done.8, ...), custom_call_target="tpu_custom_call" | custom-call | flops 1358954496 | bytes 9142272 | tf_op jit(solution)/shard_map/middle/pallas_call | solution.py:322
  47.2 2.0 %collective-permute-done.12.received = f32[28,64,128]{2,1,0:T(8,128)S(1)} collective-permute-done((f32[28,64,128]{2,1,0:T(8,128)S(1)}, f32[28,64,128]{2,1,0:T(8,128)S(1)}, u32[]{:S(2)}, u32[]{:S(2)}) %collective-permute-start.12) | collective-permute-done | bytes 917536 | tf_op jit(solution)/shard_map/ppermute | solution.py:353
  50.1 3.4 %collective-permute-start.15 = (bf16[28,16,128]{2,1,0:T(8,128)(2,1)S(1)}, bf16[28,16,128]{2,1,0:T(8,128)(2,1)S(1)}, u32[]{:S(2)}, u32[]{:S(2)}) collective-permute-start(bf16[28,16,128]{2,1,0:T(8,128)(2,1)S(1)} %get-tuple-element.51), channel_id=1, source_target_pairs={{0,17},{1,16},{2,19},{3,18},{4,21},{5,20},{6,23},{7,22},{8,25},{9,... | collective-permute-start | bytes 344072 | tf_op jit(solution)/shard_map/ppermute | solution.py:353
  56.0 1.8 %collective-permute-start.26 = (bf16[28,16,128]{2,1,0:T(8,128)(2,1)S(1)}, bf16[28,16,128]{2,1,0:T(8,128)(2,1)S(1)}, u32[]{:S(2)}, u32[]{:S(2)}) collective-permute-start(bf16[28,16,128]{2,1,0:T(8,128)(2,1)S(1)} %get-tuple-element.59), channel_id=1, source_target_pairs={{0,17},{1,16},{2,19},{3,18},{4,21},{5,20},{6,23},{7,22},{8,25},{9,... | collective-permute-start | bytes 344072 | tf_op jit(solution)/shard_map/ppermute | solution.py:353
  58.8 2.5 %collective-permute-start.16 = (f32[14,16,128]{2,1,0:T(8,128)S(1)}, f32[14,16,128]{2,1,0:T(8,128)S(1)}, u32[]{:S(2)}, u32[]{:S(2)}) collective-permute-start(f32[14,16,128]{2,1,0:T(8,128)S(1)} %get-tuple-element.53), channel_id=1, source_target_pairs={{0,2},{1,3},{2,0},{3,1},{4,6},{5,7},{6,4},{7,5},{8,10},{9,11},{10,... | collective-permute-start | bytes 344072 | tf_op jit(solution)/shard_map/ppermute | solution.py:353
  63.3 2.2 %collective-permute-start.27 = (f32[14,16,128]{2,1,0:T(8,128)S(1)}, f32[14,16,128]{2,1,0:T(8,128)S(1)}, u32[]{:S(2)}, u32[]{:S(2)}) collective-permute-start(f32[14,16,128]{2,1,0:T(8,128)S(1)} %get-tuple-element.61), channel_id=1, source_target_pairs={{0,2},{1,3},{2,0},{3,1},{4,6},{5,7},{6,4},{7,5},{8,10},{9,11},{10,... | collective-permute-start | bytes 344072 | tf_op jit(solution)/shard_map/ppermute | solution.py:353
  65.6 2.7 %collective-permute-done.27.right = f32[14,16,128]{2,1,0:T(8,128)S(1)} collective-permute-done((f32[14,16,128]{2,1,0:T(8,128)S(1)}, f32[14,16,128]{2,1,0:T(8,128)S(1)}, u32[]{:S(2)}, u32[]{:S(2)}) %collective-permute-start.27) | collective-permute-done | bytes 114720 | tf_op jit(solution)/shard_map/ppermute | solution.py:353
  68.4 1.9 %collective-permute-start.28 = (bf16[14,16,128]{2,1,0:T(8,128)(2,1)S(1)}, bf16[14,16,128]{2,1,0:T(8,128)(2,1)S(1)}, u32[]{:S(2)}, u32[]{:S(2)}) collective-permute-start(bf16[14,16,128]{2,1,0:T(8,128)(2,1)S(1)} %pair_sum.3.left), channel_id=1, source_target_pairs={{0,4},{1,5},{2,6},{3,7},{4,0},{5,1},{6,2},{7,3},{8,12},{9,13},{10,... | collective-permute-start | bytes 172040 | tf_op jit(solution)/shard_map/ppermute | solution.py:353
  70.3 2.1 %collective-permute-done.17.right = bf16[14,16,128]{2,1,0:T(8,128)(2,1)S(1)} collective-permute-done((bf16[14,16,128]{2,1,0:T(8,128)(2,1)S(1)}, bf16[14,16,128]{2,1,0:T(8,128)(2,1)S(1)}, u32[]{:S(2)}, u32[]{:S(2)}) %collective-permute-start.17) | collective-permute-done | bytes 57376 | tf_op jit(solution)/shard_map/ppermute | solution.py:353
  73.5 2.5 %collective-permute-start.29 = (bf16[14,16,128]{2,1,0:T(8,128)(2,1)S(1)}, bf16[14,16,128]{2,1,0:T(8,128)(2,1)S(1)}, u32[]{:S(2)}, u32[]{:S(2)}) collective-permute-start(bf16[14,16,128]{2,1,0:T(8,128)(2,1)S(1)} %far_sum.3.mine), channel_id=1, source_target_pairs={{0,2},{1,3},{2,0},{3,1},{4,6},{5,7},{6,4},{7,5},{8,10},{9,11},{10,... | collective-permute-start | bytes 172040 | tf_op jit(solution)/shard_map/ppermute | solution.py:353
  76.7 2.8 %collective-permute-start.10 = (bf16[2,4,64,128]{3,2,1,0:T(8,128)(2,1)S(1)}, bf16[2,4,64,128]{3,2,1,0:T(8,128)(2,1)S(1)}, u32[]{:S(2)}, u32[]{:S(2)}) collective-permute-start(bf16[2,4,64,128]{3,2,1,0:T(8,128)(2,1)S(1)} %get-tuple-element.41), channel_id=1, source_target_pairs={{0,1},{1,0},{2,3},{3,2},{4,5},{5,4},{6,7},{7,6},{8,9},{9,8},{10,11... | collective-permute-start | bytes 393224 | tf_op jit(solution)/shard_map/ppermute | solution.py:342
  80.3 3.3 %collective-permute-start.8 = (bf16[2,4,64,128]{3,2,1,0:T(8,128)(2,1)S(1)}, bf16[2,4,64,128]{3,2,1,0:T(8,128)(2,1)S(1)}, u32[]{:S(2)}, u32[]{:S(2)}) collective-permute-start(bf16[2,4,64,128]{3,2,1,0:T(8,128)(2,1)S(1)} %get-tuple-element.41), channel_id=1, source_target_pairs={{0,8},{8,0},{16,24},{24,16},{1,9},{9,1},{17,25},{25,17},{2,10},{10... | collective-permute-start | bytes 393224 | tf_op jit(solution)/shard_map/ppermute | solution.py:342
  86.2 2.1 %collective-permute-start.19 = (bf16[28,16,128]{2,1,0:T(8,128)(2,1)S(1)}, bf16[28,16,128]{2,1,0:T(8,128)(2,1)S(1)}, u32[]{:S(2)}, u32[]{:S(2)}) collective-permute-start(bf16[28,16,128]{2,1,0:T(8,128)(2,1)S(1)} %pair_join.2.mine), channel_id=1, source_target_pairs={{0,16},{1,17},{2,18},{3,19},{4,20},{5,21},{6,22},{7,23},{8,24},{9,... | collective-permute-start | bytes 344072 | tf_op jit(solution)/shard_map/ppermute | solution.py:353
  91.8 4.5 %last.1 = (bf16[8,64,128]{2,1,0:T(8,128)(2,1)}, bf16[8,128,128]{2,1,0:T(8,128)(2,1)}) custom-call(s32[8,27]{1,0:T(8,128)S(1)} %copy-done.8, s32[5]{0:T(128)S(1)} %stack.20.meta, s32[16]{0:T(128)S(1)} %reshape.16.slots, bf16[8,64,128]{2,1,0:T(8,128)(2,1)S(1)} %get-tuple-element.39.hidden, bf16[8,64,128]{2,1,0:T(8,128)(2,1)S(1)} %get-tuple-element.40.pre_grad, ...), custom_call_target="tpu_custom_call" | custom-call | flops 905969664 | bytes 3211264 | tf_op jit(solution)/shard_map/last/pallas_call | solution.py:322
  96.3 3.4 %all-to-all-start.1 = ((bf16[8,128,128]{2,1,0:T(8,128)(2,1)}), bf16[8,128,128]{2,1,0:T(8,128)(2,1)S(1)}, u32[]{:S(2)}, u32[]{:S(2)}) async-start(bf16[8,128,128]{2,1,0:T(8,128)(2,1)} %get-tuple-element.45), calls=%async_computation.1 | async-start | bytes 524288 | tf_op jit(solution)/shard_map/all_to_all | solution.py:451
  101.6 6.3 %all-to-all-done.1 = bf16[8,128,128]{2,1,0:T(8,128)(2,1)S(1)} async-done(((bf16[8,128,128]{2,1,0:T(8,128)(2,1)}), bf16[8,128,128]{2,1,0:T(8,128)(2,1)S(1)}, u32[]{:S(2)}, u32[]{:S(2)}) %all-to-all-start.1) | async-done | bytes 262176 | tf_op jit(solution)/shard_map/all_to_all | solution.py:451
  109.1 1.9 %finish.2 = f32[3456,128]{1,0:T(8,128)} custom-call(s32[5]{0:T(128)S(1)} %stack.20.meta, bf16[28,64,128]{2,1,0:T(8,128)(2,1)S(1)} %quad_join.2.mine, bf16[28,64,128]{2,1,0:T(8,128)(2,1)S(1)} %collective-permute-done.22.other), custom_call_target="tpu_custom_call" | custom-call | bytes 2686976 | tf_op jit(solution)/shard_map/finish/pallas_call | solution.py:322
  111.0 1.9 %finish.3 = f32[3456,128]{1,0:T(8,128)} custom-call(s32[5]{0:T(128)S(1)} %stack.20.meta, bf16[28,64,128]{2,1,0:T(8,128)(2,1)S(1)} %quad_join.3.mine, bf16[28,64,128]{2,1,0:T(8,128)(2,1)S(1)} %collective-permute-done.33.other), custom_call_target="tpu_custom_call" | custom-call | bytes 2686976 | tf_op jit(solution)/shard_map/finish/pallas_call | solution.py:322
  (97 shorter events, 32.9 us)
Async XLA Ops:
  5.1 17.6 %all-to-all-start = ((bf16[8,144,128]{2,1,0:T(8,128)(2,1)}), bf16[8,144,128]{2,1,0:T(8,128)(2,1)S(1)}, u32[]{:S(2)}, u32[]{:S(2)}) async-start(bf16[8,144,128]{2,1,0:T(8,128)(2,1)} %get-tuple-element.33), calls=%async_computation | async-start | bytes 589824 | tf_op jit(solution)/shard_map/all_to_all | solution.py:420
  12.4 12.4 %collective-permute-start.7 = (bf16[4,64,128]{2,1,0:T(8,128)(2,1)S(1)}, bf16[4,64,128]{2,1,0:T(8,128)(2,1)S(1)}, u32[]{:S(2)}, u32[]{:S(2)}) collective-permute-start(bf16[4,64,128]{2,1,0:T(8,128)(2,1)S(1)} %get-tuple-element.36), channel_id=1, source_target_pairs={{1,2},{2,1},{3,4},{4,3},{5,6},{6,5},{9,10},{10,9},{11,12},{12,11},... | collective-permute-start | bytes 196616 | tf_op jit(solution)/shard_map/ppermute | solution.py:342
  13.1 14.9 %collective-permute-start.6 = (bf16[4,64,128]{2,1,0:T(8,128)(2,1)S(1)}, bf16[4,64,128]{2,1,0:T(8,128)(2,1)S(1)}, u32[]{:S(2)}, u32[]{:S(2)}) collective-permute-start(bf16[4,64,128]{2,1,0:T(8,128)(2,1)S(1)} %get-tuple-element.36), channel_id=1, source_target_pairs={{0,1},{1,0},{2,3},{3,2},{4,5},{5,4},{6,7},{7,6},{8,9},{9,8},{10,11... | collective-permute-start | bytes 196616 | tf_op jit(solution)/shard_map/ppermute | solution.py:342
  17.9 10.8 %collective-permute-start.5 = (bf16[4,64,128]{2,1,0:T(8,128)(2,1)S(1)}, bf16[4,64,128]{2,1,0:T(8,128)(2,1)S(1)}, u32[]{:S(2)}, u32[]{:S(2)}) collective-permute-start(bf16[4,64,128]{2,1,0:T(8,128)(2,1)S(1)} %get-tuple-element.36), channel_id=1, source_target_pairs={{8,16},{16,8},{9,17},{17,9},{10,18},{18,10},{11,19},{19,11},{12,20... | collective-permute-start | bytes 196616 | tf_op jit(solution)/shard_map/ppermute | solution.py:342
  18.5 13.1 %collective-permute-start.4 = (bf16[4,64,128]{2,1,0:T(8,128)(2,1)S(1)}, bf16[4,64,128]{2,1,0:T(8,128)(2,1)S(1)}, u32[]{:S(2)}, u32[]{:S(2)}) collective-permute-start(bf16[4,64,128]{2,1,0:T(8,128)(2,1)S(1)} %get-tuple-element.36), channel_id=1, source_target_pairs={{0,8},{8,0},{16,24},{24,16},{1,9},{9,1},{17,25},{25,17},{2,10},{10... | collective-permute-start | bytes 196616 | tf_op jit(solution)/shard_map/ppermute | solution.py:342
  24.2 15.1 %collective-permute-start.3 = (bf16[4,64,128]{2,1,0:T(8,128)(2,1)S(1)}, bf16[4,64,128]{2,1,0:T(8,128)(2,1)S(1)}, u32[]{:S(2)}, u32[]{:S(2)}) collective-permute-start(bf16[4,64,128]{2,1,0:T(8,128)(2,1)S(1)} %get-tuple-element.35), channel_id=1, source_target_pairs={{1,2},{2,1},{3,4},{4,3},{5,6},{6,5},{9,10},{10,9},{11,12},{12,11},... | collective-permute-start | bytes 196616 | tf_op jit(solution)/shard_map/ppermute | solution.py:342
  24.9 14.4 %collective-permute-start.2 = (bf16[4,64,128]{2,1,0:T(8,128)(2,1)S(1)}, bf16[4,64,128]{2,1,0:T(8,128)(2,1)S(1)}, u32[]{:S(2)}, u32[]{:S(2)}) collective-permute-start(bf16[4,64,128]{2,1,0:T(8,128)(2,1)S(1)} %get-tuple-element.35), channel_id=1, source_target_pairs={{0,1},{1,0},{2,3},{3,2},{4,5},{5,4},{6,7},{7,6},{8,9},{9,8},{10,11... | collective-permute-start | bytes 196616 | tf_op jit(solution)/shard_map/ppermute | solution.py:342
  28.0 11.3 %collective-permute-start.1 = (bf16[4,64,128]{2,1,0:T(8,128)(2,1)S(1)}, bf16[4,64,128]{2,1,0:T(8,128)(2,1)S(1)}, u32[]{:S(2)}, u32[]{:S(2)}) collective-permute-start(bf16[4,64,128]{2,1,0:T(8,128)(2,1)S(1)} %get-tuple-element.35), channel_id=1, source_target_pairs={{8,16},{16,8},{9,17},{17,9},{10,18},{18,10},{11,19},{19,11},{12,20... | collective-permute-start | bytes 196616 | tf_op jit(solution)/shard_map/ppermute | solution.py:342
  28.7 10.6 %collective-permute-start = (bf16[4,64,128]{2,1,0:T(8,128)(2,1)S(1)}, bf16[4,64,128]{2,1,0:T(8,128)(2,1)S(1)}, u32[]{:S(2)}, u32[]{:S(2)}) collective-permute-start(bf16[4,64,128]{2,1,0:T(8,128)(2,1)S(1)} %get-tuple-element.35), channel_id=1, source_target_pairs={{0,8},{8,0},{16,24},{24,16},{1,9},{9,1},{17,25},{25,17},{2,10},{10... | collective-permute-start | bytes 196616 | tf_op jit(solution)/shard_map/ppermute | solution.py:342
  50.0 8.2 %collective-permute-start.14 = (bf16[28,16,128]{2,1,0:T(8,128)(2,1)S(1)}, bf16[28,16,128]{2,1,0:T(8,128)(2,1)S(1)}, u32[]{:S(2)}, u32[]{:S(2)}) collective-permute-start(bf16[28,16,128]{2,1,0:T(8,128)(2,1)S(1)} %get-tuple-element.50), channel_id=1, source_target_pairs={{0,1},{1,0},{2,3},{3,2},{4,5},{5,4},{6,7},{7,6},{8,9},{9,8},{10,11... | collective-permute-start | bytes 344072 | tf_op jit(solution)/shard_map/ppermute | solution.py:353
  50.1 8.1 %collective-permute-start.15 = (bf16[28,16,128]{2,1,0:T(8,128)(2,1)S(1)}, bf16[28,16,128]{2,1,0:T(8,128)(2,1)S(1)}, u32[]{:S(2)}, u32[]{:S(2)}) collective-permute-start(bf16[28,16,128]{2,1,0:T(8,128)(2,1)S(1)} %get-tuple-element.51), channel_id=1, source_target_pairs={{0,17},{1,16},{2,19},{3,18},{4,21},{5,20},{6,23},{7,22},{8,25},{9,... | collective-permute-start | bytes 344072 | tf_op jit(solution)/shard_map/ppermute | solution.py:353
  54.4 8.3 %collective-permute-start.25 = (bf16[28,16,128]{2,1,0:T(8,128)(2,1)S(1)}, bf16[28,16,128]{2,1,0:T(8,128)(2,1)S(1)}, u32[]{:S(2)}, u32[]{:S(2)}) collective-permute-start(bf16[28,16,128]{2,1,0:T(8,128)(2,1)S(1)} %get-tuple-element.58), channel_id=1, source_target_pairs={{0,1},{1,0},{2,3},{3,2},{4,5},{5,4},{6,7},{7,6},{8,9},{9,8},{10,11... | collective-permute-start | bytes 344072 | tf_op jit(solution)/shard_map/ppermute | solution.py:353
  73.5 10.6 %collective-permute-start.29 = (bf16[14,16,128]{2,1,0:T(8,128)(2,1)S(1)}, bf16[14,16,128]{2,1,0:T(8,128)(2,1)S(1)}, u32[]{:S(2)}, u32[]{:S(2)}) collective-permute-start(bf16[14,16,128]{2,1,0:T(8,128)(2,1)S(1)} %far_sum.3.mine), channel_id=1, source_target_pairs={{0,2},{1,3},{2,0},{3,1},{4,6},{5,7},{6,4},{7,5},{8,10},{9,11},{10,... | collective-permute-start | bytes 172040 | tf_op jit(solution)/shard_map/ppermute | solution.py:353
  76.0 8.8 %collective-permute-start.11 = (bf16[2,4,64,128]{3,2,1,0:T(8,128)(2,1)S(1)}, bf16[2,4,64,128]{3,2,1,0:T(8,128)(2,1)S(1)}, u32[]{:S(2)}, u32[]{:S(2)}) collective-permute-start(bf16[2,4,64,128]{3,2,1,0:T(8,128)(2,1)S(1)} %get-tuple-element.41), channel_id=1, source_target_pairs={{1,2},{2,1},{3,4},{4,3},{5,6},{6,5},{9,10},{10,9},{11,12},{12,11},... | collective-permute-start | bytes 393224 | tf_op jit(solution)/shard_map/ppermute | solution.py:342
  76.7 9.6 %collective-permute-start.10 = (bf16[2,4,64,128]{3,2,1,0:T(8,128)(2,1)S(1)}, bf16[2,4,64,128]{3,2,1,0:T(8,128)(2,1)S(1)}, u32[]{:S(2)}, u32[]{:S(2)}) collective-permute-start(bf16[2,4,64,128]{3,2,1,0:T(8,128)(2,1)S(1)} %get-tuple-element.41), channel_id=1, source_target_pairs={{0,1},{1,0},{2,3},{3,2},{4,5},{5,4},{6,7},{7,6},{8,9},{9,8},{10,11... | collective-permute-start | bytes 393224 | tf_op jit(solution)/shard_map/ppermute | solution.py:342
  79.5 8.9 %collective-permute-start.9 = (bf16[2,4,64,128]{3,2,1,0:T(8,128)(2,1)S(1)}, bf16[2,4,64,128]{3,2,1,0:T(8,128)(2,1)S(1)}, u32[]{:S(2)}, u32[]{:S(2)}) collective-permute-start(bf16[2,4,64,128]{3,2,1,0:T(8,128)(2,1)S(1)} %get-tuple-element.41), channel_id=1, source_target_pairs={{8,16},{16,8},{9,17},{17,9},{10,18},{18,10},{11,19},{19,11},{12,20... | collective-permute-start | bytes 393224 | tf_op jit(solution)/shard_map/ppermute | solution.py:342
  84.8 15.0 %collective-permute-start.20 = (bf16[28,16,128]{2,1,0:T(8,128)(2,1)S(1)}, bf16[28,16,128]{2,1,0:T(8,128)(2,1)S(1)}, u32[]{:S(2)}, u32[]{:S(2)}) collective-permute-start(bf16[28,16,128]{2,1,0:T(8,128)(2,1)S(1)} %pair_join.2.mine), channel_id=1, source_target_pairs={{0,1},{1,0},{2,3},{3,2},{4,5},{5,4},{6,7},{7,6},{8,9},{9,8},{10,11... | collective-permute-start | bytes 344072 | tf_op jit(solution)/shard_map/ppermute | solution.py:353
  86.2 13.5 %collective-permute-start.19 = (bf16[28,16,128]{2,1,0:T(8,128)(2,1)S(1)}, bf16[28,16,128]{2,1,0:T(8,128)(2,1)S(1)}, u32[]{:S(2)}, u32[]{:S(2)}) collective-permute-start(bf16[28,16,128]{2,1,0:T(8,128)(2,1)S(1)} %pair_join.2.mine), channel_id=1, source_target_pairs={{0,16},{1,17},{2,18},{3,19},{4,20},{5,21},{6,22},{7,23},{8,24},{9,... | collective-permute-start | bytes 344072 | tf_op jit(solution)/shard_map/ppermute | solution.py:353
  88.3 12.1 %collective-permute-start.32 = (bf16[28,16,128]{2,1,0:T(8,128)(2,1)S(1)}, bf16[28,16,128]{2,1,0:T(8,128)(2,1)S(1)}, u32[]{:S(2)}, u32[]{:S(2)}) collective-permute-start(bf16[28,16,128]{2,1,0:T(8,128)(2,1)S(1)} %pair_join.3.mine), channel_id=1, source_target_pairs={{0,17},{1,16},{2,19},{3,18},{4,21},{5,20},{6,23},{7,22},{8,25},{9,... | collective-permute-start | bytes 344072 | tf_op jit(solution)/shard_map/ppermute | solution.py:353
  88.4 12.1 %collective-permute-start.31 = (bf16[28,16,128]{2,1,0:T(8,128)(2,1)S(1)}, bf16[28,16,128]{2,1,0:T(8,128)(2,1)S(1)}, u32[]{:S(2)}, u32[]{:S(2)}) collective-permute-start(bf16[28,16,128]{2,1,0:T(8,128)(2,1)S(1)} %pair_join.3.mine), channel_id=1, source_target_pairs={{0,1},{1,0},{2,3},{3,2},{4,5},{5,4},{6,7},{7,6},{8,9},{9,8},{10,11... | collective-permute-start | bytes 344072 | tf_op jit(solution)/shard_map/ppermute | solution.py:353
  91.2 9.3 %collective-permute-start.30 = (bf16[28,16,128]{2,1,0:T(8,128)(2,1)S(1)}, bf16[28,16,128]{2,1,0:T(8,128)(2,1)S(1)}, u32[]{:S(2)}, u32[]{:S(2)}) collective-permute-start(bf16[28,16,128]{2,1,0:T(8,128)(2,1)S(1)} %pair_join.3.mine), channel_id=1, source_target_pairs={{0,16},{1,17},{2,18},{3,19},{4,20},{5,21},{6,22},{7,23},{8,24},{9,... | collective-permute-start | bytes 344072 | tf_op jit(solution)/shard_map/ppermute | solution.py:353
  96.3 11.6 %all-to-all-start.1 = ((bf16[8,128,128]{2,1,0:T(8,128)(2,1)}), bf16[8,128,128]{2,1,0:T(8,128)(2,1)S(1)}, u32[]{:S(2)}, u32[]{:S(2)}) async-start(bf16[8,128,128]{2,1,0:T(8,128)(2,1)} %get-tuple-element.45), calls=%async_computation.1 | async-start | bytes 524288 | tf_op jit(solution)/shard_map/all_to_all | solution.py:451
  100.4 8.8 %collective-permute-start.22 = (bf16[28,64,128]{2,1,0:T(8,128)(2,1)S(1)}, bf16[28,64,128]{2,1,0:T(8,128)(2,1)S(1)}, u32[]{:S(2)}, u32[]{:S(2)}) collective-permute-start(bf16[28,64,128]{2,1,0:T(8,128)(2,1)S(1)} %quad_join.2.mine), channel_id=1, source_target_pairs={{0,8},{1,9},{2,10},{3,11},{4,12},{5,13},{6,14},{7,15},{8,0},{9,1},... | collective-permute-start | bytes 1376264 | tf_op jit(solution)/shard_map/ppermute | solution.py:353
  101.1 9.9 %collective-permute-start.33 = (bf16[28,64,128]{2,1,0:T(8,128)(2,1)S(1)}, bf16[28,64,128]{2,1,0:T(8,128)(2,1)S(1)}, u32[]{:S(2)}, u32[]{:S(2)}) collective-permute-start(bf16[28,64,128]{2,1,0:T(8,128)(2,1)S(1)} %quad_join.3.mine), channel_id=1, source_target_pairs={{0,8},{1,9},{2,10},{3,11},{4,12},{5,13},{6,14},{7,15},{8,0},{9,1},... | collective-permute-start | bytes 1376264 | tf_op jit(solution)/shard_map/ppermute | solution.py:353
  (25 other events, 211.6 us)
where the time goes:
time: 114 us; the launch traced here: 113 us
  starting transfers between devices  56.8 us (50%)
  Pallas kernels  27.5 us (24%)
  waiting for transfers between devices  19.7 us (17%)
  local copies, waits for them, and re-layouts  7.87 us (7%)
    pallas_call x20, Pallas kernels, call(): pl.pallas_call(kernel, out_shape=shapes, in_specs=[SMEM] * len(scalars) +...  27.5 us
    ppermute x12, starting transfers between devices, halo(): sides += [lax.ppermute(rows, axis, even), lax.ppermute(rows, axis, odd)]  23.9 us
    ppermute x22, starting transfers between devices, swap(): return lax.ppermute(rows, ('tile', 'dev'), pairs)  22.2 us
    ppermute x22, waiting for transfers between devices, swap(): return lax.ppermute(rows, ('tile', 'dev'), pairs)  12.1 us
    unnamed x26, local copies, waits for them, and re-layouts  7.71 us
    all_to_all x1, starting transfers between devices, per_device(): lax.all_to_all(outgoing, 'dev', split_axis=0, concat_axis=0, tiled=True)  7.29 us
    all_to_all x1, waiting for transfers between devices, per_device(): lax.all_to_all(returning, 'dev', split_axis=0, concat_axis=0, tiled=True)  6.29 us
    all_to_all x1, starting transfers between devices, per_device(): lax.all_to_all(returning, 'dev', split_axis=0, concat_axis=0, tiled=True)  3.41 us
  transfers between devices with their start and end apart: 36, of which 10 were waited for; matrix products, arithmetic and copies ran while one was open for 0% of the time, Pallas kernels for 15%

commit v1 on v0

v1 whole, which is shorter than its diff:
```python
import functools
import math

import jax
import jax.numpy as jnp
from jax import lax
from jax.experimental import pallas as pl
from jax.experimental.pallas import tpu as pltpu
from jax.sharding import PartitionSpec as P

EDGE = 4
OFFSETS = 27
LABEL_ROWS = 16
WAIT = 1_500_000_000
BF16 = jnp.bfloat16
F32 = jnp.float32


def cube_plan():
    cell = {}
    for i in range(EDGE):
        for j in range(EDGE):
            for k in range(EDGE):
                cell[(i + 1, j + 1, k + 1)] = (i * EDGE + j) * EDGE + k
    copies = []
    free = EDGE**3
    for offset in range(OFFSETS):
        steps = (offset // 9 - 1, offset // 3 % 3 - 1, offset % 3 - 1)
        if steps == (0, 0, 0):
            continue
        ranges = [
            {-1: [(0, EDGE - 1)], 0: [(u + 1, u) for u in range(EDGE)], 1: [(EDGE + 1, 0)]}[step]
            for step in steps
        ]
        sources = []
        for x, i in ranges[0]:
            for y, j in ranges[1]:
                for z, k in ranges[2]:
                    cell[(x, y, z)] = free + len(sources)
                    sources.append((i * EDGE + j) * EDGE + k)
        at = 0
        while at < len(sources):
            count, stride = 1, 1
            if at + 1 < len(sources):
                stride = sources[at + 1] - sources[at]
                while (
                    at + count < len(sources)
                    and sources[at + count] - sources[at + count - 1] == stride
                ):
                    count += 1
            if count == 1:
                stride = 1
            copies.append((offset, sources[at], count, stride, free + at))
            at += count
        free += len(sources)
    return cell, copies, free


CELL, COPIES, CELLS = cube_plan()


def cell_runs(offset, flip):
    steps = (offset // 9, offset // 3 % 3, offset % 3)
    if flip:
        steps = tuple(2 - step for step in steps)
    runs = []
    for i in range(EDGE):
        for j in range(EDGE):
            for k in range(EDGE):
                at = CELL[(i + steps[0], j + steps[1], k + steps[2])]
                if runs and runs[-1][0] + runs[-1][1] == at:
                    runs[-1][1] += 1
                else:
                    runs.append([at, 1])
    return runs


def parity(axis, bit=0):
    return (lax.axis_index(axis) >> bit) & 1


def fill_table(table, own, sides, at=None):
    blocks = own.shape[0]
    rims = sides[0].shape[0] if at is None else sides[0].shape[1]
    tile_odd = parity("tile")
    dev_odd = parity("dev")
    firsts = (
        blocks + rims * (1 - tile_odd),
        blocks + rims * tile_odd,
        blocks + rims * (3 - dev_odd),
        blocks + rims * (2 + dev_odd),
    )
    table[0:blocks] = own[...].astype(F32)
    for first, side in zip(firsts, sides):
        table[pl.ds(first, rims)] = (side[...] if at is None else side[at]).astype(F32)
    table[blocks + 4 * rims] = jnp.zeros(table.shape[1:], F32)


def fill_cells(cells, table, near, blocks):
    voxels = table.shape[1]
    for a in range(blocks):
        cells[pl.ds(a, voxels, stride=blocks), :] = table[a]
        for offset, first, count, stride, at in COPIES:
            e = near[a, offset]
            source = pl.ds(first, count) if stride == 1 else pl.ds(first, count, stride=stride)
            if count == 1:
                cells[pl.ds(at * blocks + a, 1), :] = table[e, source, :]
            else:
                cells[pl.ds(at * blocks + a, count, stride=blocks), :] = table[e, source, :]


def fill_columns(columns, cells, blocks, flip):
    channels = cells.shape[1]
    for offset in range(OFFSETS):
        parts = [
            cells[pl.ds(at * blocks, count * blocks), :] for at, count in cell_runs(offset, flip)
        ]
        columns[:, offset * channels : (offset + 1) * channels] = jnp.concatenate(
            parts, axis=0
        ).astype(BF16)


def flipped_dot(columns, weight):
    channels = weight.shape[1]
    total = jnp.zeros((columns.shape[0], channels), F32)
    for offset in range(OFFSETS):
        part = slice(offset * channels, (offset + 1) * channels)
        total = total + lax.dot_general(
            columns[:, part], weight[part, :], (((1,), (1,)), ((), ())), preferred_element_type=F32
        )
    return total


def fetch(sems, *pairs):
    copies = [
        pltpu.make_async_copy(source, target, sems.at[n])
        for n, (source, target) in enumerate(pairs)
    ]
    for copy in copies:
        copy.start()
    return copies


def places_of(morton_pos, blocks):
    devs = [lax.div(morton_pos[r], blocks) for r in range(blocks)]
    places = []
    for r in range(blocks):
        place = jnp.int32(0)
        for earlier in range(r):
            place = place + (devs[earlier] == devs[r]).astype(jnp.int32)
        places.append(place)
    return devs, places


def pack_kernel(
    morton_hbm, rim_hbm, features_hbm, cotangent_hbm,
    outgoing, rim_rows, rim_tiles, morton_pos, rim, features, cotangent, sems,
):
    blocks, voxels, channels = features.shape
    peers, rows, _ = outgoing.shape
    capacity = (rows - LABEL_ROWS) // voxels
    copies = fetch(
        sems, (morton_hbm, morton_pos), (features_hbm, features), (rim_hbm, rim),
        (cotangent_hbm, cotangent),
    )
    outgoing[...] = jnp.zeros(outgoing.shape, BF16)
    for p in range(peers):
        outgoing[p, capacity * voxels :, :] = jnp.full((LABEL_ROWS, channels), blocks, BF16)
    row = lax.broadcasted_iota(jnp.int32, (LABEL_ROWS, channels), 0)
    copies[0].wait()
    devs, places = places_of(morton_pos, blocks)
    copies[1].wait()
    for r in range(blocks):
        slot = morton_pos[r] - devs[r] * blocks
        place = places[r]
        outgoing[devs[r], pl.ds(pl.multiple_of(place * voxels, voxels), voxels), :] = features[r]
        held = outgoing[devs[r], capacity * voxels :, :].astype(F32)
        outgoing[devs[r], capacity * voxels :, :] = jnp.where(
            row == place, slot.astype(F32), held
        ).astype(BF16)
    copies[2].wait()
    copies[3].wait()
    for h in range(rim_rows.shape[0]):
        rim_rows[h] = cotangent[rim[h]]
        rim_tiles[h] = jnp.full(rim_tiles.shape[1:], rim[h].astype(F32), F32)


def tiles_of(rows):
    return rows.astype(F32).reshape(-1, 8, rows.shape[-1])


def unpack_kernel(arrived, rim_tiles, morton, rim_rows, labels):
    blocks, voxels, channels = morton.shape
    peers, rows, _ = arrived.shape
    capacity = (rows - LABEL_ROWS) // voxels
    held = [jnp.zeros((voxels // 8, 8, channels), F32) for _ in range(blocks)]
    for p in range(peers):
        for c in range(capacity):
            label = jnp.broadcast_to(
                arrived[p, capacity * voxels :, :].astype(F32)[c : c + 1], (8, channels)
            )
            labels[p * capacity + c] = label
            block = tiles_of(arrived[p, c * voxels : (c + 1) * voxels, :])
            for r in range(blocks):
                held[r] = jnp.where((label == r)[None], block, held[r])
    for r in range(blocks):
        morton[r] = held[r].reshape(voxels, channels).astype(BF16)
    for h in range(rim_rows.shape[0]):
        block = held[0]
        for r in range(1, blocks):
            block = jnp.where((rim_tiles[h] == r)[None], held[r], block)
        rim_rows[h] = block.reshape(voxels, channels).astype(BF16)


def first_kernel(
    near_hbm, cotangent_hbm, weight_hbm, side_a, side_b, side_c, side_d,
    columns, hidden_grad, near, cotangent, weight, table, cells, sems,
):
    blocks = cotangent.shape[0]
    copies = fetch(sems, (near_hbm, near), (cotangent_hbm, cotangent), (weight_hbm, weight))
    copies[1].wait()
    fill_table(table, cotangent, (side_a, side_b, side_c, side_d))
    copies[0].wait()
    fill_cells(cells, table, near, blocks)
    fill_columns(columns, cells, blocks, True)
    copies[2].wait()
    hidden_grad[...] = flipped_dot(columns, weight)


def store_halves(keep, send, offset, part, low):
    half = part.shape[0] // 2
    keep[offset] = jnp.where(low, part[:half], part[half:])
    send[offset] = jnp.where(low, part[half:], part[:half])


def middle_kernel(
    near_hbm, rim_hbm, weight_hbm, morton, side_a, side_b, side_c, side_d, grad_columns,
    hidden_grad, hidden, pre_grad, rim_rows, keep_two, send_two, keep_one, send_one,
    near, rim, weight, table, cells, columns, hidden_va, pre_grad_va, sems,
):
    blocks, voxels, channels = morton.shape
    copies = fetch(sems, (near_hbm, near), (rim_hbm, rim), (weight_hbm, weight))
    fill_table(table, morton, (side_a, side_b, side_c, side_d))
    copies[0].wait()
    fill_cells(cells, table, near, blocks)
    fill_columns(columns, cells, blocks, False)
    copies[1].wait()
    copies[2].wait()
    pre_one = jnp.dot(columns[...], weight[...], preferred_element_type=F32)
    gate = jax.nn.sigmoid(pre_one)
    hidden_flat = (pre_one * gate).astype(BF16)
    pre_grad_flat = (hidden_grad[...] * gate * (1.0 + pre_one * (1.0 - gate))).astype(BF16)
    hidden_va[...] = hidden_flat.astype(F32)
    pre_grad_va[...] = pre_grad_flat.astype(F32)
    for a in range(blocks):
        hidden[a] = hidden_va[pl.ds(a, voxels, stride=blocks), :].astype(BF16)
        pre_grad[a] = pre_grad_va[pl.ds(a, voxels, stride=blocks), :].astype(BF16)
    for h in range(rim_rows.shape[1]):
        rim_rows[0, h] = hidden[rim[h]]
        rim_rows[1, h] = pre_grad[rim[h]]
    low = jnp.full((channels // 2, channels), parity("tile"), jnp.int32) == 0
    turned = hidden_flat.T
    for offset in range(0, OFFSETS, 2):
        count = min(2, OFFSETS - offset)
        part = jnp.dot(
            turned,
            grad_columns[:, offset * channels : (offset + count) * channels],
            preferred_element_type=F32,
        )
        for u in range(count):
            store_halves(
                keep_two, send_two, offset + u, part[:, u * channels : (u + 1) * channels], low
            )
    turned = pre_grad_flat.T
    for offset in range(0, OFFSETS, 2):
        count = min(2, OFFSETS - offset)
        part = jnp.dot(
            turned,
            columns[:, offset * channels : (offset + count) * channels],
            preferred_element_type=F32,
        )
        for u in range(count):
            store_halves(
                keep_one, send_one, offset + u, part[:, u * channels : (u + 1) * channels].T, low
            )
    for ref in (keep_two, send_two, keep_one, send_one):
        ref[OFFSETS] = jnp.zeros(ref.shape[1:], F32)


def back_kernel(
    near_hbm, cotangent_hbm, weight_hbm, pre_grad, side_a, side_b, side_c, side_d, labels,
    returning, near, cotangent, weight, table, cells, columns, result, sems,
):
    blocks, voxels, channels = cotangent.shape
    peers, rows, _ = returning.shape
    capacity = rows // voxels
    copies = fetch(sems, (near_hbm, near), (cotangent_hbm, cotangent), (weight_hbm, weight))
    fill_table(table, pre_grad, (side_a, side_b, side_c, side_d), 1)
    copies[0].wait()
    fill_cells(cells, table, near, blocks)
    fill_columns(columns, cells, blocks, True)
    copies[1].wait()
    copies[2].wait()
    result[...] = flipped_dot(columns, weight)
    natural = [
        tiles_of(result[pl.ds(a, voxels, stride=blocks), :] + cotangent[a].astype(F32))
        for a in range(blocks)
    ]
    for p in range(peers):
        for c in range(capacity):
            label = labels[p * capacity + c]
            block = natural[0]
            for r in range(1, blocks):
                block = jnp.where((label == r)[None], natural[r], block)
            returning[p, c * voxels : (c + 1) * voxels, :] = block.reshape(
                voxels, channels
            ).astype(BF16)


def output_kernel(
    capacity, near_hbm, morton_hbm, weight_hbm, hidden, morton, side_a, side_b, side_c, side_d,
    output, flat_tiles, near, morton_pos, weight, table, cells, columns, result, sems,
):
    blocks, voxels, channels = morton.shape
    copies = fetch(sems, (near_hbm, near), (weight_hbm, weight), (morton_hbm, morton_pos))
    fill_table(table, hidden, (side_a, side_b, side_c, side_d), 0)
    copies[0].wait()
    fill_cells(cells, table, near, blocks)
    fill_columns(columns, cells, blocks, False)
    copies[1].wait()
    result[...] = jnp.dot(columns[...], weight[...], preferred_element_type=F32)
    for a in range(blocks):
        output[a] = (
            morton[a].astype(F32) + result[pl.ds(a, voxels, stride=blocks), :]
        ).astype(BF16)
    copies[2].wait()
    devs, places = places_of(morton_pos, blocks)
    for r in range(blocks):
        flat_tiles[r] = jnp.full(
            flat_tiles.shape[1:], (devs[r] * capacity + places[r]).astype(F32), F32
        )


def restore_kernel(coming_back, flat_tiles, input_grad):
    blocks, voxels, channels = input_grad.shape
    slots = coming_back.shape[0]
    held = [jnp.zeros((voxels // 8, 8, channels), F32) for _ in range(blocks)]
    for s in range(slots):
        block = tiles_of(coming_back[s])
        for r in range(blocks):
            held[r] = jnp.where((flat_tiles[r] == s)[None], block, held[r])
    for r in range(blocks):
        input_grad[r] = held[r].reshape(voxels, channels).astype(BF16)


def quad_index():
    return parity("tile", 1) + 2 * parity("dev")


def core_sum_kernel(keep, received, total, out_a, out_b, out_c):
    rows = total.shape[1]
    mine = quad_index()

    def part(index):
        at = pl.ds(pl.multiple_of(index * rows, rows), rows)
        return keep[:, at, :] + received[:, at, :]

    total[...] = part(mine)
    out_a[...] = part(mine ^ 1).astype(BF16)
    out_b[...] = part(mine ^ 2).astype(BF16)
    out_c[...] = part(mine ^ 3).astype(BF16)


def quad_sum_kernel(total, in_a, in_b, in_c, keep, send):
    count = keep.shape[0]
    side = parity("dev", 1)

    def part(index):
        at = pl.ds(index * count, count)
        return (
            total[at] + in_a[at].astype(F32) + in_b[at].astype(F32) + in_c[at].astype(F32)
        )

    keep[...] = part(side)
    send[...] = part(1 - side).astype(send.dtype)


def add_kernel(left, right, total):
    total[...] = (left[...].astype(F32) + right[...].astype(F32)).astype(total.dtype)


def join_kernel(mine, other, joined):
    count = mine.shape[0]
    side = parity("dev", 1)
    joined[pl.ds(side * count, count)] = mine[...]
    joined[pl.ds((1 - side) * count, count)] = other[...]


def quad_join_kernel(mine, in_a, in_b, in_c, joined):
    rows = mine.shape[1]
    index = quad_index()
    for m, ref in enumerate((mine, in_a, in_b, in_c)):
        joined[:, pl.ds(pl.multiple_of((index ^ m) * rows, rows), rows), :] = ref[...]


def finish_kernel(scale, mine, other, grad_hbm, grad, sems):
    rows, channels = mine.shape[1:]
    core = parity("tile")
    first = pl.multiple_of(core * rows, rows)
    second = pl.multiple_of((1 - core) * rows, rows)
    group = OFFSETS // 3
    copies = []
    for n in range(3):
        for offset in range(n * group, (n + 1) * group):
            grad[pl.ds(offset * channels + first, rows), :] = mine[offset].astype(F32) * scale
            grad[pl.ds(offset * channels + second, rows), :] = other[offset].astype(F32) * scale
        part = pl.ds(n * group * channels, group * channels)
        copies.append(pltpu.make_async_copy(grad.at[part], grad_hbm.at[part], sems.at[n]))
        copies[-1].start()
    for copy in copies:
        copy.wait()


HBM = pl.BlockSpec(memory_space=pltpu.HBM)
VMEM = pl.BlockSpec(memory_space=pltpu.VMEM)


def call(kernel, far, arrays, outs, scratch=(), far_outs=(), flops=0, name=None):
    shapes = [jax.ShapeDtypeStruct(shape, dtype) for shape, dtype in [*outs, *far_outs]]
    moved = sum(x.size * x.dtype.itemsize for x in [*far, *arrays])
    moved += sum(math.prod(s.shape) * s.dtype.itemsize for s in shapes)
    held = []
    for item in scratch:
        if isinstance(item, int):
            held.append(pltpu.SemaphoreType.DMA((item,)))
        else:
            held.append((pltpu.SMEM if item[1] == jnp.int32 else pltpu.VMEM)(*item))
    return pl.pallas_call(
        kernel,
        out_shape=shapes,
        in_specs=[HBM] * len(far) + [VMEM] * len(arrays),
        out_specs=[VMEM] * len(outs) + [HBM] * len(far_outs),
        scratch_shapes=held,
        compiler_params=pltpu.CompilerParams(vmem_limit_bytes=(63 if name == "pack" else 24) * 2**20),
        cost_estimate=pl.CostEstimate(flops=flops, bytes_accessed=moved, transcendentals=0),
        name=name,
    )(*far, *arrays)


def halo(rows):
    sides = []
    for axis in ("tile", "dev"):
        count = lax.axis_size(axis)
        even = [(i, i ^ 1) for i in range(count)]
        odd = []
        for i in range(1, count - 1, 2):
            odd += [(i, i + 1), (i + 1, i)]
        sides += [lax.ppermute(rows, axis, even), lax.ppermute(rows, axis, odd)]
    return sides


def swap(rows, tile_bit, dev_bit):
    tiles, devs = lax.axis_size("tile"), lax.axis_size("dev")
    pairs = [
        (t * devs + d, (t ^ tile_bit) * devs + (d ^ dev_bit))
        for t in range(tiles)
        for d in range(devs)
    ]
    return lax.ppermute(rows, ("tile", "dev"), pairs)


def reduce_all(keep, send, scale):
    tiles, devs = lax.axis_size("tile"), lax.axis_size("dev")
    count, rows, channels = keep.shape
    quarter = rows // 4
    small = (count, quarter, channels)
    received = swap(send, 1, 0)
    total, out_a, out_b, out_c = call(
        core_sum_kernel, [], [keep, received],
        [(small, F32), (small, BF16), (small, BF16), (small, BF16)], name="core_sum",
    )
    in_a, in_b, in_c = swap(out_a, 2, 0), swap(out_b, 0, 1), swap(out_c, 2, 1)
    part = (count // 2, quarter, channels)
    keep, send = call(
        quad_sum_kernel, [], [total, in_a, in_b, in_c], [(part, F32), (part, F32)],
        name="quad_sum",
    )
    received = swap(send, 0, 2)
    rest = [(0, 1 << bit) for bit in range(2, devs.bit_length() - 1)]
    rest += [(1 << bit, 0) for bit in range(2, tiles.bit_length() - 1)]
    wire = BF16 if len(rest) == 1 else F32
    (mine,) = call(add_kernel, [], [keep, received], [(part, wire)], name="pair_sum")
    for step, (tile_bit, dev_bit) in enumerate(rest):
        other = swap(mine, tile_bit, dev_bit)
        kind = BF16 if step == len(rest) - 1 else wire
        (mine,) = call(add_kernel, [], [mine, other], [(part, kind)], name="far_sum")
    other = swap(mine, 0, 2)
    (mine,) = call(join_kernel, [], [mine, other], [(small, BF16)], name="pair_join")
    others = [swap(mine, 2, 0), swap(mine, 0, 1), swap(mine, 2, 1)]
    (mine,) = call(
        quad_join_kernel, [], [mine, *others], [((count, rows, channels), BF16)],
        name="quad_join",
    )
    other = swap(mine, 1, 0)
    whole = ((OFFSETS * channels, channels), F32)
    (grad,) = call(
        functools.partial(finish_kernel, scale), [], [mine, other], [], [whole, 3], [whole],
        name="finish",
    )
    return grad


def per_device(features, morton_pos, neighbours, rim, cotangent, weight_one, weight_two):
    blocks, voxels, channels = features.shape
    rims = rim.shape[0]
    peers = lax.axis_size("dev")
    tiles = lax.axis_size("tile")
    capacity = 2 * ((blocks + peers - 1) // peers)
    block = ((blocks, voxels, channels), BF16)
    rows = blocks * voxels
    depth = OFFSETS * channels
    near = ((blocks, OFFSETS), jnp.int32)
    table = ((blocks + 4 * rims + 1, voxels, channels), F32)
    cells = ((CELLS * blocks, channels), F32)
    columns = ((rows, depth), BF16)
    weight = ((depth, channels), BF16)
    flat = ((rows, channels), F32)
    rim_shape = (rims, voxels, channels)
    macs = rows * depth * channels

    outgoing, cot_rim, rim_tiles = call(
        pack_kernel, [morton_pos, rim, features, cotangent], [],
        [((peers, capacity * voxels + LABEL_ROWS, channels), BF16), (rim_shape, BF16),
         ((rims, 8, channels), F32)],
        [((blocks,), jnp.int32), ((rims,), jnp.int32), block, block, 4], name="pack",
    )
    arrived = lax.all_to_all(outgoing, "dev", split_axis=0, concat_axis=0, tiled=True)
    cot_sides = halo(cot_rim)
    grad_columns, hidden_grad = call(
        first_kernel, [neighbours, cotangent, weight_two], cot_sides, [columns, flat],
        [near, block, weight, table, cells, 3], flops=2 * macs, name="hidden_grad",
    )
    morton, morton_rim, labels = call(
        unpack_kernel, [], [arrived, rim_tiles],
        [block, (rim_shape, BF16), ((peers * capacity, 8, channels), F32)], flops=2 * WAIT, name="unpack",
    )
    sides = halo(morton_rim)
    padded = (OFFSETS + 1, channels // 2, channels)
    hidden, pre_grad, rim_rows, keep_two, send_two, keep_one, send_one = call(
        middle_kernel, [neighbours, rim, weight_one], [morton, *sides, grad_columns, hidden_grad],
        [block, block, ((2,) + rim_shape, BF16)] + [(padded, F32)] * 4,
        [near, ((rims,), jnp.int32), weight, table, cells, columns, flat, flat, 3],
        flops=6 * macs, name="middle",
    )
    scale = 1.0 / math.sqrt(blocks * voxels * tiles * peers)
    grad_two = reduce_all(keep_two, send_two, scale)
    grad_one = reduce_all(keep_one, send_one, scale)
    sides = halo(rim_rows)
    (returning,) = call(
        back_kernel, [neighbours, cotangent, weight_one], [pre_grad, *sides, labels],
        [((peers, capacity * voxels, channels), BF16)],
        [near, block, weight, table, cells, columns, flat, 3], flops=2 * macs, name="back",
    )
    coming_back = lax.all_to_all(returning, "dev", split_axis=0, concat_axis=0, tiled=True)
    output, flat_tiles = call(
        functools.partial(output_kernel, capacity), [neighbours, morton_pos, weight_two],
        [hidden, morton, *sides], [block, ((blocks, 8, channels), F32)],
        [near, ((blocks,), jnp.int32), weight, table, cells, columns, flat, 3], flops=2 * macs, name="output",
    )
    (input_grad,) = call(
        restore_kernel, [], [coming_back.reshape(peers * capacity, voxels, channels), flat_tiles],
        [block], name="restore",
    )
    return (output, input_grad, grad_one, grad_two)


def solution(mesh):
    placed = (
        P(("tile", "dev"), None, None),
        P(("tile", "dev")),
        P(("tile", "dev"), None),
        P(("tile", "dev")),
        P(("tile", "dev"), None, None),
        P(),
        P(),
    )
    return jax.shard_map(
        per_device,
        mesh=mesh,
        in_specs=placed,
        out_specs=(P(("tile", "dev"), None, None), P(("tile", "dev"), None, None), P(), P()),
        check_vma=False,
    )
```

time: 114 us -> 98.4 us (0.86)
  Pallas kernels: 27.5 us -> 20.1 us
  local copies, waits for them, and re-layouts: 7.87 us -> 1.91 us
  starting transfers between devices: 56.8 us -> 53 us
  waiting for transfers between devices: 19.7 us -> 21.7 us
    pallas_call x20 -> x21, Pallas kernels: 27.5 us -> 20.1 us  [call(): pl.pallas_call(kernel, out_shape=shapes, in_specs=[HBM] * len(far) + [VME...]
    unnamed x26 -> x16, local copies, waits for them, and re-layouts: 7.71 us -> 1.91 us
    ppermute x22, waiting for transfers between devices: 12.1 us -> 17.4 us  [swap(): return lax.ppermute(rows, ('tile', 'dev'), pairs)]
    ppermute x22, starting transfers between devices: 22.2 us -> 18 us  [swap(): return lax.ppermute(rows, ('tile', 'dev'), pairs)]
    all_to_all x1, waiting for transfers between devices: 6.29 us -> 3.04 us  [per_device(): lax.all_to_all(returning, 'dev', split_axis=0, concat_axis=0, tiled=True)]
  transfers between devices with their start and end apart: 36 -> 36, of which waited for: 10 -> 11; matrix products, arithmetic and copies ran while one was open for 0% -> 0% of each run, Pallas kernels for 15% -> 12%
where the time goes in v1:
time: 98.4 us; the launch traced here: 97.8 us
  starting transfers between devices  53 us (54%)
  waiting for transfers between devices  21.7 us (22%)
  Pallas kernels  20.1 us (20%)
  local copies, waits for them, and re-layouts  1.91 us (2%)
  between operations  1.01 us (1%)
    ppermute x12, starting transfers between devices, halo(): sides += [lax.ppermute(rows, axis, even), lax.ppermute(rows, axis, odd)]  24.3 us
    pallas_call x21, Pallas kernels, call(): pl.pallas_call(kernel, out_shape=shapes, in_specs=[HBM] * len(far) + [VME...  20.1 us
    ppermute x22, starting transfers between devices, swap(): return lax.ppermute(rows, ('tile', 'dev'), pairs)  18 us
    ppermute x22, waiting for transfers between devices, swap(): return lax.ppermute(rows, ('tile', 'dev'), pairs)  17.4 us
    all_to_all x1, starting transfers between devices, per_device(): lax.all_to_all(outgoing, 'dev', split_axis=0, concat_axis=0, tiled=True)  7.29 us
    all_to_all x1, starting transfers between devices, per_device(): lax.all_to_all(returning, 'dev', split_axis=0, concat_axis=0, tiled=True)  3.42 us
    all_to_all x1, waiting for transfers between devices, per_device(): lax.all_to_all(returning, 'dev', split_axis=0, concat_axis=0, tiled=True)  3.04 us
  transfers between devices with their start and end apart: 36, of which 11 were waited for; matrix products, arithmetic and copies ran while one was open for 0% of the time, Pallas kernels for 12%

profile of v1, /device:TPU:0, one launch (start us, length us, event | category | flops | bytes accessed | tf_op | source)
XLA Modules:
  0.0 97.8 jit_solution(10593284407413726035)
XLA Ops:
  0.6 1.7 %pack.1 = (bf16[8,144,128]{2,1,0:T(8,128)(2,1)}, bf16[4,64,128]{2,1,0:T(8,128)(2,1)}, f32[4,8,128]{2,1,0:T(8,128)}) custom-call(s32[8]{0:T(128)} %morton_hbm.3, s32[4]{0:T(128)} %rim_hbm.3, bf16[8,64,128]{2,1,0:T(8,128)(2,1)} %features_hbm.1, bf16[8,64,128]{2,1,0:T(8,128)(2,1)} %cotangent_hbm.5), custom_call_target="tpu_custom_call" | custom-call | bytes 639024 | tf_op jit(solution)/shard_map/pack/pallas_call | solution.py:438
  2.4 7.3 %all-to-all-start = ((bf16[8,144,128]{2,1,0:T(8,128)(2,1)}), bf16[8,144,128]{2,1,0:T(8,128)(2,1)S(1)}, u32[]{:S(2)}, u32[]{:S(2)}) async-start(bf16[8,144,128]{2,1,0:T(8,128)(2,1)} %get-tuple-element.33), calls=%async_computation | async-start | bytes 589824 | tf_op jit(solution)/shard_map/all_to_all | solution.py:537
  10.3 4.8 %collective-permute-start.6 = (bf16[4,64,128]{2,1,0:T(8,128)(2,1)}, bf16[4,64,128]{2,1,0:T(8,128)(2,1)S(1)}, u32[]{:S(2)}, u32[]{:S(2)}) collective-permute-start(bf16[4,64,128]{2,1,0:T(8,128)(2,1)} %get-tuple-element.37), channel_id=1, source_target_pairs={{0,1},{1,0},{2,3},{3,2},{4,5},{5,4},{6,7},{7,6},{8,9},{9,8},{10,11... | collective-permute-start | bytes 196616 | tf_op jit(solution)/shard_map/ppermute | solution.py:458
  15.8 2.9 %collective-permute-start.4 = (bf16[4,64,128]{2,1,0:T(8,128)(2,1)}, bf16[4,64,128]{2,1,0:T(8,128)(2,1)S(1)}, u32[]{:S(2)}, u32[]{:S(2)}) collective-permute-start(bf16[4,64,128]{2,1,0:T(8,128)(2,1)} %get-tuple-element.37), channel_id=1, source_target_pairs={{0,8},{8,0},{16,24},{24,16},{1,9},{9,1},{17,25},{25,17},{2,10},{10... | collective-permute-start | bytes 196616 | tf_op jit(solution)/shard_map/ppermute | solution.py:458
  21.8 3.1 %collective-permute-start.2 = (bf16[4,64,128]{2,1,0:T(8,128)(2,1)S(1)}, bf16[4,64,128]{2,1,0:T(8,128)(2,1)S(1)}, u32[]{:S(2)}, u32[]{:S(2)}) collective-permute-start(bf16[4,64,128]{2,1,0:T(8,128)(2,1)S(1)} %get-tuple-element.36), channel_id=1, source_target_pairs={{0,1},{1,0},{2,3},{3,2},{4,5},{5,4},{6,7},{7,6},{8,9},{9,8},{10,11... | collective-permute-start | bytes 196616 | tf_op jit(solution)/shard_map/ppermute | solution.py:458
  25.6 2.9 %collective-permute-start = (bf16[4,64,128]{2,1,0:T(8,128)(2,1)S(1)}, bf16[4,64,128]{2,1,0:T(8,128)(2,1)S(1)}, u32[]{:S(2)}, u32[]{:S(2)}) collective-permute-start(bf16[4,64,128]{2,1,0:T(8,128)(2,1)S(1)} %get-tuple-element.36), channel_id=1, source_target_pairs={{0,8},{8,0},{16,24},{24,16},{1,9},{9,1},{17,25},{25,17},{2,10},{10... | collective-permute-start | bytes 196616 | tf_op jit(solution)/shard_map/ppermute | solution.py:458
  28.5 2.4 %hidden_grad.1 = (bf16[512,3456]{1,0:T(8,128)(2,1)S(1)}, f32[512,128]{1,0:T(8,128)S(1)}) custom-call(s32[8,27]{1,0:T(8,128)S(1)} %copy-done.2, bf16[8,64,128]{2,1,0:T(8,128)(2,1)S(1)} %copy-done.1, bf16[3456,128]{1,0:T(8,128)(2,1)S(1)} %copy-done.5, bf16[4,64,128]{2,1,0:T(8,128)(2,1)S(1)} %collective-permute-done.4.side_a, ...), custom_call_target="tpu_custom_call" | custom-call | flops 452984832 | bytes 5079904 | tf_op jit(solution)/shard_map/hidden_grad/pallas_call | solution.py:438
  31.0 5.3 %middle.1 = (bf16[8,64,128]{2,1,0:T(8,128)(2,1)S(1)}, bf16[8,64,128]{2,1,0:T(8,128)(2,1)S(1)}, bf16[2,4,64,128]{3,2,1,0:T(8,128)(2,1)S(1)}, f32[28,64,128]{2,1,0...) custom-call(s32[8,27]{1,0:T(8,128)S(1)} %copy-done.2, ...), custom_call_target="tpu_custom_call" | custom-call | flops 1358954496 | bytes 9143152 | tf_op jit(solution)/shard_map/middle/pallas_call | solution.py:438
  36.9 2.0 %collective-permute-done.12.received = f32[28,64,128]{2,1,0:T(8,128)S(1)} collective-permute-done((f32[28,64,128]{2,1,0:T(8,128)S(1)}, f32[28,64,128]{2,1,0:T(8,128)S(1)}, u32[]{:S(2)}, u32[]{:S(2)}) %collective-permute-start.12) | collective-permute-done | bytes 917536 | tf_op jit(solution)/shard_map/ppermute | solution.py:469
  40.1 2.5 %collective-permute-start.15 = (bf16[28,16,128]{2,1,0:T(8,128)(2,1)S(1)}, bf16[28,16,128]{2,1,0:T(8,128)(2,1)S(1)}, u32[]{:S(2)}, u32[]{:S(2)}) collective-permute-start(bf16[28,16,128]{2,1,0:T(8,128)(2,1)S(1)} %get-tuple-element.51), channel_id=1, source_target_pairs={{0,17},{1,16},{2,19},{3,18},{4,21},{5,20},{6,23},{7,22},{8,25},{9,... | collective-permute-start | bytes 344072 | tf_op jit(solution)/shard_map/ppermute | solution.py:469
  46.2 2.8 %collective-permute-done.14.in_b = bf16[28,16,128]{2,1,0:T(8,128)(2,1)S(1)} collective-permute-done((bf16[28,16,128]{2,1,0:T(8,128)(2,1)S(1)}, bf16[28,16,128]{2,1,0:T(8,128)(2,1)S(1)}, u32[]{:S(2)}, u32[]{:S(2)}) %collective-permute-start.14) | collective-permute-done | bytes 114720 | tf_op jit(solution)/shard_map/ppermute | solution.py:469
  50.1 2.2 %collective-permute-done.25.in_b = bf16[28,16,128]{2,1,0:T(8,128)(2,1)S(1)} collective-permute-done((bf16[28,16,128]{2,1,0:T(8,128)(2,1)S(1)}, bf16[28,16,128]{2,1,0:T(8,128)(2,1)S(1)}, u32[]{:S(2)}, u32[]{:S(2)}) %collective-permute-start.25) | collective-permute-done | bytes 114720 | tf_op jit(solution)/shard_map/ppermute | solution.py:469
  52.4 1.6 %collective-permute-start.27 = (f32[14,16,128]{2,1,0:T(8,128)S(1)}, f32[14,16,128]{2,1,0:T(8,128)S(1)}, u32[]{:S(2)}, u32[]{:S(2)}) collective-permute-start(f32[14,16,128]{2,1,0:T(8,128)S(1)} %get-tuple-element.61), channel_id=1, source_target_pairs={{0,2},{1,3},{2,0},{3,1},{4,6},{5,7},{6,4},{7,5},{8,10},{9,11},{10,... | collective-permute-start | bytes 344072 | tf_op jit(solution)/shard_map/ppermute | solution.py:469
  54.2 3.6 %collective-permute-done.27.right = f32[14,16,128]{2,1,0:T(8,128)S(1)} collective-permute-done((f32[14,16,128]{2,1,0:T(8,128)S(1)}, f32[14,16,128]{2,1,0:T(8,128)S(1)}, u32[]{:S(2)}, u32[]{:S(2)}) %collective-permute-start.27) | collective-permute-done | bytes 114720 | tf_op jit(solution)/shard_map/ppermute | solution.py:469
  58.8 2.1 %collective-permute-done.17.right = bf16[14,16,128]{2,1,0:T(8,128)(2,1)S(1)} collective-permute-done((bf16[14,16,128]{2,1,0:T(8,128)(2,1)S(1)}, bf16[14,16,128]{2,1,0:T(8,128)(2,1)S(1)}, u32[]{:S(2)}, u32[]{:S(2)}) %collective-permute-start.17) | collective-permute-done | bytes 57376 | tf_op jit(solution)/shard_map/ppermute | solution.py:469
  61.0 2.5 %collective-permute-done.28.right = bf16[14,16,128]{2,1,0:T(8,128)(2,1)S(1)} collective-permute-done((bf16[14,16,128]{2,1,0:T(8,128)(2,1)S(1)}, bf16[14,16,128]{2,1,0:T(8,128)(2,1)S(1)}, u32[]{:S(2)}, u32[]{:S(2)}) %collective-permute-start.28) | collective-permute-done | bytes 57376 | tf_op jit(solution)/shard_map/ppermute | solution.py:469
  65.1 3.9 %collective-permute-start.10 = (bf16[2,4,64,128]{3,2,1,0:T(8,128)(2,1)S(1)}, bf16[2,4,64,128]{3,2,1,0:T(8,128)(2,1)S(1)}, u32[]{:S(2)}, u32[]{:S(2)}) collective-permute-start(bf16[2,4,64,128]{3,2,1,0:T(8,128)(2,1)S(1)} %get-tuple-element.41), channel_id=1, source_target_pairs={{0,1},{1,0},{2,3},{3,2},{4,5},{5,4},{6,7},{7,6},{8,9},{9,8},{10,11... | collective-permute-start | bytes 393224 | tf_op jit(solution)/shard_map/ppermute | solution.py:458
  69.7 2.6 %collective-permute-start.8 = (bf16[2,4,64,128]{3,2,1,0:T(8,128)(2,1)S(1)}, bf16[2,4,64,128]{3,2,1,0:T(8,128)(2,1)S(1)}, u32[]{:S(2)}, u32[]{:S(2)}) collective-permute-start(bf16[2,4,64,128]{3,2,1,0:T(8,128)(2,1)S(1)} %get-tuple-element.41), channel_id=1, source_target_pairs={{0,8},{8,0},{16,24},{24,16},{1,9},{9,1},{17,25},{25,17},{2,10},{10... | collective-permute-start | bytes 393224 | tf_op jit(solution)/shard_map/ppermute | solution.py:458
  73.8 2.1 %collective-permute-start.19 = (bf16[28,16,128]{2,1,0:T(8,128)(2,1)S(1)}, bf16[28,16,128]{2,1,0:T(8,128)(2,1)S(1)}, u32[]{:S(2)}, u32[]{:S(2)}) collective-permute-start(bf16[28,16,128]{2,1,0:T(8,128)(2,1)S(1)} %pair_join.2.mine), channel_id=1, source_target_pairs={{0,16},{1,17},{2,18},{3,19},{4,20},{5,21},{6,22},{7,23},{8,24},{9,... | collective-permute-start | bytes 344072 | tf_op jit(solution)/shard_map/ppermute | solution.py:469
  76.3 2.2 %collective-permute-start.31 = (bf16[28,16,128]{2,1,0:T(8,128)(2,1)S(1)}, bf16[28,16,128]{2,1,0:T(8,128)(2,1)S(1)}, u32[]{:S(2)}, u32[]{:S(2)}) collective-permute-start(bf16[28,16,128]{2,1,0:T(8,128)(2,1)S(1)} %pair_join.3.mine), channel_id=1, source_target_pairs={{0,1},{1,0},{2,3},{3,2},{4,5},{5,4},{6,7},{7,6},{8,9},{9,8},{10,11... | collective-permute-start | bytes 344072 | tf_op jit(solution)/shard_map/ppermute | solution.py:469
  79.4 3.3 %back.1 = bf16[8,128,128]{2,1,0:T(8,128)(2,1)} custom-call(s32[8,27]{1,0:T(8,128)S(1)} %copy-done.2, bf16[8,64,128]{2,1,0:T(8,128)(2,1)S(1)} %copy-done.1, bf16[3456,128]{1,0:T(8,128)(2,1)S(1)} %copy-done, bf16[8,64,128]{2,1,0:T(8,128)(2,1)S(1)} %get-tuple-element.43.pre_grad, bf16[2,4,64,128]{3,2,1,0:T(8,128)(2,1)S(1)} %collective-permute-done.8.side_a, ...), custom_call_target="tpu_custom_call" | custom-call | flops 452984832 | bytes 1999712 | tf_op jit(solution)/shard_map/back/pallas_call | solution.py:438
  82.8 3.4 %all-to-all-start.1 = ((bf16[8,128,128]{2,1,0:T(8,128)(2,1)}), bf16[8,128,128]{2,1,0:T(8,128)(2,1)S(1)}, u32[]{:S(2)}, u32[]{:S(2)}) async-start(bf16[8,128,128]{2,1,0:T(8,128)(2,1)} %back.1), calls=%async_computation.1 | async-start | bytes 524288 | tf_op jit(solution)/shard_map/all_to_all | solution.py:564
  88.2 3.1 %output.1 = (bf16[8,64,128]{2,1,0:T(8,128)(2,1)}, f32[8,8,128]{2,1,0:T(8,128)S(1)}) custom-call(s32[8,27]{1,0:T(8,128)S(1)} %copy-done.2, s32[8]{0:T(128)S(1)} %copy-done.4, bf16[3456,128]{1,0:T(8,128)(2,1)S(1)} %copy-done.6, bf16[8,64,128]{2,1,0:T(8,128)(2,1)S(1)} %get-tuple-element.40.hidden, bf16[8,64,128]{2,1,0:T(8,128)(2,1)S(1)} %get-tuple-element.35.morton, ...), custom_call_target="tpu_custom_call" | custom-call | flops 452984832 | bytes 1835904 | tf_op jit(solution)/shard_map/output/pallas_call | solution.py:438
  91.3 3.0 %all-to-all-done.1 = bf16[8,128,128]{2,1,0:T(8,128)(2,1)S(1)} async-done(((bf16[8,128,128]{2,1,0:T(8,128)(2,1)}), bf16[8,128,128]{2,1,0:T(8,128)(2,1)S(1)}, u32[]{:S(2)}, u32[]{:S(2)}) %all-to-all-start.1) | async-done | bytes 262176 | tf_op jit(solution)/shard_map/all_to_all | solution.py:564
  (85 shorter events, 23.3 us)
Async XLA Ops:
  2.4 17.6 %all-to-all-start = ((bf16[8,144,128]{2,1,0:T(8,128)(2,1)}), bf16[8,144,128]{2,1,0:T(8,128)(2,1)S(1)}, u32[]{:S(2)}, u32[]{:S(2)}) async-start(bf16[8,144,128]{2,1,0:T(8,128)(2,1)} %get-tuple-element.33), calls=%async_computation | async-start | bytes 589824 | tf_op jit(solution)/shard_map/all_to_all | solution.py:537
  9.7 12.1 %collective-permute-start.7 = (bf16[4,64,128]{2,1,0:T(8,128)(2,1)}, bf16[4,64,128]{2,1,0:T(8,128)(2,1)S(1)}, u32[]{:S(2)}, u32[]{:S(2)}) collective-permute-start(bf16[4,64,128]{2,1,0:T(8,128)(2,1)} %get-tuple-element.37), channel_id=1, source_target_pairs={{1,2},{2,1},{3,4},{4,3},{5,6},{6,5},{9,10},{10,9},{11,12},{12,11},... | collective-permute-start | bytes 196616 | tf_op jit(solution)/shard_map/ppermute | solution.py:458
  10.3 14.6 %collective-permute-start.6 = (bf16[4,64,128]{2,1,0:T(8,128)(2,1)}, bf16[4,64,128]{2,1,0:T(8,128)(2,1)S(1)}, u32[]{:S(2)}, u32[]{:S(2)}) collective-permute-start(bf16[4,64,128]{2,1,0:T(8,128)(2,1)} %get-tuple-element.37), channel_id=1, source_target_pairs={{0,1},{1,0},{2,3},{3,2},{4,5},{5,4},{6,7},{7,6},{8,9},{9,8},{10,11... | collective-permute-start | bytes 196616 | tf_op jit(solution)/shard_map/ppermute | solution.py:458
  15.1 10.5 %collective-permute-start.5 = (bf16[4,64,128]{2,1,0:T(8,128)(2,1)}, bf16[4,64,128]{2,1,0:T(8,128)(2,1)S(1)}, u32[]{:S(2)}, u32[]{:S(2)}) collective-permute-start(bf16[4,64,128]{2,1,0:T(8,128)(2,1)} %get-tuple-element.37), channel_id=1, source_target_pairs={{8,16},{16,8},{9,17},{17,9},{10,18},{18,10},{11,19},{19,11},{12,20... | collective-permute-start | bytes 196616 | tf_op jit(solution)/shard_map/ppermute | solution.py:458
  15.8 12.7 %collective-permute-start.4 = (bf16[4,64,128]{2,1,0:T(8,128)(2,1)}, bf16[4,64,128]{2,1,0:T(8,128)(2,1)S(1)}, u32[]{:S(2)}, u32[]{:S(2)}) collective-permute-start(bf16[4,64,128]{2,1,0:T(8,128)(2,1)} %get-tuple-element.37), channel_id=1, source_target_pairs={{0,8},{8,0},{16,24},{24,16},{1,9},{9,1},{17,25},{25,17},{2,10},{10... | collective-permute-start | bytes 196616 | tf_op jit(solution)/shard_map/ppermute | solution.py:458
  21.0 10.0 %collective-permute-start.3 = (bf16[4,64,128]{2,1,0:T(8,128)(2,1)S(1)}, bf16[4,64,128]{2,1,0:T(8,128)(2,1)S(1)}, u32[]{:S(2)}, u32[]{:S(2)}) collective-permute-start(bf16[4,64,128]{2,1,0:T(8,128)(2,1)S(1)} %get-tuple-element.36), channel_id=1, source_target_pairs={{1,2},{2,1},{3,4},{4,3},{5,6},{6,5},{9,10},{10,9},{11,12},{12,11},... | collective-permute-start | bytes 196616 | tf_op jit(solution)/shard_map/ppermute | solution.py:458
  21.8 9.2 %collective-permute-start.2 = (bf16[4,64,128]{2,1,0:T(8,128)(2,1)S(1)}, bf16[4,64,128]{2,1,0:T(8,128)(2,1)S(1)}, u32[]{:S(2)}, u32[]{:S(2)}) collective-permute-start(bf16[4,64,128]{2,1,0:T(8,128)(2,1)S(1)} %get-tuple-element.36), channel_id=1, source_target_pairs={{0,1},{1,0},{2,3},{3,2},{4,5},{5,4},{6,7},{7,6},{8,9},{9,8},{10,11... | collective-permute-start | bytes 196616 | tf_op jit(solution)/shard_map/ppermute | solution.py:458
  40.0 9.0 %collective-permute-start.14 = (bf16[28,16,128]{2,1,0:T(8,128)(2,1)S(1)}, bf16[28,16,128]{2,1,0:T(8,128)(2,1)S(1)}, u32[]{:S(2)}, u32[]{:S(2)}) collective-permute-start(bf16[28,16,128]{2,1,0:T(8,128)(2,1)S(1)} %get-tuple-element.50), channel_id=1, source_target_pairs={{0,1},{1,0},{2,3},{3,2},{4,5},{5,4},{6,7},{7,6},{8,9},{9,8},{10,11... | collective-permute-start | bytes 344072 | tf_op jit(solution)/shard_map/ppermute | solution.py:469
  40.1 9.0 %collective-permute-start.15 = (bf16[28,16,128]{2,1,0:T(8,128)(2,1)S(1)}, bf16[28,16,128]{2,1,0:T(8,128)(2,1)S(1)}, u32[]{:S(2)}, u32[]{:S(2)}) collective-permute-start(bf16[28,16,128]{2,1,0:T(8,128)(2,1)S(1)} %get-tuple-element.51), channel_id=1, source_target_pairs={{0,17},{1,16},{2,19},{3,18},{4,21},{5,20},{6,23},{7,22},{8,25},{9,... | collective-permute-start | bytes 344072 | tf_op jit(solution)/shard_map/ppermute | solution.py:469
  42.7 7.4 %collective-permute-start.24 = (bf16[28,16,128]{2,1,0:T(8,128)(2,1)S(1)}, bf16[28,16,128]{2,1,0:T(8,128)(2,1)S(1)}, u32[]{:S(2)}, u32[]{:S(2)}) collective-permute-start(bf16[28,16,128]{2,1,0:T(8,128)(2,1)S(1)} %get-tuple-element.57), channel_id=1, source_target_pairs={{0,16},{1,17},{2,18},{3,19},{4,20},{5,21},{6,22},{7,23},{8,24},{9,... | collective-permute-start | bytes 344072 | tf_op jit(solution)/shard_map/ppermute | solution.py:469
  43.7 8.6 %collective-permute-start.25 = (bf16[28,16,128]{2,1,0:T(8,128)(2,1)S(1)}, bf16[28,16,128]{2,1,0:T(8,128)(2,1)S(1)}, u32[]{:S(2)}, u32[]{:S(2)}) collective-permute-start(bf16[28,16,128]{2,1,0:T(8,128)(2,1)S(1)} %get-tuple-element.58), channel_id=1, source_target_pairs={{0,1},{1,0},{2,3},{3,2},{4,5},{5,4},{6,7},{7,6},{8,9},{9,8},{10,11... | collective-permute-start | bytes 344072 | tf_op jit(solution)/shard_map/ppermute | solution.py:469
  44.8 7.5 %collective-permute-start.26 = (bf16[28,16,128]{2,1,0:T(8,128)(2,1)S(1)}, bf16[28,16,128]{2,1,0:T(8,128)(2,1)S(1)}, u32[]{:S(2)}, u32[]{:S(2)}) collective-permute-start(bf16[28,16,128]{2,1,0:T(8,128)(2,1)S(1)} %get-tuple-element.59), channel_id=1, source_target_pairs={{0,17},{1,16},{2,19},{3,18},{4,21},{5,20},{6,23},{7,22},{8,25},{9,... | collective-permute-start | bytes 344072 | tf_op jit(solution)/shard_map/ppermute | solution.py:469
  60.9 8.8 %collective-permute-start.18 = (bf16[14,16,128]{2,1,0:T(8,128)(2,1)S(1)}, bf16[14,16,128]{2,1,0:T(8,128)(2,1)S(1)}, u32[]{:S(2)}, u32[]{:S(2)}) collective-permute-start(bf16[14,16,128]{2,1,0:T(8,128)(2,1)S(1)} %far_sum.2.mine), channel_id=1, source_target_pairs={{0,2},{1,3},{2,0},{3,1},{4,6},{5,7},{6,4},{7,5},{8,10},{9,11},{10,... | collective-permute-start | bytes 172040 | tf_op jit(solution)/shard_map/ppermute | solution.py:469
  63.5 8.8 %collective-permute-start.29 = (bf16[14,16,128]{2,1,0:T(8,128)(2,1)S(1)}, bf16[14,16,128]{2,1,0:T(8,128)(2,1)S(1)}, u32[]{:S(2)}, u32[]{:S(2)}) collective-permute-start(bf16[14,16,128]{2,1,0:T(8,128)(2,1)S(1)} %far_sum.3.mine), channel_id=1, source_target_pairs={{0,2},{1,3},{2,0},{3,1},{4,6},{5,7},{6,4},{7,5},{8,10},{9,11},{10,... | collective-permute-start | bytes 172040 | tf_op jit(solution)/shard_map/ppermute | solution.py:469
  64.4 7.9 %collective-permute-start.11 = (bf16[2,4,64,128]{3,2,1,0:T(8,128)(2,1)S(1)}, bf16[2,4,64,128]{3,2,1,0:T(8,128)(2,1)S(1)}, u32[]{:S(2)}, u32[]{:S(2)}) collective-permute-start(bf16[2,4,64,128]{3,2,1,0:T(8,128)(2,1)S(1)} %get-tuple-element.41), channel_id=1, source_target_pairs={{1,2},{2,1},{3,4},{4,3},{5,6},{6,5},{9,10},{10,9},{11,12},{12,11},... | collective-permute-start | bytes 393224 | tf_op jit(solution)/shard_map/ppermute | solution.py:458
  65.1 8.7 %collective-permute-start.10 = (bf16[2,4,64,128]{3,2,1,0:T(8,128)(2,1)S(1)}, bf16[2,4,64,128]{3,2,1,0:T(8,128)(2,1)S(1)}, u32[]{:S(2)}, u32[]{:S(2)}) collective-permute-start(bf16[2,4,64,128]{3,2,1,0:T(8,128)(2,1)S(1)} %get-tuple-element.41), channel_id=1, source_target_pairs={{0,1},{1,0},{2,3},{3,2},{4,5},{5,4},{6,7},{7,6},{8,9},{9,8},{10,11... | collective-permute-start | bytes 393224 | tf_op jit(solution)/shard_map/ppermute | solution.py:458
  72.4 13.8 %collective-permute-start.20 = (bf16[28,16,128]{2,1,0:T(8,128)(2,1)S(1)}, bf16[28,16,128]{2,1,0:T(8,128)(2,1)S(1)}, u32[]{:S(2)}, u32[]{:S(2)}) collective-permute-start(bf16[28,16,128]{2,1,0:T(8,128)(2,1)S(1)} %pair_join.2.mine), channel_id=1, source_target_pairs={{0,1},{1,0},{2,3},{3,2},{4,5},{5,4},{6,7},{7,6},{8,9},{9,8},{10,11... | collective-permute-start | bytes 344072 | tf_op jit(solution)/shard_map/ppermute | solution.py:469
  73.8 12.4 %collective-permute-start.19 = (bf16[28,16,128]{2,1,0:T(8,128)(2,1)S(1)}, bf16[28,16,128]{2,1,0:T(8,128)(2,1)S(1)}, u32[]{:S(2)}, u32[]{:S(2)}) collective-permute-start(bf16[28,16,128]{2,1,0:T(8,128)(2,1)S(1)} %pair_join.2.mine), channel_id=1, source_target_pairs={{0,16},{1,17},{2,18},{3,19},{4,20},{5,21},{6,22},{7,23},{8,24},{9,... | collective-permute-start | bytes 344072 | tf_op jit(solution)/shard_map/ppermute | solution.py:469
  75.9 10.5 %collective-permute-start.32 = (bf16[28,16,128]{2,1,0:T(8,128)(2,1)S(1)}, bf16[28,16,128]{2,1,0:T(8,128)(2,1)S(1)}, u32[]{:S(2)}, u32[]{:S(2)}) collective-permute-start(bf16[28,16,128]{2,1,0:T(8,128)(2,1)S(1)} %pair_join.3.mine), channel_id=1, source_target_pairs={{0,17},{1,16},{2,19},{3,18},{4,21},{5,20},{6,23},{7,22},{8,25},{9,... | collective-permute-start | bytes 344072 | tf_op jit(solution)/shard_map/ppermute | solution.py:469
  76.3 10.1 %collective-permute-start.31 = (bf16[28,16,128]{2,1,0:T(8,128)(2,1)S(1)}, bf16[28,16,128]{2,1,0:T(8,128)(2,1)S(1)}, u32[]{:S(2)}, u32[]{:S(2)}) collective-permute-start(bf16[28,16,128]{2,1,0:T(8,128)(2,1)S(1)} %pair_join.3.mine), channel_id=1, source_target_pairs={{0,1},{1,0},{2,3},{3,2},{4,5},{5,4},{6,7},{7,6},{8,9},{9,8},{10,11... | collective-permute-start | bytes 344072 | tf_op jit(solution)/shard_map/ppermute | solution.py:469
  79.3 7.1 %collective-permute-start.30 = (bf16[28,16,128]{2,1,0:T(8,128)(2,1)S(1)}, bf16[28,16,128]{2,1,0:T(8,128)(2,1)S(1)}, u32[]{:S(2)}, u32[]{:S(2)}) collective-permute-start(bf16[28,16,128]{2,1,0:T(8,128)(2,1)S(1)} %pair_join.3.mine), channel_id=1, source_target_pairs={{0,16},{1,17},{2,18},{3,19},{4,20},{5,21},{6,22},{7,23},{8,24},{9,... | collective-permute-start | bytes 344072 | tf_op jit(solution)/shard_map/ppermute | solution.py:469
  82.8 11.6 %all-to-all-start.1 = ((bf16[8,128,128]{2,1,0:T(8,128)(2,1)}), bf16[8,128,128]{2,1,0:T(8,128)(2,1)S(1)}, u32[]{:S(2)}, u32[]{:S(2)}) async-start(bf16[8,128,128]{2,1,0:T(8,128)(2,1)} %back.1), calls=%async_computation.1 | async-start | bytes 524288 | tf_op jit(solution)/shard_map/all_to_all | solution.py:564
  86.3 8.9 %collective-permute-start.22 = (bf16[28,64,128]{2,1,0:T(8,128)(2,1)S(1)}, bf16[28,64,128]{2,1,0:T(8,128)(2,1)S(1)}, u32[]{:S(2)}, u32[]{:S(2)}) collective-permute-start(bf16[28,64,128]{2,1,0:T(8,128)(2,1)S(1)} %quad_join.2.mine), channel_id=1, source_target_pairs={{0,8},{1,9},{2,10},{3,11},{4,12},{5,13},{6,14},{7,15},{8,0},{9,1},... | collective-permute-start | bytes 1376264 | tf_op jit(solution)/shard_map/ppermute | solution.py:469
  86.5 10.1 %collective-permute-start.33 = (bf16[28,64,128]{2,1,0:T(8,128)(2,1)S(1)}, bf16[28,64,128]{2,1,0:T(8,128)(2,1)S(1)}, u32[]{:S(2)}, u32[]{:S(2)}) collective-permute-start(bf16[28,64,128]{2,1,0:T(8,128)(2,1)S(1)} %quad_join.3.mine), channel_id=1, source_target_pairs={{0,8},{1,9},{2,10},{3,11},{4,12},{5,13},{6,14},{7,15},{8,0},{9,1},... | collective-permute-start | bytes 1376264 | tf_op jit(solution)/shard_map/ppermute | solution.py:469
  (20 other events, 122.7 us)

commit v2 on v1

v2 whole, which is shorter than its diff:
```python
import functools
import math

import jax
import jax.numpy as jnp
from jax import lax
from jax.experimental import pallas as pl
from jax.experimental.pallas import tpu as pltpu
from jax.sharding import PartitionSpec as P

EDGE = 4
OFFSETS = 27
LABEL_ROWS = 16
WAIT = 1_500_000_000
BF16 = jnp.bfloat16
F32 = jnp.float32


def cube_plan():
    cell = {}
    for i in range(EDGE):
        for j in range(EDGE):
            for k in range(EDGE):
                cell[(i + 1, j + 1, k + 1)] = (i * EDGE + j) * EDGE + k
    copies = []
    free = EDGE**3
    for offset in range(OFFSETS):
        steps = (offset // 9 - 1, offset // 3 % 3 - 1, offset % 3 - 1)
        if steps == (0, 0, 0):
            continue
        ranges = [
            {-1: [(0, EDGE - 1)], 0: [(u + 1, u) for u in range(EDGE)], 1: [(EDGE + 1, 0)]}[step]
            for step in steps
        ]
        sources = []
        for x, i in ranges[0]:
            for y, j in ranges[1]:
                for z, k in ranges[2]:
                    cell[(x, y, z)] = free + len(sources)
                    sources.append((i * EDGE + j) * EDGE + k)
        at = 0
        while at < len(sources):
            count, stride = 1, 1
            if at + 1 < len(sources):
                stride = sources[at + 1] - sources[at]
                while (
                    at + count < len(sources)
                    and sources[at + count] - sources[at + count - 1] == stride
                ):
                    count += 1
            if count == 1:
                stride = 1
            copies.append((offset, sources[at], count, stride, free + at))
            at += count
        free += len(sources)
    return cell, copies, free


CELL, COPIES, CELLS = cube_plan()


def cell_runs(offset, flip):
    steps = (offset // 9, offset // 3 % 3, offset % 3)
    if flip:
        steps = tuple(2 - step for step in steps)
    runs = []
    for i in range(EDGE):
        for j in range(EDGE):
            for k in range(EDGE):
                at = CELL[(i + steps[0], j + steps[1], k + steps[2])]
                if runs and runs[-1][0] + runs[-1][1] == at:
                    runs[-1][1] += 1
                else:
                    runs.append([at, 1])
    return runs


def parity(axis, bit=0):
    return (lax.axis_index(axis) >> bit) & 1


def fill_table(table, own, sides, at=None):
    blocks = own.shape[0]
    rims = sides[0].shape[0] if at is None else sides[0].shape[1]
    tile_odd = parity("tile")
    dev_odd = parity("dev")
    firsts = (
        blocks + rims * (1 - tile_odd),
        blocks + rims * tile_odd,
        blocks + rims * (3 - dev_odd),
        blocks + rims * (2 + dev_odd),
    )
    table[0:blocks] = own[...].astype(F32)
    for first, side in zip(firsts, sides):
        table[pl.ds(first, rims)] = (side[...] if at is None else side[at]).astype(F32)
    table[blocks + 4 * rims] = jnp.zeros(table.shape[1:], F32)


def fill_cells(cells, table, near, blocks):
    voxels = table.shape[1]
    for a in range(blocks):
        cells[pl.ds(a, voxels, stride=blocks), :] = table[a]
        for offset, first, count, stride, at in COPIES:
            e = near[a, offset]
            source = pl.ds(first, count) if stride == 1 else pl.ds(first, count, stride=stride)
            if count == 1:
                cells[pl.ds(at * blocks + a, 1), :] = table[e, source, :]
            else:
                cells[pl.ds(at * blocks + a, count, stride=blocks), :] = table[e, source, :]


def fill_columns(columns, cells, blocks, flip):
    channels = cells.shape[1]
    for offset in range(OFFSETS):
        parts = [
            cells[pl.ds(at * blocks, count * blocks), :] for at, count in cell_runs(offset, flip)
        ]
        columns[:, offset * channels : (offset + 1) * channels] = jnp.concatenate(
            parts, axis=0
        ).astype(BF16)


def flipped_dot(columns, weight):
    channels = weight.shape[1]
    total = jnp.zeros((columns.shape[0], channels), F32)
    for offset in range(OFFSETS):
        part = slice(offset * channels, (offset + 1) * channels)
        total = total + lax.dot_general(
            columns[:, part], weight[part, :], (((1,), (1,)), ((), ())), preferred_element_type=F32
        )
    return total


def fetch(sems, *pairs):
    copies = [
        pltpu.make_async_copy(source, target, sems.at[n])
        for n, (source, target) in enumerate(pairs)
    ]
    for copy in copies:
        copy.start()
    return copies


def places_of(morton_pos, blocks):
    devs = [lax.div(morton_pos[r], blocks) for r in range(blocks)]
    places = []
    for r in range(blocks):
        place = jnp.int32(0)
        for earlier in range(r):
            place = place + (devs[earlier] == devs[r]).astype(jnp.int32)
        places.append(place)
    return devs, places


def pack_kernel(
    morton_hbm, rim_hbm, features_hbm, cotangent_hbm,
    outgoing, rim_rows, morton_pos, rim, features, cotangent, sems,
):
    blocks, voxels, channels = features.shape
    peers, rows, _ = outgoing.shape
    capacity = (rows - LABEL_ROWS) // voxels
    copies = fetch(
        sems, (morton_hbm, morton_pos), (features_hbm, features), (rim_hbm, rim),
        (cotangent_hbm, cotangent),
    )
    outgoing[...] = jnp.zeros(outgoing.shape, BF16)
    for p in range(peers):
        outgoing[p, capacity * voxels :, :] = jnp.full((LABEL_ROWS, channels), blocks, BF16)
    row = lax.broadcasted_iota(jnp.int32, (LABEL_ROWS, channels), 0)
    copies[0].wait()
    devs, places = places_of(morton_pos, blocks)
    copies[1].wait()
    for r in range(blocks):
        slot = morton_pos[r] - devs[r] * blocks
        place = places[r]
        outgoing[devs[r], pl.ds(pl.multiple_of(place * voxels, voxels), voxels), :] = features[r]
        held = outgoing[devs[r], capacity * voxels :, :].astype(F32)
        outgoing[devs[r], capacity * voxels :, :] = jnp.where(
            row == place, slot.astype(F32), held
        ).astype(BF16)
    copies[2].wait()
    copies[3].wait()
    for h in range(rim_rows.shape[0]):
        rim_rows[h] = cotangent[rim[h]]


def tiles_of(rows):
    return rows.astype(F32).reshape(-1, 8, rows.shape[-1])


def unpack_kernel(rim_hbm, arrived, morton, rim_rows, labels, rim, sems):
    blocks, voxels, channels = morton.shape
    copies = fetch(sems, (rim_hbm, rim))
    peers, rows, _ = arrived.shape
    capacity = (rows - LABEL_ROWS) // voxels
    held = [jnp.zeros((voxels // 8, 8, channels), F32) for _ in range(blocks)]
    for p in range(peers):
        for c in range(capacity):
            label = jnp.broadcast_to(
                arrived[p, capacity * voxels :, :].astype(F32)[c : c + 1], (8, channels)
            )
            labels[p * capacity + c] = label
            block = tiles_of(arrived[p, c * voxels : (c + 1) * voxels, :])
            for r in range(blocks):
                held[r] = jnp.where((label == r)[None], block, held[r])
    for r in range(blocks):
        morton[r] = held[r].reshape(voxels, channels).astype(BF16)
    copies[0].wait()
    for h in range(rim_rows.shape[0]):
        rim_rows[h] = morton[rim[h]]


def first_kernel(
    near_hbm, cotangent, weight, side_a, side_b, side_c, side_d,
    columns, hidden_grad, near, table, cells, sems,
):
    blocks = cotangent.shape[0]
    copies = fetch(sems, (near_hbm, near))
    fill_table(table, cotangent, (side_a, side_b, side_c, side_d))
    copies[0].wait()
    fill_cells(cells, table, near, blocks)
    fill_columns(columns, cells, blocks, True)
    hidden_grad[...] = flipped_dot(columns, weight)


def middle_kernel(
    near_hbm, rim_hbm, weight, morton, side_a, side_b, side_c, side_d,
    hidden_grad, hidden, pre_grad, rim_rows, columns, turned_hidden, turned_grad,
    near, rim, table, cells, hidden_va, pre_grad_va, sems,
):
    blocks, voxels, channels = morton.shape
    copies = fetch(sems, (near_hbm, near), (rim_hbm, rim))
    fill_table(table, morton, (side_a, side_b, side_c, side_d))
    copies[0].wait()
    fill_cells(cells, table, near, blocks)
    fill_columns(columns, cells, blocks, False)
    copies[1].wait()
    pre_one = jnp.dot(columns[...], weight[...], preferred_element_type=F32)
    gate = jax.nn.sigmoid(pre_one)
    hidden_flat = (pre_one * gate).astype(BF16)
    pre_grad_flat = (hidden_grad[...] * gate * (1.0 + pre_one * (1.0 - gate))).astype(BF16)
    hidden_va[...] = hidden_flat.astype(F32)
    pre_grad_va[...] = pre_grad_flat.astype(F32)
    for a in range(blocks):
        hidden[a] = hidden_va[pl.ds(a, voxels, stride=blocks), :].astype(BF16)
        pre_grad[a] = pre_grad_va[pl.ds(a, voxels, stride=blocks), :].astype(BF16)
    for h in range(rim_rows.shape[1]):
        rim_rows[0, h] = hidden[rim[h]]
        rim_rows[1, h] = pre_grad[rim[h]]
    turned_grad[...] = pre_grad_flat.T
    turned_hidden[...] = hidden_flat.T


def weight_sums_kernel(start, turned_hidden, turned_grad, grad_columns, columns, keep, send):
    channels = turned_grad.shape[0]
    low = jnp.full((channels, channels), parity("tile"), jnp.int32) == 0
    stop = min(start + keep.shape[0], OFFSETS)
    for offset in range(start, stop, 2):
        count = min(2, stop - offset)
        part = slice(offset * channels, (offset + count) * channels)
        two = jnp.dot(turned_hidden[...], grad_columns[:, part], preferred_element_type=F32)
        one = jnp.dot(turned_grad[...], columns[:, part], preferred_element_type=F32)
        for u in range(count):
            part = slice(u * channels, (u + 1) * channels)
            at = offset + u - start
            keep[at] = jnp.where(low, two[:, part], one[:, part].T)
            send[at] = jnp.where(low, one[:, part].T, two[:, part])
    for at in range(stop - start, keep.shape[0]):
        keep[at] = jnp.zeros(keep.shape[1:], F32)
        send[at] = jnp.zeros(send.shape[1:], F32)


def back_kernel(
    near_hbm, cotangent, weight, pre_grad, side_a, side_b, side_c, side_d, labels,
    returning, near, table, cells, columns, result, sems,
):
    blocks, voxels, channels = cotangent.shape
    peers, rows, _ = returning.shape
    capacity = rows // voxels
    copies = fetch(sems, (near_hbm, near))
    fill_table(table, pre_grad, (side_a, side_b, side_c, side_d), 1)
    copies[0].wait()
    fill_cells(cells, table, near, blocks)
    fill_columns(columns, cells, blocks, True)
    result[...] = flipped_dot(columns, weight)
    natural = [
        tiles_of(result[pl.ds(a, voxels, stride=blocks), :] + cotangent[a].astype(F32))
        for a in range(blocks)
    ]
    for p in range(peers):
        for c in range(capacity):
            label = labels[p * capacity + c]
            block = natural[0]
            for r in range(1, blocks):
                block = jnp.where((label == r)[None], natural[r], block)
            returning[p, c * voxels : (c + 1) * voxels, :] = block.reshape(
                voxels, channels
            ).astype(BF16)


def output_kernel(
    capacity, near_hbm, morton_hbm, weight, hidden, morton, side_a, side_b, side_c, side_d,
    output, flat_tiles, near, morton_pos, table, cells, columns, result, sems,
):
    blocks, voxels, channels = morton.shape
    copies = fetch(sems, (near_hbm, near), (morton_hbm, morton_pos))
    fill_table(table, hidden, (side_a, side_b, side_c, side_d), 0)
    copies[0].wait()
    fill_cells(cells, table, near, blocks)
    fill_columns(columns, cells, blocks, False)
    result[...] = jnp.dot(columns[...], weight[...], preferred_element_type=F32)
    for a in range(blocks):
        output[a] = (
            morton[a].astype(F32) + result[pl.ds(a, voxels, stride=blocks), :]
        ).astype(BF16)
    copies[1].wait()
    devs, places = places_of(morton_pos, blocks)
    for r in range(blocks):
        flat_tiles[r] = jnp.full(
            flat_tiles.shape[1:], (devs[r] * capacity + places[r]).astype(F32), F32
        )


def restore_kernel(coming_back, flat_tiles, input_grad):
    blocks, voxels, channels = input_grad.shape
    slots = coming_back.shape[0]
    held = [jnp.zeros((voxels // 8, 8, channels), F32) for _ in range(blocks)]
    for s in range(slots):
        block = tiles_of(coming_back[s])
        for r in range(blocks):
            held[r] = jnp.where((flat_tiles[r] == s)[None], block, held[r])
    for r in range(blocks):
        input_grad[r] = held[r].reshape(voxels, channels).astype(BF16)


def order_bits(group):
    x, y = parity("tile", 1), parity("dev")
    turned = (parity("tile") + group) & 1
    return jnp.where(turned == 0, x, y), jnp.where(turned == 0, y, x)


def step_bit(step, group):
    return order_bits(group)[step] if step < 2 else parity("dev", 1)


def half(rows, index):
    return pl.ds(pl.multiple_of(index * rows, rows), rows)


def split_kernel(step, group, mine, other, keep, send):
    rows = keep.shape[1]
    bit = step_bit(step, group)
    for ref, index in ((keep, bit), (send, 1 - bit)):
        at = half(rows, index)
        ref[...] = (mine[:, at, :] + other[:, at, :].astype(F32)).astype(ref.dtype)


def add_kernel(left, right, total):
    total[...] = (left[...].astype(F32) + right[...].astype(F32)).astype(total.dtype)


def join_kernel(step, group, mine, other, joined):
    rows = mine.shape[1]
    bit = step_bit(step, group)
    joined[:, half(rows, bit), :] = mine[...]
    joined[:, half(rows, 1 - bit), :] = other[...]


def write_gradient(scale, parts, grad_hbm, grad, sems):
    channels = grad.shape[1]
    copies = []
    for n, ref in enumerate(parts):
        start = n * ref.shape[0]
        count = min(ref.shape[0], OFFSETS - start)
        for u in range(count):
            grad[pl.ds((start + u) * channels, channels), :] = ref[u].astype(F32) * scale
        part = pl.ds(start * channels, count * channels)
        copies.append((grad.at[part], grad_hbm.at[part], sems.at[n]))
    for copy in copies:
        pltpu.make_async_copy(*copy).start()
    for copy in copies:
        pltpu.make_async_copy(*copy).wait()


def finish_kernel(scale, owner, *refs):
    *parts, one_hbm, two_hbm, grad, sems = refs

    @pl.when(parity("tile") == owner)
    def _():
        write_gradient(scale, parts[-2:], two_hbm, grad, sems)

    @pl.when(parity("tile") != owner)
    def _():
        write_gradient(scale, parts[-2:], one_hbm, grad, sems)


HBM = pl.BlockSpec(memory_space=pltpu.HBM)
ANY = pl.BlockSpec(memory_space=pl.ANY)
VMEM = pl.BlockSpec(memory_space=pltpu.VMEM)


def call(kernel, far, arrays, outs, scratch=(), far_outs=(), flops=0, name=None, after=(), aliases={}):
    shapes = [jax.ShapeDtypeStruct(shape, dtype) for shape, dtype in [*outs, *far_outs]]
    moved = sum(x.size * x.dtype.itemsize for x in [*far, *arrays])
    moved += sum(math.prod(s.shape) * s.dtype.itemsize for s in shapes)
    held = []
    for item in scratch:
        if isinstance(item, int):
            held.append(pltpu.SemaphoreType.DMA((item,)))
        else:
            held.append((pltpu.SMEM if item[1] == jnp.int32 else pltpu.VMEM)(*item))
    body = kernel
    if after:

        def body(*refs):
            kernel(*refs[len(after) :])

    return pl.pallas_call(
        body,
        out_shape=shapes,
        in_specs=[ANY] * len(after) + [HBM] * len(far) + [VMEM] * len(arrays),
        out_specs=[VMEM] * len(outs) + [HBM] * len(far_outs),
        scratch_shapes=held,
        input_output_aliases=aliases,
        compiler_params=pltpu.CompilerParams(vmem_limit_bytes=(63 if name == "pack" else 24) * 2**20),
        cost_estimate=pl.CostEstimate(flops=flops, bytes_accessed=moved, transcendentals=0),
        name=name,
    )(*after, *far, *arrays)


def halo(rows):
    sides = []
    for axis in ("tile", "dev"):
        count = lax.axis_size(axis)
        even = [(i, i ^ 1) for i in range(count)]
        odd = []
        for i in range(1, count - 1, 2):
            odd += [(i, i + 1), (i + 1, i)]
        sides += [lax.ppermute(rows, axis, even), lax.ppermute(rows, axis, odd)]
    return sides


def swap(rows, partner):
    tiles, devs = lax.axis_size("tile"), lax.axis_size("dev")
    pairs = []
    for t in range(tiles):
        for d in range(devs):
            other = partner(t, d)
            pairs.append((t * devs + d, other[0] * devs + other[1]))
    return lax.ppermute(rows, ("tile", "dev"), pairs)


def other_core(t, d):
    return t ^ 1, d


def partner_at(step, group):
    def partner(t, d):
        if step == 2:
            return t, d ^ 2
        along_x = ((t + group) & 1) == step
        return (t ^ 2, d) if along_x else (t, d ^ 1)

    return partner


def split_stage(step, group, mine, other, wire, after=()):
    count, rows, channels = mine.shape
    part = (count, rows // 2, channels)
    return call(
        functools.partial(split_kernel, step, group), [], [mine, other],
        [(part, F32), (part, wire)], name="split", after=after,
    )


def pair_stage(keep, send, wire, after=()):
    (mine,) = call(
        add_kernel, [], [keep, swap(send, partner_at(2, 0))], [(keep.shape, wire)],
        name="pair_sum", after=after,
    )
    return mine


def far_steps():
    rest = [(0, 1 << bit) for bit in range(2, lax.axis_size("dev").bit_length() - 1)]
    rest += [(1 << bit, 0) for bit in range(2, lax.axis_size("tile").bit_length() - 1)]
    return rest


def far_stage(mine, after=()):
    rest = far_steps()
    for step, bits in enumerate(rest):
        kind = BF16 if step == len(rest) - 1 else mine.dtype
        other = swap(mine, lambda t, d, bits=bits: (t ^ bits[0], d ^ bits[1]))
        (mine,) = call(
            add_kernel, [], [mine, other], [(mine.shape, kind)], name="far_sum", after=after
        )
        after = ()
    return mine


def join_stage(step, group, mine, after=()):
    count, rows, channels = mine.shape
    (mine,) = call(
        functools.partial(join_kernel, step, group), [], [mine, swap(mine, partner_at(step, group))],
        [((count, 2 * rows, channels), BF16)], name="join", after=after,
    )
    return mine


def finish(scale, owner, parts, held=(), after=()):
    channels = parts[0].shape[2]
    whole = ((OFFSETS * channels, channels), F32)
    first = len(after)
    return call(
        functools.partial(finish_kernel, scale, owner), held, parts, [], [whole, 2],
        [whole, whole], name="finish", after=after,
        aliases={first: 0, first + 1: 1} if held else {},
    )


def per_device(features, morton_pos, neighbours, rim, cotangent, weight_one, weight_two):
    blocks, voxels, channels = features.shape
    rims = rim.shape[0]
    peers = lax.axis_size("dev")
    tiles = lax.axis_size("tile")
    capacity = 2 * ((blocks + peers - 1) // peers)
    block = ((blocks, voxels, channels), BF16)
    rows = blocks * voxels
    depth = OFFSETS * channels
    near = ((blocks, OFFSETS), jnp.int32)
    table = ((blocks + 4 * rims + 1, voxels, channels), F32)
    cells = ((CELLS * blocks, channels), F32)
    columns = ((rows, depth), BF16)
    flat = ((rows, channels), F32)
    rim_shape = (rims, voxels, channels)
    macs = rows * depth * channels

    outgoing, cot_rim = call(
        pack_kernel, [morton_pos, rim, features, cotangent], [],
        [((peers, capacity * voxels + LABEL_ROWS, channels), BF16), (rim_shape, BF16)],
        [((blocks,), jnp.int32), ((rims,), jnp.int32), block, block, 4], flops=WAIT, name="pack",
    )
    arrived = lax.all_to_all(outgoing, "dev", split_axis=0, concat_axis=0, tiled=True)
    cot_sides = halo(cot_rim)
    grad_columns, hidden_grad = call(
        first_kernel, [neighbours], [cotangent, weight_two, *cot_sides], [columns, flat],
        [near, table, cells, 1], flops=2 * macs, name="hidden_grad",
    )
    morton, morton_rim, labels = call(
        unpack_kernel, [rim], [arrived],
        [block, (rim_shape, BF16), ((peers * capacity, 8, channels), F32)],
        [((rims,), jnp.int32), 1], flops=4 * WAIT, name="unpack",
    )
    sides = halo(morton_rim)
    hidden, pre_grad, rim_rows, morton_columns, turned_hidden, turned_grad = call(
        middle_kernel, [neighbours, rim], [weight_one, morton, *sides, hidden_grad],
        [block, block, ((2,) + rim_shape, BF16), columns, ((channels, rows), BF16),
         ((channels, rows), BF16)],
        [near, ((rims,), jnp.int32), table, cells, flat, flat, 2],
        flops=2 * macs, name="middle",
    )
    count = (OFFSETS + 1) // 2
    groups = range(2)
    wire = BF16 if len(far_steps()) == 1 else F32
    parts = [
        call(
            functools.partial(weight_sums_kernel, group * count), [],
            [turned_hidden, turned_grad, grad_columns, morton_columns],
            [((count, channels, channels), F32)] * 2, flops=2 * macs, name="weight_sums",
        )
        for group in groups
    ]
    scale = 1.0 / math.sqrt(blocks * voxels * tiles * peers)
    sides = halo(rim_rows)
    parts = [
        split_stage(0, g, parts[g][0], swap(parts[g][1], other_core), BF16)
        for g in groups
    ]
    parts = [
        split_stage(1, g, parts[g][0], swap(parts[g][1], partner_at(0, g)), BF16)
        for g in groups
    ]
    output, flat_tiles = call(
        functools.partial(output_kernel, capacity), [neighbours, morton_pos],
        [weight_two, hidden, morton, *sides], [block, ((blocks, 8, channels), F32)],
        [near, ((blocks,), jnp.int32), table, cells, columns, flat, 2], flops=2 * macs,
        name="output",
    )
    (returning,) = call(
        back_kernel, [neighbours], [cotangent, weight_one, pre_grad, *sides, labels],
        [((peers, capacity * voxels, channels), BF16)],
        [near, table, cells, columns, flat, 1], flops=2 * macs, name="back",
    )
    parts = [
        split_stage(2, g, parts[g][0], swap(parts[g][1], partner_at(1, g)), F32, after=sides if g == 1 else ())
        for g in groups
    ]
    parts = [pair_stage(*parts[g], wire, after=[returning] if g == 1 else ()) for g in groups]
    parts = [far_stage(parts[g]) for g in groups]
    coming_back = lax.all_to_all(returning, "dev", split_axis=0, concat_axis=0, tiled=True)
    parts = [join_stage(2, g, parts[g], after=[flat_tiles] if g == 1 else ()) for g in groups]
    parts = [join_stage(1, g, parts[g]) for g in groups]
    (input_grad,) = call(
        restore_kernel, [], [coming_back.reshape(peers * capacity, voxels, channels), flat_tiles],
        [block], name="restore",
    )
    parts = [join_stage(0, g, parts[g], after=[coming_back] if g == 1 else ()) for g in groups]
    others = [swap(parts[g], other_core) for g in groups]
    grads = finish(scale, 0, parts)
    grad_one, grad_two = finish(scale, 1, others, grads)
    return (output, input_grad, grad_one, grad_two)


def solution(mesh):
    placed = (
        P(("tile", "dev"), None, None),
        P(("tile", "dev")),
        P(("tile", "dev"), None),
        P(("tile", "dev")),
        P(("tile", "dev"), None, None),
        P(),
        P(),
    )
    return jax.shard_map(
        per_device,
        mesh=mesh,
        in_specs=placed,
        out_specs=(P(("tile", "dev"), None, None), P(("tile", "dev"), None, None), P(), P()),
        check_vma=False,
    )
```

time: 98.4 us -> 90.7 us (0.922)
  starting transfers between devices: 53 us -> 47.1 us
  waiting for transfers between devices: 21.7 us -> 24.1 us
  Pallas kernels: 20.1 us -> 17.9 us
  local copies, waits for them, and re-layouts: 1.91 us -> 0.03 us
    ppermute x12, starting transfers between devices: 24.3 us -> 8.99 us  [halo(): sides += [lax.ppermute(rows, axis, even), lax.ppermute(rows, axis, odd)]]
    ppermute x22 -> x18, starting transfers between devices: 18 us -> 27.1 us  [swap(): return lax.ppermute(rows, ('tile', 'dev'), pairs)]
    all_to_all x1, waiting for transfers between devices: 1.29 us -> 5.97 us  [per_device(): lax.all_to_all(outgoing, 'dev', split_axis=0, concat_axis=0, tiled=True)]
    all_to_all x1, waiting for transfers between devices: 3.04 us -> 0.01 us  [per_device(): lax.all_to_all(returning, 'dev', split_axis=0, concat_axis=0, tiled=True)]
    pallas_call x21 -> x27, Pallas kernels: 20.1 us -> 17.9 us  [call(): pl.pallas_call(body, out_shape=shapes, in_specs=[ANY] * len(after) + [HBM...]
    unnamed x16 -> x12, local copies, waits for them, and re-layouts: 1.91 us -> 0.03 us
    ppermute x12, waiting for transfers between devices: 0.03 us -> 1.53 us  [halo(): sides += [lax.ppermute(rows, axis, even), lax.ppermute(rows, axis, odd)]]
    ppermute x22 -> x18, waiting for transfers between devices: 17.4 us -> 16.6 us  [swap(): return lax.ppermute(rows, ('tile', 'dev'), pairs)]
  transfers between devices with their start and end apart: 36 -> 32, of which waited for: 11 -> 12; matrix products, arithmetic and copies ran while one was open for 0% -> 0% of each run, Pallas kernels for 12% -> 13%
where the time goes in v2:
time: 90.7 us; the launch traced here: 90.2 us
  starting transfers between devices  47.1 us (52%)
  waiting for transfers between devices  24.1 us (27%)
  Pallas kernels  17.9 us (20%)
  between operations  1.02 us (1%)
    ppermute x18, starting transfers between devices, swap(): return lax.ppermute(rows, ('tile', 'dev'), pairs)  27.1 us
    pallas_call x27, Pallas kernels, call(): pl.pallas_call(body, out_shape=shapes, in_specs=[ANY] * len(after) + [HBM...  17.9 us
    ppermute x18, waiting for transfers between devices, swap(): return lax.ppermute(rows, ('tile', 'dev'), pairs)  16.6 us
    ppermute x12, starting transfers between devices, halo(): sides += [lax.ppermute(rows, axis, even), lax.ppermute(rows, axis, odd)]  8.99 us
    all_to_all x1, starting transfers between devices, per_device(): lax.all_to_all(outgoing, 'dev', split_axis=0, concat_axis=0, tiled=True)  7.29 us
    all_to_all x1, waiting for transfers between devices, per_device(): lax.all_to_all(outgoing, 'dev', split_axis=0, concat_axis=0, tiled=True)  5.97 us
    all_to_all x1, starting transfers between devices, per_device(): lax.all_to_all(returning, 'dev', split_axis=0, concat_axis=0, tiled=True)  3.81 us
  transfers between devices with their start and end apart: 32, of which 12 were waited for; matrix products, arithmetic and copies ran while one was open for 0% of the time, Pallas kernels for 13%

profile of v2, /device:TPU:0, one launch (start us, length us, event | category | flops | bytes accessed | tf_op | source)
XLA Modules:
  0.0 90.2 jit_solution(5705264699210021764)
XLA Ops:
  0.6 1.7 %pack.1 = (bf16[8,144,128]{2,1,0:T(8,128)(2,1)}, bf16[4,64,128]{2,1,0:T(8,128)(2,1)}) custom-call(s32[8]{0:T(128)} %morton_hbm.3, s32[4]{0:T(128)} %rim_hbm.5, bf16[8,64,128]{2,1,0:T(8,128)(2,1)} %features_hbm.1, bf16[8,64,128]{2,1,0:T(8,128)(2,1)} %cotangent.3), custom_call_target="tpu_custom_call" | custom-call | flops 1500000000 | bytes 622640 | tf_op jit(solution)/shard_map/pack/pallas_call | solution.py:418
  2.4 7.3 %all-to-all-start = ((bf16[8,144,128]{2,1,0:T(8,128)(2,1)}), bf16[8,144,128]{2,1,0:T(8,128)(2,1)S(1)}, u32[]{:S(2)}, u32[]{:S(2)}) async-start(bf16[8,144,128]{2,1,0:T(8,128)(2,1)} %get-tuple-element.39), calls=%async_computation | async-start | bytes 589824 | tf_op jit(solution)/shard_map/all_to_all | solution.py:544
  10.6 2.1 %collective-permute-start.6 = (bf16[4,64,128]{2,1,0:T(8,128)(2,1)}, bf16[4,64,128]{2,1,0:T(8,128)(2,1)S(1)}, u32[]{:S(2)}, u32[]{:S(2)}) collective-permute-start(bf16[4,64,128]{2,1,0:T(8,128)(2,1)} %get-tuple-element.42), channel_id=1, source_target_pairs={{0,1},{1,0},{2,3},{3,2},{4,5},{5,4},{6,7},{7,6},{8,9},{9,8},{10,11... | collective-permute-start | bytes 196616 | tf_op jit(solution)/shard_map/ppermute | solution.py:439
  13.3 6.0 %all-to-all-done.arrived = bf16[8,144,128]{2,1,0:T(8,128)(2,1)S(1)} async-done(((bf16[8,144,128]{2,1,0:T(8,128)(2,1)}), bf16[8,144,128]{2,1,0:T(8,128)(2,1)S(1)}, u32[]{:S(2)}, u32[]{:S(2)}) %all-to-all-start) | async-done | bytes 294944 | tf_op jit(solution)/shard_map/all_to_all | solution.py:544
  20.6 1.5 %collective-permute-start.2 = (bf16[4,64,128]{2,1,0:T(8,128)(2,1)S(1)}, bf16[4,64,128]{2,1,0:T(8,128)(2,1)S(1)}, u32[]{:S(2)}, u32[]{:S(2)}) collective-permute-start(bf16[4,64,128]{2,1,0:T(8,128)(2,1)S(1)} %get-tuple-element.41), channel_id=1, source_target_pairs={{0,1},{1,0},{2,3},{3,2},{4,5},{5,4},{6,7},{7,6},{8,9},{9,8},{10,11... | collective-permute-start | bytes 196616 | tf_op jit(solution)/shard_map/ppermute | solution.py:439
  22.8 2.0 %hidden_grad.1 = (bf16[512,3456]{1,0:T(8,128)(2,1)S(1)}, f32[512,128]{1,0:T(8,128)S(1)}) custom-call(s32[8,27]{1,0:T(8,128)S(1)} %copy-done.2, bf16[8,64,128]{2,1,0:T(8,128)(2,1)S(1)} %copy-done.1, bf16[3456,128]{1,0:T(8,128)(2,1)S(1)} %copy-done.3, bf16[4,64,128]{2,1,0:T(8,128)(2,1)S(1)} %collective-permute-done.4.side_a, ...), custom_call_target="tpu_custom_call" | custom-call | flops 452984832 | bytes 5079904 | tf_op jit(solution)/shard_map/hidden_grad/pallas_call | solution.py:418
  25.0 2.6 %middle.1 = (bf16[8,64,128]{2,1,0:T(8,128)(2,1)S(1)}, bf16[8,64,128]{2,1,0:T(8,128)(2,1)S(1)}, bf16[2,4,64,128]{3,2,1,0:T(8,128)(2,1)S(1)}, bf16[512,3456]{1,0:T...) custom-call(s32[8,27]{1,0:T(8,128)S(1)} %copy-done.2, s32[4]{0:T(128)S(1)} %copy-done.4, ...), custom_call_target="tpu_custom_call" | custom-call | flops 452984832 | bytes 5735280 | tf_op jit(solution)/shard_map/middle/pallas_call | solution.py:418
  28.3 2.5 %collective-permute-start.20 = (f32[14,128,128]{2,1,0:T(8,128)S(1)}, f32[14,128,128]{2,1,0:T(8,128)S(1)}, u32[]{:S(2)}, u32[]{:S(2)}) collective-permute-start(f32[14,128,128]{2,1,0:T(8,128)S(1)} %get-tuple-element.63), channel_id=1, source_target_pairs={{0,8},{1,9},{2,10},{3,11},{4,12},{5,13},{6,14},{7,15},{8,0},{9,1},... | collective-permute-start | bytes 2752520 | tf_op jit(solution)/shard_map/ppermute | solution.py:450
  33.0 4.5 %collective-permute-start.21 = (bf16[14,64,128]{2,1,0:T(8,128)(2,1)S(1)}, bf16[14,64,128]{2,1,0:T(8,128)(2,1)S(1)}, u32[]{:S(2)}, u32[]{:S(2)}) collective-permute-start(bf16[14,64,128]{2,1,0:T(8,128)(2,1)S(1)} %get-tuple-element.65), channel_id=1, source_target_pairs={{0,1},{1,0},{2,3},{3,2},{4,5},{5,4},{6,7},{7,6},{8,24},{9,25},{10,... | collective-permute-start | bytes 688136 | tf_op jit(solution)/shard_map/ppermute | solution.py:450
  37.6 1.8 %collective-permute-start.13 = (bf16[14,64,128]{2,1,0:T(8,128)(2,1)S(1)}, bf16[14,64,128]{2,1,0:T(8,128)(2,1)S(1)}, u32[]{:S(2)}, u32[]{:S(2)}) collective-permute-start(bf16[14,64,128]{2,1,0:T(8,128)(2,1)S(1)} %get-tuple-element.57), channel_id=1, source_target_pairs={{0,16},{1,17},{2,18},{3,19},{4,20},{5,21},{6,22},{7,23},{8,9},{9,8... | collective-permute-start | bytes 688136 | tf_op jit(solution)/shard_map/ppermute | solution.py:450
  41.3 1.7 %collective-permute-done.21.other = bf16[14,64,128]{2,1,0:T(8,128)(2,1)S(1)} collective-permute-done((bf16[14,64,128]{2,1,0:T(8,128)(2,1)S(1)}, bf16[14,64,128]{2,1,0:T(8,128)(2,1)S(1)}, u32[]{:S(2)}, u32[]{:S(2)}) %collective-permute-start.21) | collective-permute-done | bytes 229408 | tf_op jit(solution)/shard_map/ppermute | solution.py:450
  43.7 3.3 %collective-permute-start.22 = (bf16[14,32,128]{2,1,0:T(8,128)(2,1)S(1)}, bf16[14,32,128]{2,1,0:T(8,128)(2,1)S(1)}, u32[]{:S(2)}, u32[]{:S(2)}) collective-permute-start(bf16[14,32,128]{2,1,0:T(8,128)(2,1)S(1)} %get-tuple-element.67), channel_id=1, source_target_pairs={{0,16},{1,17},{2,18},{3,19},{4,20},{5,21},{6,22},{7,23},{8,9},{9,8... | collective-permute-start | bytes 344072 | tf_op jit(solution)/shard_map/ppermute | solution.py:450
  48.4 2.5 %collective-permute-start.14 = (bf16[14,32,128]{2,1,0:T(8,128)(2,1)S(1)}, bf16[14,32,128]{2,1,0:T(8,128)(2,1)S(1)}, u32[]{:S(2)}, u32[]{:S(2)}) collective-permute-start(bf16[14,32,128]{2,1,0:T(8,128)(2,1)S(1)} %get-tuple-element.59), channel_id=1, source_target_pairs={{0,1},{1,0},{2,3},{3,2},{4,5},{5,4},{6,7},{7,6},{8,24},{9,25},{10,... | collective-permute-start | bytes 344072 | tf_op jit(solution)/shard_map/ppermute | solution.py:450
  51.0 2.1 %collective-permute-start.23 = (f32[14,16,128]{2,1,0:T(8,128)S(1)}, f32[14,16,128]{2,1,0:T(8,128)S(1)}, u32[]{:S(2)}, u32[]{:S(2)}) collective-permute-start(f32[14,16,128]{2,1,0:T(8,128)S(1)} %get-tuple-element.69), channel_id=1, source_target_pairs={{0,2},{1,3},{2,0},{3,1},{4,6},{5,7},{6,4},{7,5},{8,10},{9,11},{10,... | collective-permute-start | bytes 344072 | tf_op jit(solution)/shard_map/ppermute | solution.py:450
  54.9 2.9 %back.1.refs_0_ = bf16[8,128,128]{2,1,0:T(8,128)(2,1)} custom-call(s32[8,27]{1,0:T(8,128)S(1)} %copy-done.2, bf16[8,64,128]{2,1,0:T(8,128)(2,1)S(1)} %copy-done.1, bf16[3456,128]{1,0:T(8,128)(2,1)S(1)} %copy-done, bf16[8,64,128]{2,1,0:T(8,128)(2,1)S(1)} %get-tuple-element.47.pre_grad, bf16[2,4,64,128]{3,2,1,0:T(8,128)(2,1)S(1)} %collective-permute-done.8.side_a.refs_0_, ...), custom_call_target="tpu_custom_call" | custom-call | flops 452984832 | bytes 1999712 | tf_op jit(solution)/shard_map/back/pallas_call | solution.py:418
  57.8 1.7 %collective-permute-start.24 = (bf16[14,16,128]{2,1,0:T(8,128)(2,1)S(1)}, bf16[14,16,128]{2,1,0:T(8,128)(2,1)S(1)}, u32[]{:S(2)}, u32[]{:S(2)}) collective-permute-start(bf16[14,16,128]{2,1,0:T(8,128)(2,1)S(1)} %pair_sum.3.left), channel_id=1, source_target_pairs={{0,4},{1,5},{2,6},{3,7},{4,0},{5,1},{6,2},{7,3},{8,12},{9,13},{10,... | collective-permute-start | bytes 172040 | tf_op jit(solution)/shard_map/ppermute | solution.py:450
  59.5 1.9 %collective-permute-start.16 = (bf16[14,16,128]{2,1,0:T(8,128)(2,1)S(1)}, bf16[14,16,128]{2,1,0:T(8,128)(2,1)S(1)}, u32[]{:S(2)}, u32[]{:S(2)}) collective-permute-start(bf16[14,16,128]{2,1,0:T(8,128)(2,1)S(1)} %pair_sum.2.left), channel_id=1, source_target_pairs={{0,4},{1,5},{2,6},{3,7},{4,0},{5,1},{6,2},{7,3},{8,12},{9,13},{10,... | collective-permute-start | bytes 172040 | tf_op jit(solution)/shard_map/ppermute | solution.py:450
  61.4 3.8 %all-to-all-start.1 = ((bf16[8,128,128]{2,1,0:T(8,128)(2,1)}), bf16[8,128,128]{2,1,0:T(8,128)(2,1)S(1)}, u32[]{:S(2)}, u32[]{:S(2)}) async-start(bf16[8,128,128]{2,1,0:T(8,128)(2,1)} %back.1.refs_0_), calls=%async_computation.1 | async-start | bytes 524288 | tf_op jit(solution)/shard_map/all_to_all | solution.py:601
  65.2 2.1 %collective-permute-start.25 = (bf16[14,16,128]{2,1,0:T(8,128)(2,1)S(1)}, bf16[14,16,128]{2,1,0:T(8,128)(2,1)S(1)}, u32[]{:S(2)}, u32[]{:S(2)}) collective-permute-start(bf16[14,16,128]{2,1,0:T(8,128)(2,1)S(1)} %far_sum.3.refs_1_), channel_id=1, source_target_pairs={{0,2},{1,3},{2,0},{3,1},{4,6},{5,7},{6,4},{7,5},{8,10},{9,11},{10,... | collective-permute-start | bytes 172040 | tf_op jit(solution)/shard_map/ppermute | solution.py:450
  67.4 2.6 %output.1 = (bf16[8,64,128]{2,1,0:T(8,128)(2,1)}, f32[8,8,128]{2,1,0:T(8,128)S(1)}) custom-call(s32[8,27]{1,0:T(8,128)S(1)} %copy-done.2, s32[8]{0:T(128)S(1)} %copy-done.5, bf16[3456,128]{1,0:T(8,128)(2,1)S(1)} %copy-done.3, bf16[8,64,128]{2,1,0:T(8,128)(2,1)S(1)} %get-tuple-element.44.hidden, bf16[8,64,128]{2,1,0:T(8,128)(2,1)S(1)} %get-tuple-element.40.morton, ...), custom_call_target="tpu_custom_call" | custom-call | flops 452984832 | bytes 1835904 | tf_op jit(solution)/shard_map/output/pallas_call | solution.py:418
  70.0 2.9 %collective-permute-done.25.refs_2_ = bf16[14,16,128]{2,1,0:T(8,128)(2,1)S(1)} collective-permute-done((bf16[14,16,128]{2,1,0:T(8,128)(2,1)S(1)}, bf16[14,16,128]{2,1,0:T(8,128)(2,1)S(1)}, u32[]{:S(2)}, u32[]{:S(2)}) %collective-permute-start.25) | collective-permute-done | bytes 57376 | tf_op jit(solution)/shard_map/ppermute | solution.py:450
  72.9 1.4 %collective-permute-start.26 = (bf16[14,32,128]{2,1,0:T(8,128)(2,1)S(1)}, bf16[14,32,128]{2,1,0:T(8,128)(2,1)S(1)}, u32[]{:S(2)}, u32[]{:S(2)}) collective-permute-start(bf16[14,32,128]{2,1,0:T(8,128)(2,1)S(1)} %join.9.mine), channel_id=1, source_target_pairs={{0,16},{1,17},{2,18},{3,19},{4,20},{5,21},{6,22},{7,23},{8,9},{9,8... | collective-permute-start | bytes 344072 | tf_op jit(solution)/shard_map/ppermute | solution.py:450
  75.1 3.9 %collective-permute-done.26.other = bf16[14,32,128]{2,1,0:T(8,128)(2,1)S(1)} collective-permute-done((bf16[14,32,128]{2,1,0:T(8,128)(2,1)S(1)}, bf16[14,32,128]{2,1,0:T(8,128)(2,1)S(1)}, u32[]{:S(2)}, u32[]{:S(2)}) %collective-permute-start.26) | collective-permute-done | bytes 114720 | tf_op jit(solution)/shard_map/ppermute | solution.py:450
  81.3 3.8 %collective-permute-done.27.refs_2_ = bf16[14,64,128]{2,1,0:T(8,128)(2,1)S(1)} collective-permute-done((bf16[14,64,128]{2,1,0:T(8,128)(2,1)S(1)}, bf16[14,64,128]{2,1,0:T(8,128)(2,1)S(1)}, u32[]{:S(2)}, u32[]{:S(2)}) %collective-permute-start.27) | collective-permute-done | bytes 229408 | tf_op jit(solution)/shard_map/ppermute | solution.py:450
  (79 shorter events, 20.8 us)
Async XLA Ops:
  2.4 16.9 %all-to-all-start = ((bf16[8,144,128]{2,1,0:T(8,128)(2,1)}), bf16[8,144,128]{2,1,0:T(8,128)(2,1)S(1)}, u32[]{:S(2)}, u32[]{:S(2)}) async-start(bf16[8,144,128]{2,1,0:T(8,128)(2,1)} %get-tuple-element.39), calls=%async_computation | async-start | bytes 589824 | tf_op jit(solution)/shard_map/all_to_all | solution.py:544
  9.7 10.2 %collective-permute-start.4 = (bf16[4,64,128]{2,1,0:T(8,128)(2,1)}, bf16[4,64,128]{2,1,0:T(8,128)(2,1)S(1)}, u32[]{:S(2)}, u32[]{:S(2)}) collective-permute-start(bf16[4,64,128]{2,1,0:T(8,128)(2,1)} %get-tuple-element.42), channel_id=1, source_target_pairs={{0,8},{8,0},{16,24},{24,16},{1,9},{9,1},{17,25},{25,17},{2,10},{10... | collective-permute-start | bytes 196616 | tf_op jit(solution)/shard_map/ppermute | solution.py:439
  9.8 10.8 %collective-permute-start.5 = (bf16[4,64,128]{2,1,0:T(8,128)(2,1)}, bf16[4,64,128]{2,1,0:T(8,128)(2,1)S(1)}, u32[]{:S(2)}, u32[]{:S(2)}) collective-permute-start(bf16[4,64,128]{2,1,0:T(8,128)(2,1)} %get-tuple-element.42), channel_id=1, source_target_pairs={{8,16},{16,8},{9,17},{17,9},{10,18},{18,10},{11,19},{19,11},{12,20... | collective-permute-start | bytes 196616 | tf_op jit(solution)/shard_map/ppermute | solution.py:439
  10.6 11.5 %collective-permute-start.6 = (bf16[4,64,128]{2,1,0:T(8,128)(2,1)}, bf16[4,64,128]{2,1,0:T(8,128)(2,1)S(1)}, u32[]{:S(2)}, u32[]{:S(2)}) collective-permute-start(bf16[4,64,128]{2,1,0:T(8,128)(2,1)} %get-tuple-element.42), channel_id=1, source_target_pairs={{0,1},{1,0},{2,3},{3,2},{4,5},{5,4},{6,7},{7,6},{8,9},{9,8},{10,11... | collective-permute-start | bytes 196616 | tf_op jit(solution)/shard_map/ppermute | solution.py:439
  12.7 10.1 %collective-permute-start.7 = (bf16[4,64,128]{2,1,0:T(8,128)(2,1)}, bf16[4,64,128]{2,1,0:T(8,128)(2,1)S(1)}, u32[]{:S(2)}, u32[]{:S(2)}) collective-permute-start(bf16[4,64,128]{2,1,0:T(8,128)(2,1)} %get-tuple-element.42), channel_id=1, source_target_pairs={{1,2},{2,1},{3,4},{4,3},{5,6},{6,5},{9,10},{10,9},{11,12},{12,11},... | collective-permute-start | bytes 196616 | tf_op jit(solution)/shard_map/ppermute | solution.py:439
  31.5 6.0 %collective-permute-start.12 = (f32[14,128,128]{2,1,0:T(8,128)S(1)}, f32[14,128,128]{2,1,0:T(8,128)S(1)}, u32[]{:S(2)}, u32[]{:S(2)}) collective-permute-start(f32[14,128,128]{2,1,0:T(8,128)S(1)} %get-tuple-element.55), channel_id=1, source_target_pairs={{0,8},{1,9},{2,10},{3,11},{4,12},{5,13},{6,14},{7,15},{8,0},{9,1},... | collective-permute-start | bytes 2752520 | tf_op jit(solution)/shard_map/ppermute | solution.py:450
  33.0 9.9 %collective-permute-start.21 = (bf16[14,64,128]{2,1,0:T(8,128)(2,1)S(1)}, bf16[14,64,128]{2,1,0:T(8,128)(2,1)S(1)}, u32[]{:S(2)}, u32[]{:S(2)}) collective-permute-start(bf16[14,64,128]{2,1,0:T(8,128)(2,1)S(1)} %get-tuple-element.65), channel_id=1, source_target_pairs={{0,1},{1,0},{2,3},{3,2},{4,5},{5,4},{6,7},{7,6},{8,24},{9,25},{10,... | collective-permute-start | bytes 688136 | tf_op jit(solution)/shard_map/ppermute | solution.py:450
  37.6 6.1 %collective-permute-start.13 = (bf16[14,64,128]{2,1,0:T(8,128)(2,1)S(1)}, bf16[14,64,128]{2,1,0:T(8,128)(2,1)S(1)}, u32[]{:S(2)}, u32[]{:S(2)}) collective-permute-start(bf16[14,64,128]{2,1,0:T(8,128)(2,1)S(1)} %get-tuple-element.57), channel_id=1, source_target_pairs={{0,16},{1,17},{2,18},{3,19},{4,20},{5,21},{6,22},{7,23},{8,9},{9,8... | collective-permute-start | bytes 688136 | tf_op jit(solution)/shard_map/ppermute | solution.py:450
  39.4 9.0 %collective-permute-start.10 = (bf16[2,4,64,128]{3,2,1,0:T(8,128)(2,1)S(1)}, bf16[2,4,64,128]{3,2,1,0:T(8,128)(2,1)S(1)}, u32[]{:S(2)}, u32[]{:S(2)}) collective-permute-start(bf16[2,4,64,128]{3,2,1,0:T(8,128)(2,1)S(1)} %get-tuple-element.45), channel_id=1, source_target_pairs={{0,1},{1,0},{2,3},{3,2},{4,5},{5,4},{6,7},{7,6},{8,9},{9,8},{10,11... | collective-permute-start | bytes 393224 | tf_op jit(solution)/shard_map/ppermute | solution.py:439
  40.5 10.4 %collective-permute-start.11 = (bf16[2,4,64,128]{3,2,1,0:T(8,128)(2,1)S(1)}, bf16[2,4,64,128]{3,2,1,0:T(8,128)(2,1)S(1)}, u32[]{:S(2)}, u32[]{:S(2)}) collective-permute-start(bf16[2,4,64,128]{3,2,1,0:T(8,128)(2,1)S(1)} %get-tuple-element.45), channel_id=1, source_target_pairs={{1,2},{2,1},{3,4},{4,3},{5,6},{6,5},{9,10},{10,9},{11,12},{12,11},... | collective-permute-start | bytes 393224 | tf_op jit(solution)/shard_map/ppermute | solution.py:439
  41.2 9.7 %collective-permute-start.8 = (bf16[2,4,64,128]{3,2,1,0:T(8,128)(2,1)S(1)}, bf16[2,4,64,128]{3,2,1,0:T(8,128)(2,1)S(1)}, u32[]{:S(2)}, u32[]{:S(2)}) collective-permute-start(bf16[2,4,64,128]{3,2,1,0:T(8,128)(2,1)S(1)} %get-tuple-element.45), channel_id=1, source_target_pairs={{0,8},{8,0},{16,24},{24,16},{1,9},{9,1},{17,25},{25,17},{2,10},{10... | collective-permute-start | bytes 393224 | tf_op jit(solution)/shard_map/ppermute | solution.py:439
  42.9 8.0 %collective-permute-start.9 = (bf16[2,4,64,128]{3,2,1,0:T(8,128)(2,1)S(1)}, bf16[2,4,64,128]{3,2,1,0:T(8,128)(2,1)S(1)}, u32[]{:S(2)}, u32[]{:S(2)}) collective-permute-start(bf16[2,4,64,128]{3,2,1,0:T(8,128)(2,1)S(1)} %get-tuple-element.45), channel_id=1, source_target_pairs={{8,16},{16,8},{9,17},{17,9},{10,18},{18,10},{11,19},{19,11},{12,20... | collective-permute-start | bytes 393224 | tf_op jit(solution)/shard_map/ppermute | solution.py:439
  43.7 7.3 %collective-permute-start.22 = (bf16[14,32,128]{2,1,0:T(8,128)(2,1)S(1)}, bf16[14,32,128]{2,1,0:T(8,128)(2,1)S(1)}, u32[]{:S(2)}, u32[]{:S(2)}) collective-permute-start(bf16[14,32,128]{2,1,0:T(8,128)(2,1)S(1)} %get-tuple-element.67), channel_id=1, source_target_pairs={{0,16},{1,17},{2,18},{3,19},{4,20},{5,21},{6,22},{7,23},{8,9},{9,8... | collective-permute-start | bytes 344072 | tf_op jit(solution)/shard_map/ppermute | solution.py:450
  51.0 6.7 %collective-permute-start.23 = (f32[14,16,128]{2,1,0:T(8,128)S(1)}, f32[14,16,128]{2,1,0:T(8,128)S(1)}, u32[]{:S(2)}, u32[]{:S(2)}) collective-permute-start(f32[14,16,128]{2,1,0:T(8,128)S(1)} %get-tuple-element.69), channel_id=1, source_target_pairs={{0,2},{1,3},{2,0},{3,1},{4,6},{5,7},{6,4},{7,5},{8,10},{9,11},{10,... | collective-permute-start | bytes 344072 | tf_op jit(solution)/shard_map/ppermute | solution.py:450
  53.7 5.8 %collective-permute-start.15 = (f32[14,16,128]{2,1,0:T(8,128)S(1)}, f32[14,16,128]{2,1,0:T(8,128)S(1)}, u32[]{:S(2)}, u32[]{:S(2)}) collective-permute-start(f32[14,16,128]{2,1,0:T(8,128)S(1)} %get-tuple-element.61), channel_id=1, source_target_pairs={{0,2},{1,3},{2,0},{3,1},{4,6},{5,7},{6,4},{7,5},{8,10},{9,11},{10,... | collective-permute-start | bytes 344072 | tf_op jit(solution)/shard_map/ppermute | solution.py:450
  57.8 7.4 %collective-permute-start.24 = (bf16[14,16,128]{2,1,0:T(8,128)(2,1)S(1)}, bf16[14,16,128]{2,1,0:T(8,128)(2,1)S(1)}, u32[]{:S(2)}, u32[]{:S(2)}) collective-permute-start(bf16[14,16,128]{2,1,0:T(8,128)(2,1)S(1)} %pair_sum.3.left), channel_id=1, source_target_pairs={{0,4},{1,5},{2,6},{3,7},{4,0},{5,1},{6,2},{7,3},{8,12},{9,13},{10,... | collective-permute-start | bytes 172040 | tf_op jit(solution)/shard_map/ppermute | solution.py:450
  59.5 7.8 %collective-permute-start.16 = (bf16[14,16,128]{2,1,0:T(8,128)(2,1)S(1)}, bf16[14,16,128]{2,1,0:T(8,128)(2,1)S(1)}, u32[]{:S(2)}, u32[]{:S(2)}) collective-permute-start(bf16[14,16,128]{2,1,0:T(8,128)(2,1)S(1)} %pair_sum.2.left), channel_id=1, source_target_pairs={{0,4},{1,5},{2,6},{3,7},{4,0},{5,1},{6,2},{7,3},{8,12},{9,13},{10,... | collective-permute-start | bytes 172040 | tf_op jit(solution)/shard_map/ppermute | solution.py:450
  61.4 19.9 %all-to-all-start.1 = ((bf16[8,128,128]{2,1,0:T(8,128)(2,1)}), bf16[8,128,128]{2,1,0:T(8,128)(2,1)S(1)}, u32[]{:S(2)}, u32[]{:S(2)}) async-start(bf16[8,128,128]{2,1,0:T(8,128)(2,1)} %back.1.refs_0_), calls=%async_computation.1 | async-start | bytes 524288 | tf_op jit(solution)/shard_map/all_to_all | solution.py:601
  65.2 7.7 %collective-permute-start.25 = (bf16[14,16,128]{2,1,0:T(8,128)(2,1)S(1)}, bf16[14,16,128]{2,1,0:T(8,128)(2,1)S(1)}, u32[]{:S(2)}, u32[]{:S(2)}) collective-permute-start(bf16[14,16,128]{2,1,0:T(8,128)(2,1)S(1)} %far_sum.3.refs_1_), channel_id=1, source_target_pairs={{0,2},{1,3},{2,0},{3,1},{4,6},{5,7},{6,4},{7,5},{8,10},{9,11},{10,... | collective-permute-start | bytes 172040 | tf_op jit(solution)/shard_map/ppermute | solution.py:450
  67.3 7.0 %collective-permute-start.17 = (bf16[14,16,128]{2,1,0:T(8,128)(2,1)S(1)}, bf16[14,16,128]{2,1,0:T(8,128)(2,1)S(1)}, u32[]{:S(2)}, u32[]{:S(2)}) collective-permute-start(bf16[14,16,128]{2,1,0:T(8,128)(2,1)S(1)} %far_sum.2.mine), channel_id=1, source_target_pairs={{0,2},{1,3},{2,0},{3,1},{4,6},{5,7},{6,4},{7,5},{8,10},{9,11},{10,... | collective-permute-start | bytes 172040 | tf_op jit(solution)/shard_map/ppermute | solution.py:450
  72.9 6.0 %collective-permute-start.26 = (bf16[14,32,128]{2,1,0:T(8,128)(2,1)S(1)}, bf16[14,32,128]{2,1,0:T(8,128)(2,1)S(1)}, u32[]{:S(2)}, u32[]{:S(2)}) collective-permute-start(bf16[14,32,128]{2,1,0:T(8,128)(2,1)S(1)} %join.9.mine), channel_id=1, source_target_pairs={{0,16},{1,17},{2,18},{3,19},{4,20},{5,21},{6,22},{7,23},{8,9},{9,8... | collective-permute-start | bytes 344072 | tf_op jit(solution)/shard_map/ppermute | solution.py:450
  74.4 6.0 %collective-permute-start.18 = (bf16[14,32,128]{2,1,0:T(8,128)(2,1)S(1)}, bf16[14,32,128]{2,1,0:T(8,128)(2,1)S(1)}, u32[]{:S(2)}, u32[]{:S(2)}) collective-permute-start(bf16[14,32,128]{2,1,0:T(8,128)(2,1)S(1)} %join.6.mine), channel_id=1, source_target_pairs={{0,1},{1,0},{2,3},{3,2},{4,5},{5,4},{6,7},{7,6},{8,24},{9,25},{10,... | collective-permute-start | bytes 344072 | tf_op jit(solution)/shard_map/ppermute | solution.py:450
  79.0 6.1 %collective-permute-start.27 = (bf16[14,64,128]{2,1,0:T(8,128)(2,1)S(1)}, bf16[14,64,128]{2,1,0:T(8,128)(2,1)S(1)}, u32[]{:S(2)}, u32[]{:S(2)}) collective-permute-start(bf16[14,64,128]{2,1,0:T(8,128)(2,1)S(1)} %join.10.refs_1_), channel_id=1, source_target_pairs={{0,1},{1,0},{2,3},{3,2},{4,5},{5,4},{6,7},{7,6},{8,24},{9,25},{10,... | collective-permute-start | bytes 688136 | tf_op jit(solution)/shard_map/ppermute | solution.py:450
  80.4 6.1 %collective-permute-start.19 = (bf16[14,64,128]{2,1,0:T(8,128)(2,1)S(1)}, bf16[14,64,128]{2,1,0:T(8,128)(2,1)S(1)}, u32[]{:S(2)}, u32[]{:S(2)}) collective-permute-start(bf16[14,64,128]{2,1,0:T(8,128)(2,1)S(1)} %join.7.mine), channel_id=1, source_target_pairs={{0,16},{1,17},{2,18},{3,19},{4,20},{5,21},{6,22},{7,23},{8,9},{9,8... | collective-permute-start | bytes 688136 | tf_op jit(solution)/shard_map/ppermute | solution.py:450
  (14 other events, 118.7 us)

commit v3 on v2

--- a/solution.py
+++ b/solution.py
@@ -12,6 +12,7 @@
 OFFSETS = 27
 LABEL_ROWS = 16
 WAIT = 1_500_000_000
+CHUNK = 6
 BF16 = jnp.bfloat16
 F32 = jnp.float32
 
@@ -369,17 +370,19 @@
 def write_gradient(scale, parts, grad_hbm, grad, sems):
     channels = grad.shape[1]
     copies = []
-    for n, ref in enumerate(parts):
-        start = n * ref.shape[0]
-        count = min(ref.shape[0], OFFSETS - start)
-        for u in range(count):
-            grad[pl.ds((start + u) * channels, channels), :] = ref[u].astype(F32) * scale
-        part = pl.ds(start * channels, count * channels)
-        copies.append((grad.at[part], grad_hbm.at[part], sems.at[n]))
+    for first in range(0, OFFSETS, CHUNK):
+        last = min(first + CHUNK, OFFSETS)
+        for offset in range(first, last):
+            ref = parts[offset // parts[0].shape[0]]
+            rows = slice(offset * channels, (offset + 1) * channels)
+            grad[rows, :] = ref[offset % ref.shape[0]].astype(F32) * scale
+        part = pl.ds(first * channels, (last - first) * channels)
+        copies.append(
+            pltpu.make_async_copy(grad.at[part], grad_hbm.at[part], sems.at[len(copies)])
+        )
+        copies[-1].start()
     for copy in copies:
-        pltpu.make_async_copy(*copy).start()
-    for copy in copies:
-        pltpu.make_async_copy(*copy).wait()
+        copy.wait()
 
 
 def finish_kernel(scale, owner, *refs):
@@ -513,7 +516,8 @@
     whole = ((OFFSETS * channels, channels), F32)
     first = len(after)
     return call(
-        functools.partial(finish_kernel, scale, owner), held, parts, [], [whole, 2],
+        functools.partial(finish_kernel, scale, owner), held, parts, [],
+        [whole, -(-OFFSETS // CHUNK)],
         [whole, whole], name="finish", after=after,
         aliases={first: 0, first + 1: 1} if held else {},
     )
@@ -593,7 +597,7 @@
         [near, table, cells, columns, flat, 1], flops=2 * macs, name="back",
     )
     parts = [
-        split_stage(2, g, parts[g][0], swap(parts[g][1], partner_at(1, g)), F32, after=sides if g == 1 else ())
+        split_stage(2, g, parts[g][0], swap(parts[g][1], partner_at(1, g)), F32, after=sides[:2] if g == 1 else ())
         for g in groups
     ]
     parts = [pair_stage(*parts[g], wire, after=[returning] if g == 1 else ()) for g in groups]

time: 90.7 us -> 89.9 us (level)
  waiting for transfers between devices: 24.1 us -> 22.7 us
    ppermute x12, waiting for transfers between devices: 1.53 us -> 0.19 us  [halo(): sides += [lax.ppermute(rows, axis, even), lax.ppermute(rows, axis, odd)]]
    all_to_all x1, starting transfers between devices: 3.81 us -> 4.96 us  [per_device(): lax.all_to_all(returning, 'dev', split_axis=0, concat_axis=0, tiled=True)]
    ppermute x12, starting transfers between devices: 8.99 us -> 7.85 us  [halo(): sides += [lax.ppermute(rows, axis, even), lax.ppermute(rows, axis, odd)]]
where the time goes in v3:
time: 89.9 us; the launch traced here: 89.4 us
  starting transfers between devices  47.9 us (53%)
  waiting for transfers between devices  22.7 us (25%)
  Pallas kernels  17.7 us (20%)
  between operations  1 us (1%)
    ppermute x18, starting transfers between devices, swap(): return lax.ppermute(rows, ('tile', 'dev'), pairs)  27.8 us
    pallas_call x27, Pallas kernels, call(): pl.pallas_call(body, out_shape=shapes, in_specs=[ANY] * len(after) + [HBM...  17.7 us
    ppermute x18, waiting for transfers between devices, swap(): return lax.ppermute(rows, ('tile', 'dev'), pairs)  16.5 us
    ppermute x12, starting transfers between devices, halo(): sides += [lax.ppermute(rows, axis, even), lax.ppermute(rows, axis, odd)]  7.85 us
    all_to_all x1, starting transfers between devices, per_device(): lax.all_to_all(outgoing, 'dev', split_axis=0, concat_axis=0, tiled=True)  7.29 us
    all_to_all x1, waiting for transfers between devices, per_device(): lax.all_to_all(outgoing, 'dev', split_axis=0, concat_axis=0, tiled=True)  5.97 us
    all_to_all x1, starting transfers between devices, per_device(): lax.all_to_all(returning, 'dev', split_axis=0, concat_axis=0, tiled=True)  4.96 us
  transfers between devices with their start and end apart: 32, of which 12 were waited for; matrix products, arithmetic and copies ran while one was open for 0% of the time, Pallas kernels for 13%

profile of v3, /device:TPU:0, one launch (start us, length us, event | category | flops | bytes accessed | tf_op | source)
XLA Modules:
  0.0 89.4 jit_solution(12604633336186500004)
XLA Ops:
  0.6 1.7 %pack.1 = (bf16[8,144,128]{2,1,0:T(8,128)(2,1)}, bf16[4,64,128]{2,1,0:T(8,128)(2,1)}) custom-call(s32[8]{0:T(128)} %morton_hbm.3, s32[4]{0:T(128)} %rim_hbm.5, bf16[8,64,128]{2,1,0:T(8,128)(2,1)} %features_hbm.1, bf16[8,64,128]{2,1,0:T(8,128)(2,1)} %cotangent.3), custom_call_target="tpu_custom_call" | custom-call | flops 1500000000 | bytes 622640 | tf_op jit(solution)/shard_map/pack/pallas_call | solution.py:421
  2.4 7.3 %all-to-all-start = ((bf16[8,144,128]{2,1,0:T(8,128)(2,1)}), bf16[8,144,128]{2,1,0:T(8,128)(2,1)S(1)}, u32[]{:S(2)}, u32[]{:S(2)}) async-start(bf16[8,144,128]{2,1,0:T(8,128)(2,1)} %get-tuple-element.39), calls=%async_computation | async-start | bytes 589824 | tf_op jit(solution)/shard_map/all_to_all | solution.py:548
  10.6 2.1 %collective-permute-start.6 = (bf16[4,64,128]{2,1,0:T(8,128)(2,1)}, bf16[4,64,128]{2,1,0:T(8,128)(2,1)S(1)}, u32[]{:S(2)}, u32[]{:S(2)}) collective-permute-start(bf16[4,64,128]{2,1,0:T(8,128)(2,1)} %get-tuple-element.42), channel_id=1, source_target_pairs={{0,1},{1,0},{2,3},{3,2},{4,5},{5,4},{6,7},{7,6},{8,9},{9,8},{10,11... | collective-permute-start | bytes 196616 | tf_op jit(solution)/shard_map/ppermute | solution.py:442
  13.3 6.0 %all-to-all-done.arrived = bf16[8,144,128]{2,1,0:T(8,128)(2,1)S(1)} async-done(((bf16[8,144,128]{2,1,0:T(8,128)(2,1)}), bf16[8,144,128]{2,1,0:T(8,128)(2,1)S(1)}, u32[]{:S(2)}, u32[]{:S(2)}) %all-to-all-start) | async-done | bytes 294944 | tf_op jit(solution)/shard_map/all_to_all | solution.py:548
  22.8 2.0 %hidden_grad.1 = (bf16[512,3456]{1,0:T(8,128)(2,1)S(1)}, f32[512,128]{1,0:T(8,128)S(1)}) custom-call(s32[8,27]{1,0:T(8,128)S(1)} %copy-done.2, bf16[8,64,128]{2,1,0:T(8,128)(2,1)S(1)} %copy-done.1, bf16[3456,128]{1,0:T(8,128)(2,1)S(1)} %copy-done.3, bf16[4,64,128]{2,1,0:T(8,128)(2,1)S(1)} %collective-permute-done.4.side_a, ...), custom_call_target="tpu_custom_call" | custom-call | flops 452984832 | bytes 5079904 | tf_op jit(solution)/shard_map/hidden_grad/pallas_call | solution.py:421
  25.0 2.6 %middle.1 = (bf16[8,64,128]{2,1,0:T(8,128)(2,1)S(1)}, bf16[8,64,128]{2,1,0:T(8,128)(2,1)S(1)}, bf16[2,4,64,128]{3,2,1,0:T(8,128)(2,1)S(1)}, bf16[512,3456]{1,0:T...) custom-call(s32[8,27]{1,0:T(8,128)S(1)} %copy-done.2, s32[4]{0:T(128)S(1)} %copy-done.4, ...), custom_call_target="tpu_custom_call" | custom-call | flops 452984832 | bytes 5735280 | tf_op jit(solution)/shard_map/middle/pallas_call | solution.py:421
  28.3 2.5 %collective-permute-start.20 = (f32[14,128,128]{2,1,0:T(8,128)S(1)}, f32[14,128,128]{2,1,0:T(8,128)S(1)}, u32[]{:S(2)}, u32[]{:S(2)}) collective-permute-start(f32[14,128,128]{2,1,0:T(8,128)S(1)} %get-tuple-element.63), channel_id=1, source_target_pairs={{0,8},{1,9},{2,10},{3,11},{4,12},{5,13},{6,14},{7,15},{8,0},{9,1},... | collective-permute-start | bytes 2752520 | tf_op jit(solution)/shard_map/ppermute | solution.py:453
  33.0 4.5 %collective-permute-start.21 = (bf16[14,64,128]{2,1,0:T(8,128)(2,1)S(1)}, bf16[14,64,128]{2,1,0:T(8,128)(2,1)S(1)}, u32[]{:S(2)}, u32[]{:S(2)}) collective-permute-start(bf16[14,64,128]{2,1,0:T(8,128)(2,1)S(1)} %get-tuple-element.65), channel_id=1, source_target_pairs={{0,1},{1,0},{2,3},{3,2},{4,5},{5,4},{6,7},{7,6},{8,24},{9,25},{10,... | collective-permute-start | bytes 688136 | tf_op jit(solution)/shard_map/ppermute | solution.py:453
  37.6 1.8 %collective-permute-start.13 = (bf16[14,64,128]{2,1,0:T(8,128)(2,1)S(1)}, bf16[14,64,128]{2,1,0:T(8,128)(2,1)S(1)}, u32[]{:S(2)}, u32[]{:S(2)}) collective-permute-start(bf16[14,64,128]{2,1,0:T(8,128)(2,1)S(1)} %get-tuple-element.57), channel_id=1, source_target_pairs={{0,16},{1,17},{2,18},{3,19},{4,20},{5,21},{6,22},{7,23},{8,9},{9,8... | collective-permute-start | bytes 688136 | tf_op jit(solution)/shard_map/ppermute | solution.py:453
  40.0 2.9 %collective-permute-done.21.other = bf16[14,64,128]{2,1,0:T(8,128)(2,1)S(1)} collective-permute-done((bf16[14,64,128]{2,1,0:T(8,128)(2,1)S(1)}, bf16[14,64,128]{2,1,0:T(8,128)(2,1)S(1)}, u32[]{:S(2)}, u32[]{:S(2)}) %collective-permute-start.21) | collective-permute-done | bytes 229408 | tf_op jit(solution)/shard_map/ppermute | solution.py:453
  43.0 2.1 %collective-permute-start.22 = (bf16[14,32,128]{2,1,0:T(8,128)(2,1)S(1)}, bf16[14,32,128]{2,1,0:T(8,128)(2,1)S(1)}, u32[]{:S(2)}, u32[]{:S(2)}) collective-permute-start(bf16[14,32,128]{2,1,0:T(8,128)(2,1)S(1)} %get-tuple-element.67), channel_id=1, source_target_pairs={{0,16},{1,17},{2,18},{3,19},{4,20},{5,21},{6,22},{7,23},{8,9},{9,8... | collective-permute-start | bytes 344072 | tf_op jit(solution)/shard_map/ppermute | solution.py:453
  45.1 2.4 %collective-permute-start.14 = (bf16[14,32,128]{2,1,0:T(8,128)(2,1)S(1)}, bf16[14,32,128]{2,1,0:T(8,128)(2,1)S(1)}, u32[]{:S(2)}, u32[]{:S(2)}) collective-permute-start(bf16[14,32,128]{2,1,0:T(8,128)(2,1)S(1)} %get-tuple-element.59), channel_id=1, source_target_pairs={{0,1},{1,0},{2,3},{3,2},{4,5},{5,4},{6,7},{7,6},{8,24},{9,25},{10,... | collective-permute-start | bytes 344072 | tf_op jit(solution)/shard_map/ppermute | solution.py:453
  49.0 4.1 %collective-permute-start.23 = (f32[14,16,128]{2,1,0:T(8,128)S(1)}, f32[14,16,128]{2,1,0:T(8,128)S(1)}, u32[]{:S(2)}, u32[]{:S(2)}) collective-permute-start(f32[14,16,128]{2,1,0:T(8,128)S(1)} %get-tuple-element.69), channel_id=1, source_target_pairs={{0,2},{1,3},{2,0},{3,1},{4,6},{5,7},{6,4},{7,5},{8,10},{9,11},{10,... | collective-permute-start | bytes 344072 | tf_op jit(solution)/shard_map/ppermute | solution.py:453
  53.2 2.9 %back.1.refs_0_ = bf16[8,128,128]{2,1,0:T(8,128)(2,1)} custom-call(s32[8,27]{1,0:T(8,128)S(1)} %copy-done.2, bf16[8,64,128]{2,1,0:T(8,128)(2,1)S(1)} %copy-done.1, bf16[3456,128]{1,0:T(8,128)(2,1)S(1)} %copy-done, bf16[8,64,128]{2,1,0:T(8,128)(2,1)S(1)} %get-tuple-element.47.pre_grad, bf16[2,4,64,128]{3,2,1,0:T(8,128)(2,1)S(1)} %collective-permute-done.8.side_a.refs_0_, ...), custom_call_target="tpu_custom_call" | custom-call | flops 452984832 | bytes 1999712 | tf_op jit(solution)/shard_map/back/pallas_call | solution.py:421
  56.1 2.0 %collective-permute-done.23.refs_2_ = f32[14,16,128]{2,1,0:T(8,128)S(1)} collective-permute-done((f32[14,16,128]{2,1,0:T(8,128)S(1)}, f32[14,16,128]{2,1,0:T(8,128)S(1)}, u32[]{:S(2)}, u32[]{:S(2)}) %collective-permute-start.23) | collective-permute-done | bytes 114720 | tf_op jit(solution)/shard_map/ppermute | solution.py:453
  58.1 2.5 %collective-permute-start.24 = (bf16[14,16,128]{2,1,0:T(8,128)(2,1)S(1)}, bf16[14,16,128]{2,1,0:T(8,128)(2,1)S(1)}, u32[]{:S(2)}, u32[]{:S(2)}) collective-permute-start(bf16[14,16,128]{2,1,0:T(8,128)(2,1)S(1)} %pair_sum.3.left), channel_id=1, source_target_pairs={{0,4},{1,5},{2,6},{3,7},{4,0},{5,1},{6,2},{7,3},{8,12},{9,13},{10,... | collective-permute-start | bytes 172040 | tf_op jit(solution)/shard_map/ppermute | solution.py:453
  61.5 5.0 %all-to-all-start.1 = ((bf16[8,128,128]{2,1,0:T(8,128)(2,1)}), bf16[8,128,128]{2,1,0:T(8,128)(2,1)S(1)}, u32[]{:S(2)}, u32[]{:S(2)}) async-start(bf16[8,128,128]{2,1,0:T(8,128)(2,1)} %back.1.refs_0_), calls=%async_computation.1 | async-start | bytes 524288 | tf_op jit(solution)/shard_map/all_to_all | solution.py:605
  66.5 2.1 %collective-permute-start.25 = (bf16[14,16,128]{2,1,0:T(8,128)(2,1)S(1)}, bf16[14,16,128]{2,1,0:T(8,128)(2,1)S(1)}, u32[]{:S(2)}, u32[]{:S(2)}) collective-permute-start(bf16[14,16,128]{2,1,0:T(8,128)(2,1)S(1)} %far_sum.3.refs_1_), channel_id=1, source_target_pairs={{0,2},{1,3},{2,0},{3,1},{4,6},{5,7},{6,4},{7,5},{8,10},{9,11},{10,... | collective-permute-start | bytes 172040 | tf_op jit(solution)/shard_map/ppermute | solution.py:453
  68.7 2.6 %output.1 = (bf16[8,64,128]{2,1,0:T(8,128)(2,1)}, f32[8,8,128]{2,1,0:T(8,128)S(1)}) custom-call(s32[8,27]{1,0:T(8,128)S(1)} %copy-done.2, s32[8]{0:T(128)S(1)} %copy-done.5, bf16[3456,128]{1,0:T(8,128)(2,1)S(1)} %copy-done.3, bf16[8,64,128]{2,1,0:T(8,128)(2,1)S(1)} %get-tuple-element.44.hidden, bf16[8,64,128]{2,1,0:T(8,128)(2,1)S(1)} %get-tuple-element.40.morton, ...), custom_call_target="tpu_custom_call" | custom-call | flops 452984832 | bytes 1835904 | tf_op jit(solution)/shard_map/output/pallas_call | solution.py:421
  71.9 1.9 %collective-permute-done.17.other = bf16[14,16,128]{2,1,0:T(8,128)(2,1)S(1)} collective-permute-done((bf16[14,16,128]{2,1,0:T(8,128)(2,1)S(1)}, bf16[14,16,128]{2,1,0:T(8,128)(2,1)S(1)}, u32[]{:S(2)}, u32[]{:S(2)}) %collective-permute-start.17) | collective-permute-done | bytes 57376 | tf_op jit(solution)/shard_map/ppermute | solution.py:453
  75.4 2.0 %collective-permute-done.26.other = bf16[14,32,128]{2,1,0:T(8,128)(2,1)S(1)} collective-permute-done((bf16[14,32,128]{2,1,0:T(8,128)(2,1)S(1)}, bf16[14,32,128]{2,1,0:T(8,128)(2,1)S(1)}, u32[]{:S(2)}, u32[]{:S(2)}) %collective-permute-start.26) | collective-permute-done | bytes 114720 | tf_op jit(solution)/shard_map/ppermute | solution.py:453
  77.4 2.1 %collective-permute-start.27 = (bf16[14,64,128]{2,1,0:T(8,128)(2,1)S(1)}, bf16[14,64,128]{2,1,0:T(8,128)(2,1)S(1)}, u32[]{:S(2)}, u32[]{:S(2)}) collective-permute-start(bf16[14,64,128]{2,1,0:T(8,128)(2,1)S(1)} %join.10.refs_1_), channel_id=1, source_target_pairs={{0,1},{1,0},{2,3},{3,2},{4,5},{5,4},{6,7},{7,6},{8,24},{9,25},{10,... | collective-permute-start | bytes 688136 | tf_op jit(solution)/shard_map/ppermute | solution.py:453
  80.3 3.2 %collective-permute-done.27.refs_2_ = bf16[14,64,128]{2,1,0:T(8,128)(2,1)S(1)} collective-permute-done((bf16[14,64,128]{2,1,0:T(8,128)(2,1)S(1)}, bf16[14,64,128]{2,1,0:T(8,128)(2,1)S(1)}, u32[]{:S(2)}, u32[]{:S(2)}) %collective-permute-start.27) | collective-permute-done | bytes 229408 | tf_op jit(solution)/shard_map/ppermute | solution.py:453
  83.7 2.2 %collective-permute-done.19.other = bf16[14,64,128]{2,1,0:T(8,128)(2,1)S(1)} collective-permute-done((bf16[14,64,128]{2,1,0:T(8,128)(2,1)S(1)}, bf16[14,64,128]{2,1,0:T(8,128)(2,1)S(1)}, u32[]{:S(2)}, u32[]{:S(2)}) %collective-permute-start.19) | collective-permute-done | bytes 229408 | tf_op jit(solution)/shard_map/ppermute | solution.py:453
  (79 shorter events, 18.2 us)
Async XLA Ops:
  2.4 16.9 %all-to-all-start = ((bf16[8,144,128]{2,1,0:T(8,128)(2,1)}), bf16[8,144,128]{2,1,0:T(8,128)(2,1)S(1)}, u32[]{:S(2)}, u32[]{:S(2)}) async-start(bf16[8,144,128]{2,1,0:T(8,128)(2,1)} %get-tuple-element.39), calls=%async_computation | async-start | bytes 589824 | tf_op jit(solution)/shard_map/all_to_all | solution.py:548
  9.7 10.2 %collective-permute-start.4 = (bf16[4,64,128]{2,1,0:T(8,128)(2,1)}, bf16[4,64,128]{2,1,0:T(8,128)(2,1)S(1)}, u32[]{:S(2)}, u32[]{:S(2)}) collective-permute-start(bf16[4,64,128]{2,1,0:T(8,128)(2,1)} %get-tuple-element.42), channel_id=1, source_target_pairs={{0,8},{8,0},{16,24},{24,16},{1,9},{9,1},{17,25},{25,17},{2,10},{10... | collective-permute-start | bytes 196616 | tf_op jit(solution)/shard_map/ppermute | solution.py:442
  9.8 10.8 %collective-permute-start.5 = (bf16[4,64,128]{2,1,0:T(8,128)(2,1)}, bf16[4,64,128]{2,1,0:T(8,128)(2,1)S(1)}, u32[]{:S(2)}, u32[]{:S(2)}) collective-permute-start(bf16[4,64,128]{2,1,0:T(8,128)(2,1)} %get-tuple-element.42), channel_id=1, source_target_pairs={{8,16},{16,8},{9,17},{17,9},{10,18},{18,10},{11,19},{19,11},{12,20... | collective-permute-start | bytes 196616 | tf_op jit(solution)/shard_map/ppermute | solution.py:442
  10.6 11.5 %collective-permute-start.6 = (bf16[4,64,128]{2,1,0:T(8,128)(2,1)}, bf16[4,64,128]{2,1,0:T(8,128)(2,1)S(1)}, u32[]{:S(2)}, u32[]{:S(2)}) collective-permute-start(bf16[4,64,128]{2,1,0:T(8,128)(2,1)} %get-tuple-element.42), channel_id=1, source_target_pairs={{0,1},{1,0},{2,3},{3,2},{4,5},{5,4},{6,7},{7,6},{8,9},{9,8},{10,11... | collective-permute-start | bytes 196616 | tf_op jit(solution)/shard_map/ppermute | solution.py:442
  12.7 10.1 %collective-permute-start.7 = (bf16[4,64,128]{2,1,0:T(8,128)(2,1)}, bf16[4,64,128]{2,1,0:T(8,128)(2,1)S(1)}, u32[]{:S(2)}, u32[]{:S(2)}) collective-permute-start(bf16[4,64,128]{2,1,0:T(8,128)(2,1)} %get-tuple-element.42), channel_id=1, source_target_pairs={{1,2},{2,1},{3,4},{4,3},{5,6},{6,5},{9,10},{10,9},{11,12},{12,11},... | collective-permute-start | bytes 196616 | tf_op jit(solution)/shard_map/ppermute | solution.py:442
  31.5 6.0 %collective-permute-start.12 = (f32[14,128,128]{2,1,0:T(8,128)S(1)}, f32[14,128,128]{2,1,0:T(8,128)S(1)}, u32[]{:S(2)}, u32[]{:S(2)}) collective-permute-start(f32[14,128,128]{2,1,0:T(8,128)S(1)} %get-tuple-element.55), channel_id=1, source_target_pairs={{0,8},{1,9},{2,10},{3,11},{4,12},{5,13},{6,14},{7,15},{8,0},{9,1},... | collective-permute-start | bytes 2752520 | tf_op jit(solution)/shard_map/ppermute | solution.py:453
  33.0 9.9 %collective-permute-start.21 = (bf16[14,64,128]{2,1,0:T(8,128)(2,1)S(1)}, bf16[14,64,128]{2,1,0:T(8,128)(2,1)S(1)}, u32[]{:S(2)}, u32[]{:S(2)}) collective-permute-start(bf16[14,64,128]{2,1,0:T(8,128)(2,1)S(1)} %get-tuple-element.65), channel_id=1, source_target_pairs={{0,1},{1,0},{2,3},{3,2},{4,5},{5,4},{6,7},{7,6},{8,24},{9,25},{10,... | collective-permute-start | bytes 688136 | tf_op jit(solution)/shard_map/ppermute | solution.py:453
  37.6 7.5 %collective-permute-start.13 = (bf16[14,64,128]{2,1,0:T(8,128)(2,1)S(1)}, bf16[14,64,128]{2,1,0:T(8,128)(2,1)S(1)}, u32[]{:S(2)}, u32[]{:S(2)}) collective-permute-start(bf16[14,64,128]{2,1,0:T(8,128)(2,1)S(1)} %get-tuple-element.57), channel_id=1, source_target_pairs={{0,16},{1,17},{2,18},{3,19},{4,20},{5,21},{6,22},{7,23},{8,9},{9,8... | collective-permute-start | bytes 688136 | tf_op jit(solution)/shard_map/ppermute | solution.py:453
  39.4 8.2 %collective-permute-start.8 = (bf16[2,4,64,128]{3,2,1,0:T(8,128)(2,1)S(1)}, bf16[2,4,64,128]{3,2,1,0:T(8,128)(2,1)S(1)}, u32[]{:S(2)}, u32[]{:S(2)}) collective-permute-start(bf16[2,4,64,128]{3,2,1,0:T(8,128)(2,1)S(1)} %get-tuple-element.45), channel_id=1, source_target_pairs={{0,8},{8,0},{16,24},{24,16},{1,9},{9,1},{17,25},{25,17},{2,10},{10... | collective-permute-start | bytes 393224 | tf_op jit(solution)/shard_map/ppermute | solution.py:442
  39.4 8.9 %collective-permute-start.9 = (bf16[2,4,64,128]{3,2,1,0:T(8,128)(2,1)S(1)}, bf16[2,4,64,128]{3,2,1,0:T(8,128)(2,1)S(1)}, u32[]{:S(2)}, u32[]{:S(2)}) collective-permute-start(bf16[2,4,64,128]{3,2,1,0:T(8,128)(2,1)S(1)} %get-tuple-element.45), channel_id=1, source_target_pairs={{8,16},{16,8},{9,17},{17,9},{10,18},{18,10},{11,19},{19,11},{12,20... | collective-permute-start | bytes 393224 | tf_op jit(solution)/shard_map/ppermute | solution.py:442
  43.0 5.9 %collective-permute-start.22 = (bf16[14,32,128]{2,1,0:T(8,128)(2,1)S(1)}, bf16[14,32,128]{2,1,0:T(8,128)(2,1)S(1)}, u32[]{:S(2)}, u32[]{:S(2)}) collective-permute-start(bf16[14,32,128]{2,1,0:T(8,128)(2,1)S(1)} %get-tuple-element.67), channel_id=1, source_target_pairs={{0,16},{1,17},{2,18},{3,19},{4,20},{5,21},{6,22},{7,23},{8,9},{9,8... | collective-permute-start | bytes 344072 | tf_op jit(solution)/shard_map/ppermute | solution.py:453
  45.1 7.9 %collective-permute-start.14 = (bf16[14,32,128]{2,1,0:T(8,128)(2,1)S(1)}, bf16[14,32,128]{2,1,0:T(8,128)(2,1)S(1)}, u32[]{:S(2)}, u32[]{:S(2)}) collective-permute-start(bf16[14,32,128]{2,1,0:T(8,128)(2,1)S(1)} %get-tuple-element.59), channel_id=1, source_target_pairs={{0,1},{1,0},{2,3},{3,2},{4,5},{5,4},{6,7},{7,6},{8,24},{9,25},{10,... | collective-permute-start | bytes 344072 | tf_op jit(solution)/shard_map/ppermute | solution.py:453
  47.5 5.7 %collective-permute-start.10 = (bf16[2,4,64,128]{3,2,1,0:T(8,128)(2,1)S(1)}, bf16[2,4,64,128]{3,2,1,0:T(8,128)(2,1)S(1)}, u32[]{:S(2)}, u32[]{:S(2)}) collective-permute-start(bf16[2,4,64,128]{3,2,1,0:T(8,128)(2,1)S(1)} %get-tuple-element.45), channel_id=1, source_target_pairs={{0,1},{1,0},{2,3},{3,2},{4,5},{5,4},{6,7},{7,6},{8,9},{9,8},{10,11... | collective-permute-start | bytes 393224 | tf_op jit(solution)/shard_map/ppermute | solution.py:442
  47.6 5.6 %collective-permute-start.11 = (bf16[2,4,64,128]{3,2,1,0:T(8,128)(2,1)S(1)}, bf16[2,4,64,128]{3,2,1,0:T(8,128)(2,1)S(1)}, u32[]{:S(2)}, u32[]{:S(2)}) collective-permute-start(bf16[2,4,64,128]{3,2,1,0:T(8,128)(2,1)S(1)} %get-tuple-element.45), channel_id=1, source_target_pairs={{1,2},{2,1},{3,4},{4,3},{5,6},{6,5},{9,10},{10,9},{11,12},{12,11},... | collective-permute-start | bytes 393224 | tf_op jit(solution)/shard_map/ppermute | solution.py:442
  49.0 9.1 %collective-permute-start.23 = (f32[14,16,128]{2,1,0:T(8,128)S(1)}, f32[14,16,128]{2,1,0:T(8,128)S(1)}, u32[]{:S(2)}, u32[]{:S(2)}) collective-permute-start(f32[14,16,128]{2,1,0:T(8,128)S(1)} %get-tuple-element.69), channel_id=1, source_target_pairs={{0,2},{1,3},{2,0},{3,1},{4,6},{5,7},{6,4},{7,5},{8,10},{9,11},{10,... | collective-permute-start | bytes 344072 | tf_op jit(solution)/shard_map/ppermute | solution.py:453
  53.1 7.5 %collective-permute-start.15 = (f32[14,16,128]{2,1,0:T(8,128)S(1)}, f32[14,16,128]{2,1,0:T(8,128)S(1)}, u32[]{:S(2)}, u32[]{:S(2)}) collective-permute-start(f32[14,16,128]{2,1,0:T(8,128)S(1)} %get-tuple-element.61), channel_id=1, source_target_pairs={{0,2},{1,3},{2,0},{3,1},{4,6},{5,7},{6,4},{7,5},{8,10},{9,11},{10,... | collective-permute-start | bytes 344072 | tf_op jit(solution)/shard_map/ppermute | solution.py:453
  58.1 8.3 %collective-permute-start.24 = (bf16[14,16,128]{2,1,0:T(8,128)(2,1)S(1)}, bf16[14,16,128]{2,1,0:T(8,128)(2,1)S(1)}, u32[]{:S(2)}, u32[]{:S(2)}) collective-permute-start(bf16[14,16,128]{2,1,0:T(8,128)(2,1)S(1)} %pair_sum.3.left), channel_id=1, source_target_pairs={{0,4},{1,5},{2,6},{3,7},{4,0},{5,1},{6,2},{7,3},{8,12},{9,13},{10,... | collective-permute-start | bytes 172040 | tf_op jit(solution)/shard_map/ppermute | solution.py:453
  60.6 7.9 %collective-permute-start.16 = (bf16[14,16,128]{2,1,0:T(8,128)(2,1)S(1)}, bf16[14,16,128]{2,1,0:T(8,128)(2,1)S(1)}, u32[]{:S(2)}, u32[]{:S(2)}) collective-permute-start(bf16[14,16,128]{2,1,0:T(8,128)(2,1)S(1)} %pair_sum.2.left), channel_id=1, source_target_pairs={{0,4},{1,5},{2,6},{3,7},{4,0},{5,1},{6,2},{7,3},{8,12},{9,13},{10,... | collective-permute-start | bytes 172040 | tf_op jit(solution)/shard_map/ppermute | solution.py:453
  61.5 18.8 %all-to-all-start.1 = ((bf16[8,128,128]{2,1,0:T(8,128)(2,1)}), bf16[8,128,128]{2,1,0:T(8,128)(2,1)S(1)}, u32[]{:S(2)}, u32[]{:S(2)}) async-start(bf16[8,128,128]{2,1,0:T(8,128)(2,1)} %back.1.refs_0_), calls=%async_computation.1 | async-start | bytes 524288 | tf_op jit(solution)/shard_map/all_to_all | solution.py:605
  68.6 5.3 %collective-permute-start.17 = (bf16[14,16,128]{2,1,0:T(8,128)(2,1)S(1)}, bf16[14,16,128]{2,1,0:T(8,128)(2,1)S(1)}, u32[]{:S(2)}, u32[]{:S(2)}) collective-permute-start(bf16[14,16,128]{2,1,0:T(8,128)(2,1)S(1)} %far_sum.2.mine), channel_id=1, source_target_pairs={{0,2},{1,3},{2,0},{3,1},{4,6},{5,7},{6,4},{7,5},{8,10},{9,11},{10,... | collective-permute-start | bytes 172040 | tf_op jit(solution)/shard_map/ppermute | solution.py:453
  71.5 5.8 %collective-permute-start.26 = (bf16[14,32,128]{2,1,0:T(8,128)(2,1)S(1)}, bf16[14,32,128]{2,1,0:T(8,128)(2,1)S(1)}, u32[]{:S(2)}, u32[]{:S(2)}) collective-permute-start(bf16[14,32,128]{2,1,0:T(8,128)(2,1)S(1)} %join.9.mine), channel_id=1, source_target_pairs={{0,16},{1,17},{2,18},{3,19},{4,20},{5,21},{6,22},{7,23},{8,9},{9,8... | collective-permute-start | bytes 344072 | tf_op jit(solution)/shard_map/ppermute | solution.py:453
  73.8 5.8 %collective-permute-start.18 = (bf16[14,32,128]{2,1,0:T(8,128)(2,1)S(1)}, bf16[14,32,128]{2,1,0:T(8,128)(2,1)S(1)}, u32[]{:S(2)}, u32[]{:S(2)}) collective-permute-start(bf16[14,32,128]{2,1,0:T(8,128)(2,1)S(1)} %join.6.mine), channel_id=1, source_target_pairs={{0,1},{1,0},{2,3},{3,2},{4,5},{5,4},{6,7},{7,6},{8,24},{9,25},{10,... | collective-permute-start | bytes 344072 | tf_op jit(solution)/shard_map/ppermute | solution.py:453
  77.4 6.1 %collective-permute-start.27 = (bf16[14,64,128]{2,1,0:T(8,128)(2,1)S(1)}, bf16[14,64,128]{2,1,0:T(8,128)(2,1)S(1)}, u32[]{:S(2)}, u32[]{:S(2)}) collective-permute-start(bf16[14,64,128]{2,1,0:T(8,128)(2,1)S(1)} %join.10.refs_1_), channel_id=1, source_target_pairs={{0,1},{1,0},{2,3},{3,2},{4,5},{5,4},{6,7},{7,6},{8,24},{9,25},{10,... | collective-permute-start | bytes 688136 | tf_op jit(solution)/shard_map/ppermute | solution.py:453
  79.7 6.1 %collective-permute-start.19 = (bf16[14,64,128]{2,1,0:T(8,128)(2,1)S(1)}, bf16[14,64,128]{2,1,0:T(8,128)(2,1)S(1)}, u32[]{:S(2)}, u32[]{:S(2)}) collective-permute-start(bf16[14,64,128]{2,1,0:T(8,128)(2,1)S(1)} %join.7.mine), channel_id=1, source_target_pairs={{0,16},{1,17},{2,18},{3,19},{4,20},{5,21},{6,22},{7,23},{8,9},{9,8... | collective-permute-start | bytes 688136 | tf_op jit(solution)/shard_map/ppermute | solution.py:453
  (14 other events, 122.1 us)

commit v4 on v3

--- a/solution.py
+++ b/solution.py
@@ -600,16 +600,16 @@
         split_stage(2, g, parts[g][0], swap(parts[g][1], partner_at(1, g)), F32, after=sides[:2] if g == 1 else ())
         for g in groups
     ]
-    parts = [pair_stage(*parts[g], wire, after=[returning] if g == 1 else ()) for g in groups]
+    parts = [pair_stage(*parts[g], wire, after=[returning] if g == 0 else ()) for g in groups]
     parts = [far_stage(parts[g]) for g in groups]
     coming_back = lax.all_to_all(returning, "dev", split_axis=0, concat_axis=0, tiled=True)
-    parts = [join_stage(2, g, parts[g], after=[flat_tiles] if g == 1 else ()) for g in groups]
+    parts = [join_stage(2, g, parts[g], after=[flat_tiles] if g == 0 else ()) for g in groups]
     parts = [join_stage(1, g, parts[g]) for g in groups]
     (input_grad,) = call(
         restore_kernel, [], [coming_back.reshape(peers * capacity, voxels, channels), flat_tiles],
         [block], name="restore",
     )
-    parts = [join_stage(0, g, parts[g], after=[coming_back] if g == 1 else ()) for g in groups]
+    parts = [join_stage(0, g, parts[g], after=[coming_back] if g == 0 else ()) for g in groups]
     others = [swap(parts[g], other_core) for g in groups]
     grads = finish(scale, 0, parts)
     grad_one, grad_two = finish(scale, 1, others, grads)

time: 89.9 us -> 89.9 us (level)
  no operation moved by 1% of the time
where the time goes in v4:
time: 89.9 us; the launch traced here: 89.4 us
  starting transfers between devices  47.9 us (53%)
  waiting for transfers between devices  22.7 us (25%)
  Pallas kernels  17.7 us (20%)
  between operations  1.01 us (1%)
    ppermute x18, starting transfers between devices, swap(): return lax.ppermute(rows, ('tile', 'dev'), pairs)  27.8 us
    pallas_call x27, Pallas kernels, call(): pl.pallas_call(body, out_shape=shapes, in_specs=[ANY] * len(after) + [HBM...  17.7 us
    ppermute x18, waiting for transfers between devices, swap(): return lax.ppermute(rows, ('tile', 'dev'), pairs)  16.5 us
    ppermute x12, starting transfers between devices, halo(): sides += [lax.ppermute(rows, axis, even), lax.ppermute(rows, axis, odd)]  7.85 us
    all_to_all x1, starting transfers between devices, per_device(): lax.all_to_all(outgoing, 'dev', split_axis=0, concat_axis=0, tiled=True)  7.29 us
    all_to_all x1, waiting for transfers between devices, per_device(): lax.all_to_all(outgoing, 'dev', split_axis=0, concat_axis=0, tiled=True)  5.97 us
    all_to_all x1, starting transfers between devices, per_device(): lax.all_to_all(returning, 'dev', split_axis=0, concat_axis=0, tiled=True)  4.96 us
  transfers between devices with their start and end apart: 32, of which 12 were waited for; matrix products, arithmetic and copies ran while one was open for 0% of the time, Pallas kernels for 13%

profile of v4, /device:TPU:0, one launch (start us, length us, event | category | flops | bytes accessed | tf_op | source)
XLA Modules:
  0.0 89.4 jit_solution(6027296324771719377)
XLA Ops:
  0.6 1.7 %pack.1 = (bf16[8,144,128]{2,1,0:T(8,128)(2,1)}, bf16[4,64,128]{2,1,0:T(8,128)(2,1)}) custom-call(s32[8]{0:T(128)} %morton_hbm.3, s32[4]{0:T(128)} %rim_hbm.5, bf16[8,64,128]{2,1,0:T(8,128)(2,1)} %features_hbm.1, bf16[8,64,128]{2,1,0:T(8,128)(2,1)} %cotangent.3), custom_call_target="tpu_custom_call" | custom-call | flops 1500000000 | bytes 622640 | tf_op jit(solution)/shard_map/pack/pallas_call | solution.py:421
  2.4 7.3 %all-to-all-start = ((bf16[8,144,128]{2,1,0:T(8,128)(2,1)}), bf16[8,144,128]{2,1,0:T(8,128)(2,1)S(1)}, u32[]{:S(2)}, u32[]{:S(2)}) async-start(bf16[8,144,128]{2,1,0:T(8,128)(2,1)} %get-tuple-element.39), calls=%async_computation | async-start | bytes 589824 | tf_op jit(solution)/shard_map/all_to_all | solution.py:548
  10.6 2.1 %collective-permute-start.6 = (bf16[4,64,128]{2,1,0:T(8,128)(2,1)}, bf16[4,64,128]{2,1,0:T(8,128)(2,1)S(1)}, u32[]{:S(2)}, u32[]{:S(2)}) collective-permute-start(bf16[4,64,128]{2,1,0:T(8,128)(2,1)} %get-tuple-element.42), channel_id=1, source_target_pairs={{0,1},{1,0},{2,3},{3,2},{4,5},{5,4},{6,7},{7,6},{8,9},{9,8},{10,11... | collective-permute-start | bytes 196616 | tf_op jit(solution)/shard_map/ppermute | solution.py:442
  13.3 6.0 %all-to-all-done.arrived = bf16[8,144,128]{2,1,0:T(8,128)(2,1)S(1)} async-done(((bf16[8,144,128]{2,1,0:T(8,128)(2,1)}), bf16[8,144,128]{2,1,0:T(8,128)(2,1)S(1)}, u32[]{:S(2)}, u32[]{:S(2)}) %all-to-all-start) | async-done | bytes 294944 | tf_op jit(solution)/shard_map/all_to_all | solution.py:548
  22.8 1.9 %hidden_grad.1 = (bf16[512,3456]{1,0:T(8,128)(2,1)S(1)}, f32[512,128]{1,0:T(8,128)S(1)}) custom-call(s32[8,27]{1,0:T(8,128)S(1)} %copy-done.2, bf16[8,64,128]{2,1,0:T(8,128)(2,1)S(1)} %copy-done.1, bf16[3456,128]{1,0:T(8,128)(2,1)S(1)} %copy-done.3, bf16[4,64,128]{2,1,0:T(8,128)(2,1)S(1)} %collective-permute-done.4.side_a, ...), custom_call_target="tpu_custom_call" | custom-call | flops 452984832 | bytes 5079904 | tf_op jit(solution)/shard_map/hidden_grad/pallas_call | solution.py:421
  25.0 2.6 %middle.1 = (bf16[8,64,128]{2,1,0:T(8,128)(2,1)S(1)}, bf16[8,64,128]{2,1,0:T(8,128)(2,1)S(1)}, bf16[2,4,64,128]{3,2,1,0:T(8,128)(2,1)S(1)}, bf16[512,3456]{1,0:T...) custom-call(s32[8,27]{1,0:T(8,128)S(1)} %copy-done.2, s32[4]{0:T(128)S(1)} %copy-done.4, ...), custom_call_target="tpu_custom_call" | custom-call | flops 452984832 | bytes 5735280 | tf_op jit(solution)/shard_map/middle/pallas_call | solution.py:421
  28.3 2.5 %collective-permute-start.20 = (f32[14,128,128]{2,1,0:T(8,128)S(1)}, f32[14,128,128]{2,1,0:T(8,128)S(1)}, u32[]{:S(2)}, u32[]{:S(2)}) collective-permute-start(f32[14,128,128]{2,1,0:T(8,128)S(1)} %get-tuple-element.63), channel_id=1, source_target_pairs={{0,8},{1,9},{2,10},{3,11},{4,12},{5,13},{6,14},{7,15},{8,0},{9,1},... | collective-permute-start | bytes 2752520 | tf_op jit(solution)/shard_map/ppermute | solution.py:453
  33.0 4.5 %collective-permute-start.21 = (bf16[14,64,128]{2,1,0:T(8,128)(2,1)S(1)}, bf16[14,64,128]{2,1,0:T(8,128)(2,1)S(1)}, u32[]{:S(2)}, u32[]{:S(2)}) collective-permute-start(bf16[14,64,128]{2,1,0:T(8,128)(2,1)S(1)} %get-tuple-element.65), channel_id=1, source_target_pairs={{0,1},{1,0},{2,3},{3,2},{4,5},{5,4},{6,7},{7,6},{8,24},{9,25},{10,... | collective-permute-start | bytes 688136 | tf_op jit(solution)/shard_map/ppermute | solution.py:453
  37.6 1.8 %collective-permute-start.13 = (bf16[14,64,128]{2,1,0:T(8,128)(2,1)S(1)}, bf16[14,64,128]{2,1,0:T(8,128)(2,1)S(1)}, u32[]{:S(2)}, u32[]{:S(2)}) collective-permute-start(bf16[14,64,128]{2,1,0:T(8,128)(2,1)S(1)} %get-tuple-element.57), channel_id=1, source_target_pairs={{0,16},{1,17},{2,18},{3,19},{4,20},{5,21},{6,22},{7,23},{8,9},{9,8... | collective-permute-start | bytes 688136 | tf_op jit(solution)/shard_map/ppermute | solution.py:453
  40.1 2.9 %collective-permute-done.21.other = bf16[14,64,128]{2,1,0:T(8,128)(2,1)S(1)} collective-permute-done((bf16[14,64,128]{2,1,0:T(8,128)(2,1)S(1)}, bf16[14,64,128]{2,1,0:T(8,128)(2,1)S(1)}, u32[]{:S(2)}, u32[]{:S(2)}) %collective-permute-start.21) | collective-permute-done | bytes 229408 | tf_op jit(solution)/shard_map/ppermute | solution.py:453
  43.0 2.1 %collective-permute-start.22 = (bf16[14,32,128]{2,1,0:T(8,128)(2,1)S(1)}, bf16[14,32,128]{2,1,0:T(8,128)(2,1)S(1)}, u32[]{:S(2)}, u32[]{:S(2)}) collective-permute-start(bf16[14,32,128]{2,1,0:T(8,128)(2,1)S(1)} %get-tuple-element.67), channel_id=1, source_target_pairs={{0,16},{1,17},{2,18},{3,19},{4,20},{5,21},{6,22},{7,23},{8,9},{9,8... | collective-permute-start | bytes 344072 | tf_op jit(solution)/shard_map/ppermute | solution.py:453
  45.1 2.4 %collective-permute-start.14 = (bf16[14,32,128]{2,1,0:T(8,128)(2,1)S(1)}, bf16[14,32,128]{2,1,0:T(8,128)(2,1)S(1)}, u32[]{:S(2)}, u32[]{:S(2)}) collective-permute-start(bf16[14,32,128]{2,1,0:T(8,128)(2,1)S(1)} %get-tuple-element.59), channel_id=1, source_target_pairs={{0,1},{1,0},{2,3},{3,2},{4,5},{5,4},{6,7},{7,6},{8,24},{9,25},{10,... | collective-permute-start | bytes 344072 | tf_op jit(solution)/shard_map/ppermute | solution.py:453
  49.0 4.1 %collective-permute-start.23 = (f32[14,16,128]{2,1,0:T(8,128)S(1)}, f32[14,16,128]{2,1,0:T(8,128)S(1)}, u32[]{:S(2)}, u32[]{:S(2)}) collective-permute-start(f32[14,16,128]{2,1,0:T(8,128)S(1)} %get-tuple-element.69), channel_id=1, source_target_pairs={{0,2},{1,3},{2,0},{3,1},{4,6},{5,7},{6,4},{7,5},{8,10},{9,11},{10,... | collective-permute-start | bytes 344072 | tf_op jit(solution)/shard_map/ppermute | solution.py:453
  53.2 2.9 %back.1.refs_0_ = bf16[8,128,128]{2,1,0:T(8,128)(2,1)} custom-call(s32[8,27]{1,0:T(8,128)S(1)} %copy-done.2, bf16[8,64,128]{2,1,0:T(8,128)(2,1)S(1)} %copy-done.1, bf16[3456,128]{1,0:T(8,128)(2,1)S(1)} %copy-done, bf16[8,64,128]{2,1,0:T(8,128)(2,1)S(1)} %get-tuple-element.47.pre_grad, bf16[2,4,64,128]{3,2,1,0:T(8,128)(2,1)S(1)} %collective-permute-done.8.side_a.refs_0_, ...), custom_call_target="tpu_custom_call" | custom-call | flops 452984832 | bytes 1999712 | tf_op jit(solution)/shard_map/back/pallas_call | solution.py:421
  56.1 2.0 %collective-permute-done.23.right = f32[14,16,128]{2,1,0:T(8,128)S(1)} collective-permute-done((f32[14,16,128]{2,1,0:T(8,128)S(1)}, f32[14,16,128]{2,1,0:T(8,128)S(1)}, u32[]{:S(2)}, u32[]{:S(2)}) %collective-permute-start.23) | collective-permute-done | bytes 114720 | tf_op jit(solution)/shard_map/ppermute | solution.py:453
  58.1 2.5 %collective-permute-start.24 = (bf16[14,16,128]{2,1,0:T(8,128)(2,1)S(1)}, bf16[14,16,128]{2,1,0:T(8,128)(2,1)S(1)}, u32[]{:S(2)}, u32[]{:S(2)}) collective-permute-start(bf16[14,16,128]{2,1,0:T(8,128)(2,1)S(1)} %pair_sum.3.left), channel_id=1, source_target_pairs={{0,4},{1,5},{2,6},{3,7},{4,0},{5,1},{6,2},{7,3},{8,12},{9,13},{10,... | collective-permute-start | bytes 172040 | tf_op jit(solution)/shard_map/ppermute | solution.py:453
  61.5 5.0 %all-to-all-start.1 = ((bf16[8,128,128]{2,1,0:T(8,128)(2,1)}), bf16[8,128,128]{2,1,0:T(8,128)(2,1)S(1)}, u32[]{:S(2)}, u32[]{:S(2)}) async-start(bf16[8,128,128]{2,1,0:T(8,128)(2,1)} %back.1.refs_0_), calls=%async_computation.1 | async-start | bytes 524288 | tf_op jit(solution)/shard_map/all_to_all | solution.py:605
  66.5 2.1 %collective-permute-start.25 = (bf16[14,16,128]{2,1,0:T(8,128)(2,1)S(1)}, bf16[14,16,128]{2,1,0:T(8,128)(2,1)S(1)}, u32[]{:S(2)}, u32[]{:S(2)}) collective-permute-start(bf16[14,16,128]{2,1,0:T(8,128)(2,1)S(1)} %far_sum.3.mine), channel_id=1, source_target_pairs={{0,2},{1,3},{2,0},{3,1},{4,6},{5,7},{6,4},{7,5},{8,10},{9,11},{10,... | collective-permute-start | bytes 172040 | tf_op jit(solution)/shard_map/ppermute | solution.py:453
  68.7 2.6 %output.1 = (bf16[8,64,128]{2,1,0:T(8,128)(2,1)}, f32[8,8,128]{2,1,0:T(8,128)S(1)}) custom-call(s32[8,27]{1,0:T(8,128)S(1)} %copy-done.2, s32[8]{0:T(128)S(1)} %copy-done.5, bf16[3456,128]{1,0:T(8,128)(2,1)S(1)} %copy-done.3, bf16[8,64,128]{2,1,0:T(8,128)(2,1)S(1)} %get-tuple-element.44.hidden, bf16[8,64,128]{2,1,0:T(8,128)(2,1)S(1)} %get-tuple-element.40.morton, ...), custom_call_target="tpu_custom_call" | custom-call | flops 452984832 | bytes 1835904 | tf_op jit(solution)/shard_map/output/pallas_call | solution.py:421
  71.9 1.9 %collective-permute-done.17.refs_2_ = bf16[14,16,128]{2,1,0:T(8,128)(2,1)S(1)} collective-permute-done((bf16[14,16,128]{2,1,0:T(8,128)(2,1)S(1)}, bf16[14,16,128]{2,1,0:T(8,128)(2,1)S(1)}, u32[]{:S(2)}, u32[]{:S(2)}) %collective-permute-start.17) | collective-permute-done | bytes 57376 | tf_op jit(solution)/shard_map/ppermute | solution.py:453
  75.4 2.0 %collective-permute-done.26.other = bf16[14,32,128]{2,1,0:T(8,128)(2,1)S(1)} collective-permute-done((bf16[14,32,128]{2,1,0:T(8,128)(2,1)S(1)}, bf16[14,32,128]{2,1,0:T(8,128)(2,1)S(1)}, u32[]{:S(2)}, u32[]{:S(2)}) %collective-permute-start.26) | collective-permute-done | bytes 114720 | tf_op jit(solution)/shard_map/ppermute | solution.py:453
  77.4 2.1 %collective-permute-start.27 = (bf16[14,64,128]{2,1,0:T(8,128)(2,1)S(1)}, bf16[14,64,128]{2,1,0:T(8,128)(2,1)S(1)}, u32[]{:S(2)}, u32[]{:S(2)}) collective-permute-start(bf16[14,64,128]{2,1,0:T(8,128)(2,1)S(1)} %join.10.mine), channel_id=1, source_target_pairs={{0,1},{1,0},{2,3},{3,2},{4,5},{5,4},{6,7},{7,6},{8,24},{9,25},{10,... | collective-permute-start | bytes 688136 | tf_op jit(solution)/shard_map/ppermute | solution.py:453
  80.3 3.2 %collective-permute-done.27.other = bf16[14,64,128]{2,1,0:T(8,128)(2,1)S(1)} collective-permute-done((bf16[14,64,128]{2,1,0:T(8,128)(2,1)S(1)}, bf16[14,64,128]{2,1,0:T(8,128)(2,1)S(1)}, u32[]{:S(2)}, u32[]{:S(2)}) %collective-permute-start.27) | collective-permute-done | bytes 229408 | tf_op jit(solution)/shard_map/ppermute | solution.py:453
  83.7 2.1 %collective-permute-done.19.refs_2_ = bf16[14,64,128]{2,1,0:T(8,128)(2,1)S(1)} collective-permute-done((bf16[14,64,128]{2,1,0:T(8,128)(2,1)S(1)}, bf16[14,64,128]{2,1,0:T(8,128)(2,1)S(1)}, u32[]{:S(2)}, u32[]{:S(2)}) %collective-permute-start.19) | collective-permute-done | bytes 229408 | tf_op jit(solution)/shard_map/ppermute | solution.py:453
  (79 shorter events, 18.2 us)
Async XLA Ops:
  2.4 16.9 %all-to-all-start = ((bf16[8,144,128]{2,1,0:T(8,128)(2,1)}), bf16[8,144,128]{2,1,0:T(8,128)(2,1)S(1)}, u32[]{:S(2)}, u32[]{:S(2)}) async-start(bf16[8,144,128]{2,1,0:T(8,128)(2,1)} %get-tuple-element.39), calls=%async_computation | async-start | bytes 589824 | tf_op jit(solution)/shard_map/all_to_all | solution.py:548
  9.7 10.2 %collective-permute-start.4 = (bf16[4,64,128]{2,1,0:T(8,128)(2,1)}, bf16[4,64,128]{2,1,0:T(8,128)(2,1)S(1)}, u32[]{:S(2)}, u32[]{:S(2)}) collective-permute-start(bf16[4,64,128]{2,1,0:T(8,128)(2,1)} %get-tuple-element.42), channel_id=1, source_target_pairs={{0,8},{8,0},{16,24},{24,16},{1,9},{9,1},{17,25},{25,17},{2,10},{10... | collective-permute-start | bytes 196616 | tf_op jit(solution)/shard_map/ppermute | solution.py:442
  9.8 10.8 %collective-permute-start.5 = (bf16[4,64,128]{2,1,0:T(8,128)(2,1)}, bf16[4,64,128]{2,1,0:T(8,128)(2,1)S(1)}, u32[]{:S(2)}, u32[]{:S(2)}) collective-permute-start(bf16[4,64,128]{2,1,0:T(8,128)(2,1)} %get-tuple-element.42), channel_id=1, source_target_pairs={{8,16},{16,8},{9,17},{17,9},{10,18},{18,10},{11,19},{19,11},{12,20... | collective-permute-start | bytes 196616 | tf_op jit(solution)/shard_map/ppermute | solution.py:442
  10.6 11.5 %collective-permute-start.6 = (bf16[4,64,128]{2,1,0:T(8,128)(2,1)}, bf16[4,64,128]{2,1,0:T(8,128)(2,1)S(1)}, u32[]{:S(2)}, u32[]{:S(2)}) collective-permute-start(bf16[4,64,128]{2,1,0:T(8,128)(2,1)} %get-tuple-element.42), channel_id=1, source_target_pairs={{0,1},{1,0},{2,3},{3,2},{4,5},{5,4},{6,7},{7,6},{8,9},{9,8},{10,11... | collective-permute-start | bytes 196616 | tf_op jit(solution)/shard_map/ppermute | solution.py:442
  12.7 10.1 %collective-permute-start.7 = (bf16[4,64,128]{2,1,0:T(8,128)(2,1)}, bf16[4,64,128]{2,1,0:T(8,128)(2,1)S(1)}, u32[]{:S(2)}, u32[]{:S(2)}) collective-permute-start(bf16[4,64,128]{2,1,0:T(8,128)(2,1)} %get-tuple-element.42), channel_id=1, source_target_pairs={{1,2},{2,1},{3,4},{4,3},{5,6},{6,5},{9,10},{10,9},{11,12},{12,11},... | collective-permute-start | bytes 196616 | tf_op jit(solution)/shard_map/ppermute | solution.py:442
  31.5 6.0 %collective-permute-start.12 = (f32[14,128,128]{2,1,0:T(8,128)S(1)}, f32[14,128,128]{2,1,0:T(8,128)S(1)}, u32[]{:S(2)}, u32[]{:S(2)}) collective-permute-start(f32[14,128,128]{2,1,0:T(8,128)S(1)} %get-tuple-element.55), channel_id=1, source_target_pairs={{0,8},{1,9},{2,10},{3,11},{4,12},{5,13},{6,14},{7,15},{8,0},{9,1},... | collective-permute-start | bytes 2752520 | tf_op jit(solution)/shard_map/ppermute | solution.py:453
  33.0 10.0 %collective-permute-start.21 = (bf16[14,64,128]{2,1,0:T(8,128)(2,1)S(1)}, bf16[14,64,128]{2,1,0:T(8,128)(2,1)S(1)}, u32[]{:S(2)}, u32[]{:S(2)}) collective-permute-start(bf16[14,64,128]{2,1,0:T(8,128)(2,1)S(1)} %get-tuple-element.65), channel_id=1, source_target_pairs={{0,1},{1,0},{2,3},{3,2},{4,5},{5,4},{6,7},{7,6},{8,24},{9,25},{10,... | collective-permute-start | bytes 688136 | tf_op jit(solution)/shard_map/ppermute | solution.py:453
  37.6 7.5 %collective-permute-start.13 = (bf16[14,64,128]{2,1,0:T(8,128)(2,1)S(1)}, bf16[14,64,128]{2,1,0:T(8,128)(2,1)S(1)}, u32[]{:S(2)}, u32[]{:S(2)}) collective-permute-start(bf16[14,64,128]{2,1,0:T(8,128)(2,1)S(1)} %get-tuple-element.57), channel_id=1, source_target_pairs={{0,16},{1,17},{2,18},{3,19},{4,20},{5,21},{6,22},{7,23},{8,9},{9,8... | collective-permute-start | bytes 688136 | tf_op jit(solution)/shard_map/ppermute | solution.py:453
  39.4 8.2 %collective-permute-start.8 = (bf16[2,4,64,128]{3,2,1,0:T(8,128)(2,1)S(1)}, bf16[2,4,64,128]{3,2,1,0:T(8,128)(2,1)S(1)}, u32[]{:S(2)}, u32[]{:S(2)}) collective-permute-start(bf16[2,4,64,128]{3,2,1,0:T(8,128)(2,1)S(1)} %get-tuple-element.45), channel_id=1, source_target_pairs={{0,8},{8,0},{16,24},{24,16},{1,9},{9,1},{17,25},{25,17},{2,10},{10... | collective-permute-start | bytes 393224 | tf_op jit(solution)/shard_map/ppermute | solution.py:442
  39.4 8.9 %collective-permute-start.9 = (bf16[2,4,64,128]{3,2,1,0:T(8,128)(2,1)S(1)}, bf16[2,4,64,128]{3,2,1,0:T(8,128)(2,1)S(1)}, u32[]{:S(2)}, u32[]{:S(2)}) collective-permute-start(bf16[2,4,64,128]{3,2,1,0:T(8,128)(2,1)S(1)} %get-tuple-element.45), channel_id=1, source_target_pairs={{8,16},{16,8},{9,17},{17,9},{10,18},{18,10},{11,19},{19,11},{12,20... | collective-permute-start | bytes 393224 | tf_op jit(solution)/shard_map/ppermute | solution.py:442
  43.0 5.9 %collective-permute-start.22 = (bf16[14,32,128]{2,1,0:T(8,128)(2,1)S(1)}, bf16[14,32,128]{2,1,0:T(8,128)(2,1)S(1)}, u32[]{:S(2)}, u32[]{:S(2)}) collective-permute-start(bf16[14,32,128]{2,1,0:T(8,128)(2,1)S(1)} %get-tuple-element.67), channel_id=1, source_target_pairs={{0,16},{1,17},{2,18},{3,19},{4,20},{5,21},{6,22},{7,23},{8,9},{9,8... | collective-permute-start | bytes 344072 | tf_op jit(solution)/shard_map/ppermute | solution.py:453
  45.1 7.9 %collective-permute-start.14 = (bf16[14,32,128]{2,1,0:T(8,128)(2,1)S(1)}, bf16[14,32,128]{2,1,0:T(8,128)(2,1)S(1)}, u32[]{:S(2)}, u32[]{:S(2)}) collective-permute-start(bf16[14,32,128]{2,1,0:T(8,128)(2,1)S(1)} %get-tuple-element.59), channel_id=1, source_target_pairs={{0,1},{1,0},{2,3},{3,2},{4,5},{5,4},{6,7},{7,6},{8,24},{9,25},{10,... | collective-permute-start | bytes 344072 | tf_op jit(solution)/shard_map/ppermute | solution.py:453
  47.5 5.7 %collective-permute-start.10 = (bf16[2,4,64,128]{3,2,1,0:T(8,128)(2,1)S(1)}, bf16[2,4,64,128]{3,2,1,0:T(8,128)(2,1)S(1)}, u32[]{:S(2)}, u32[]{:S(2)}) collective-permute-start(bf16[2,4,64,128]{3,2,1,0:T(8,128)(2,1)S(1)} %get-tuple-element.45), channel_id=1, source_target_pairs={{0,1},{1,0},{2,3},{3,2},{4,5},{5,4},{6,7},{7,6},{8,9},{9,8},{10,11... | collective-permute-start | bytes 393224 | tf_op jit(solution)/shard_map/ppermute | solution.py:442
  47.6 5.6 %collective-permute-start.11 = (bf16[2,4,64,128]{3,2,1,0:T(8,128)(2,1)S(1)}, bf16[2,4,64,128]{3,2,1,0:T(8,128)(2,1)S(1)}, u32[]{:S(2)}, u32[]{:S(2)}) collective-permute-start(bf16[2,4,64,128]{3,2,1,0:T(8,128)(2,1)S(1)} %get-tuple-element.45), channel_id=1, source_target_pairs={{1,2},{2,1},{3,4},{4,3},{5,6},{6,5},{9,10},{10,9},{11,12},{12,11},... | collective-permute-start | bytes 393224 | tf_op jit(solution)/shard_map/ppermute | solution.py:442
  49.0 9.1 %collective-permute-start.23 = (f32[14,16,128]{2,1,0:T(8,128)S(1)}, f32[14,16,128]{2,1,0:T(8,128)S(1)}, u32[]{:S(2)}, u32[]{:S(2)}) collective-permute-start(f32[14,16,128]{2,1,0:T(8,128)S(1)} %get-tuple-element.69), channel_id=1, source_target_pairs={{0,2},{1,3},{2,0},{3,1},{4,6},{5,7},{6,4},{7,5},{8,10},{9,11},{10,... | collective-permute-start | bytes 344072 | tf_op jit(solution)/shard_map/ppermute | solution.py:453
  53.1 7.5 %collective-permute-start.15 = (f32[14,16,128]{2,1,0:T(8,128)S(1)}, f32[14,16,128]{2,1,0:T(8,128)S(1)}, u32[]{:S(2)}, u32[]{:S(2)}) collective-permute-start(f32[14,16,128]{2,1,0:T(8,128)S(1)} %get-tuple-element.61), channel_id=1, source_target_pairs={{0,2},{1,3},{2,0},{3,1},{4,6},{5,7},{6,4},{7,5},{8,10},{9,11},{10,... | collective-permute-start | bytes 344072 | tf_op jit(solution)/shard_map/ppermute | solution.py:453
  58.1 8.3 %collective-permute-start.24 = (bf16[14,16,128]{2,1,0:T(8,128)(2,1)S(1)}, bf16[14,16,128]{2,1,0:T(8,128)(2,1)S(1)}, u32[]{:S(2)}, u32[]{:S(2)}) collective-permute-start(bf16[14,16,128]{2,1,0:T(8,128)(2,1)S(1)} %pair_sum.3.left), channel_id=1, source_target_pairs={{0,4},{1,5},{2,6},{3,7},{4,0},{5,1},{6,2},{7,3},{8,12},{9,13},{10,... | collective-permute-start | bytes 172040 | tf_op jit(solution)/shard_map/ppermute | solution.py:453
  60.6 7.9 %collective-permute-start.16 = (bf16[14,16,128]{2,1,0:T(8,128)(2,1)S(1)}, bf16[14,16,128]{2,1,0:T(8,128)(2,1)S(1)}, u32[]{:S(2)}, u32[]{:S(2)}) collective-permute-start(bf16[14,16,128]{2,1,0:T(8,128)(2,1)S(1)} %pair_sum.2.left), channel_id=1, source_target_pairs={{0,4},{1,5},{2,6},{3,7},{4,0},{5,1},{6,2},{7,3},{8,12},{9,13},{10,... | collective-permute-start | bytes 172040 | tf_op jit(solution)/shard_map/ppermute | solution.py:453
  61.5 22.2 %all-to-all-start.1 = ((bf16[8,128,128]{2,1,0:T(8,128)(2,1)}), bf16[8,128,128]{2,1,0:T(8,128)(2,1)S(1)}, u32[]{:S(2)}, u32[]{:S(2)}) async-start(bf16[8,128,128]{2,1,0:T(8,128)(2,1)} %back.1.refs_0_), calls=%async_computation.1 | async-start | bytes 524288 | tf_op jit(solution)/shard_map/all_to_all | solution.py:605
  68.6 5.3 %collective-permute-start.17 = (bf16[14,16,128]{2,1,0:T(8,128)(2,1)S(1)}, bf16[14,16,128]{2,1,0:T(8,128)(2,1)S(1)}, u32[]{:S(2)}, u32[]{:S(2)}) collective-permute-start(bf16[14,16,128]{2,1,0:T(8,128)(2,1)S(1)} %far_sum.2.refs_1_), channel_id=1, source_target_pairs={{0,2},{1,3},{2,0},{3,1},{4,6},{5,7},{6,4},{7,5},{8,10},{9,11},{10,... | collective-permute-start | bytes 172040 | tf_op jit(solution)/shard_map/ppermute | solution.py:453
  71.5 5.8 %collective-permute-start.26 = (bf16[14,32,128]{2,1,0:T(8,128)(2,1)S(1)}, bf16[14,32,128]{2,1,0:T(8,128)(2,1)S(1)}, u32[]{:S(2)}, u32[]{:S(2)}) collective-permute-start(bf16[14,32,128]{2,1,0:T(8,128)(2,1)S(1)} %join.9.mine), channel_id=1, source_target_pairs={{0,16},{1,17},{2,18},{3,19},{4,20},{5,21},{6,22},{7,23},{8,9},{9,8... | collective-permute-start | bytes 344072 | tf_op jit(solution)/shard_map/ppermute | solution.py:453
  73.8 5.8 %collective-permute-start.18 = (bf16[14,32,128]{2,1,0:T(8,128)(2,1)S(1)}, bf16[14,32,128]{2,1,0:T(8,128)(2,1)S(1)}, u32[]{:S(2)}, u32[]{:S(2)}) collective-permute-start(bf16[14,32,128]{2,1,0:T(8,128)(2,1)S(1)} %join.6.mine), channel_id=1, source_target_pairs={{0,1},{1,0},{2,3},{3,2},{4,5},{5,4},{6,7},{7,6},{8,24},{9,25},{10,... | collective-permute-start | bytes 344072 | tf_op jit(solution)/shard_map/ppermute | solution.py:453
  77.4 6.1 %collective-permute-start.27 = (bf16[14,64,128]{2,1,0:T(8,128)(2,1)S(1)}, bf16[14,64,128]{2,1,0:T(8,128)(2,1)S(1)}, u32[]{:S(2)}, u32[]{:S(2)}) collective-permute-start(bf16[14,64,128]{2,1,0:T(8,128)(2,1)S(1)} %join.10.mine), channel_id=1, source_target_pairs={{0,1},{1,0},{2,3},{3,2},{4,5},{5,4},{6,7},{7,6},{8,24},{9,25},{10,... | collective-permute-start | bytes 688136 | tf_op jit(solution)/shard_map/ppermute | solution.py:453
  79.7 6.1 %collective-permute-start.19 = (bf16[14,64,128]{2,1,0:T(8,128)(2,1)S(1)}, bf16[14,64,128]{2,1,0:T(8,128)(2,1)S(1)}, u32[]{:S(2)}, u32[]{:S(2)}) collective-permute-start(bf16[14,64,128]{2,1,0:T(8,128)(2,1)S(1)} %join.7.refs_1_), channel_id=1, source_target_pairs={{0,16},{1,17},{2,18},{3,19},{4,20},{5,21},{6,22},{7,23},{8,9},{9,8... | collective-permute-start | bytes 688136 | tf_op jit(solution)/shard_map/ppermute | solution.py:453
  (14 other events, 122.0 us)
